TPU v7x, 32 devices: a whole 2x2x4 slice. The times are simulated.
32 devices in a mesh: dp: 8 (over z, y), tensor: 4 (over x, core).
Axes of the slice: x: 2, y: 2, z: 4, core: 2. Of those that a mesh axis runs over, the one named last changes fastest.
Arguments:
- hidden_in: float32 [8192, 1536], P(('dp', 'tensor')), may hold values from -6 to 6
- norm_gain: float32 [1536], replicated, may hold values from 0.5 to 1.5
- gate_value_weight: bfloat16 [1536, 2, 3072], P('dp', None, 'tensor'), may hold values from -0.15625 to 0.15625
- state_proj_weight: bfloat16 [1536, 256], P('dp'), may hold values from -0.15625 to 0.15625
- step_weight: bfloat16 [1536, 48], P('dp', 'tensor'), may hold values from -0.15625 to 0.15625
- conv_value_kernel: float32 [3072, 4], P('tensor'), may hold values from -3 to 3
- conv_value_bias: float32 [3072], P('tensor'), may hold values from -3 to 3
- conv_state_kernel: float32 [256, 4], replicated, may hold values from -3 to 3
- conv_state_bias: float32 [256], replicated, may hold values from -3 to 3
- step_bias: float32 [48], P('tensor'), may hold values from -6 to -1
- decay_log: float32 [48], P('tensor'), may hold values from -3 to 2
- skip_scale: float32 [48], P('tensor'), may hold values from 0.5 to 1.5
- gate_norm_gain: float32 [3072], P('tensor'), may hold values from 0.5 to 1.5
- out_weight: bfloat16 [1536, 3072], P('dp', 'tensor'), may hold values from -0.109375 to 0.109375
- out_cotangent: float32 [8192, 1536], P(('dp', 'tensor')), may hold values from -6 to 6
- seq_lengths: int32 [32], replicated, may hold values from 0 to 1024, as said below
- seq_device: int32 [32], replicated, may hold values from 0 to 7, as said below
- seq_offset: int32 [32], replicated, may hold values from 0 to 3, as said below
Outputs:
- output: float32 [8192, 1536], P(('dp', 'tensor'))
- hidden_gradient: float32 [8192, 1536], P(('dp', 'tensor'))
- norm_gain_gradient: float32 [1536], P(('dp', 'tensor'))
- gate_value_weight_gradient: float32 [1536, 2, 3072], P('dp', None, 'tensor')
- state_proj_weight_gradient: float32 [1536, 256], P(('dp', 'tensor'))
- step_weight_gradient: float32 [1536, 48], P('dp', 'tensor')
- conv_value_kernel_gradient: float32 [3072, 4], P('tensor')
- conv_value_bias_gradient: float32 [3072], P('tensor')
- conv_state_kernel_gradient: float32 [256, 4], P(('dp', 'tensor'))
- conv_state_bias_gradient: float32 [256], P(('dp', 'tensor'))
- step_bias_gradient: float32 [48], P('tensor')
- decay_log_gradient: float32 [48], P('tensor')
- skip_scale_gradient: float32 [48], P('tensor')
- gate_norm_gain_gradient: float32 [3072], P('tensor')
- out_weight_gradient: float32 [1536, 3072], P('dp', 'tensor')
Inputs may be any that keep to these rules, and one draw needn't show every extreme that they name: A slot with seq_lengths > 0 is a sequence that occupies spans seq_offset to seq_offset + ceil(seq_lengths / 256) - 1 of the 4 spans of dp index seq_device; sequences of one dp index never share a span; a slot of length 0 occupies nothing. Some sequence has length 1024, and some slot is empty. `seq_device`: each dp index is named by 4 slots. `seq_offset`: some sequence begins at the last span of its dp index.
All inputs are finite; a program needn't handle non-finite values.
Results may differ from a plain program's by a relative error of at most 0.011.
Values may be sent and summed in bfloat16 or wider, within the bound.
No kernel may reach another device: no remote copies, remote signals or barrier semaphores. Data moves between devices by JAX's collectives and lax.ppermute only.
A program may use at most 192 MiB of HBM per device.

v0:
```python
from functools import partial

import jax, jax.numpy as jnp
from jax import lax
from jax.experimental import pallas as pl
from jax.experimental.pallas import tpu as pltpu
from jax.sharding import PartitionSpec as P
f32=jnp.float32; bf16=jnp.bfloat16
Q=128
NS=128
VW=768
HW=64
CW=1024
RW=1152
SPAN=256
FWD_LIMIT=14<<20
BACK_LIMIT=18<<20
NEG=-1e30

def mm(a,b,ca=1,cb=0):
    return lax.dot_general(a,b,(((ca,),(cb,)),((),())),preferred_element_type=f32)

def split2(x):
    hi=x.astype(bf16); return hi,(x-hi.astype(f32)).astype(bf16)

def split3(x):
    hi=x.astype(bf16); r=x-hi.astype(f32); mid=r.astype(bf16); return hi,mid,(r-mid.astype(f32)).astype(bf16)

def mm3(a,b,ca=1,cb=0):
    ah,al=split2(a); bh,bl=split2(b)
    return mm(jnp.concatenate([ah,ah,al],axis=ca),jnp.concatenate([bh,bl,bh],axis=cb),ca,cb)

def tri_sum(tri,x):
    a,b,c=split3(x); w=x.shape[1]
    p=mm(tri,jnp.concatenate([a,b,c],axis=1))
    return p[:,:w]+p[:,w:2*w]+p[:,2*w:]

def spread(x,ee):
    a,b=split2(x)
    return mm(jnp.concatenate([a,b],axis=1),ee)

def iotas():
    return lax.broadcasted_iota(jnp.int32,(Q,Q),0),lax.broadcasted_iota(jnp.int32,(Q,Q),1)

def softplus(z):
    return jnp.maximum(z,0.0)+jnp.log(1.0+jnp.exp(-jnp.abs(z)))

def sig(z):
    return 1.0/(1.0+jnp.exp(-z))

def halves(x):
    lane=lax.broadcasted_iota(jnp.int32,x.shape,1)
    lo=jnp.where(lane<HW,x,0.0); hi=jnp.where(lane<HW,0.0,x)
    return jnp.concatenate([lo.astype(bf16),hi.astype(bf16)],axis=0)

def spread_matrix(shape):
    r=lax.broadcasted_iota(jnp.int32,shape,0)%128; c=lax.broadcasted_iota(jnp.int32,shape,1)//HW
    return jnp.where(r==c,1.0,0.0).astype(bf16)

def sum_matrix(shape):
    r=lax.broadcasted_iota(jnp.int32,shape,0)%VW//HW; c=lax.broadcasted_iota(jnp.int32,shape,1)
    return jnp.where(r==c,1.0,0.0).astype(bf16)

def halves2(x):
    lane=lax.broadcasted_iota(jnp.int32,x.shape,1)
    h,l=split2(jnp.concatenate([jnp.where(lane<HW,x,0.0),jnp.where(lane<HW,0.0,x)],axis=0))
    return h,l

def fwd_kernel(c0,nc,first_ref,raw_ref,par_ref,*rest):
    y_ref,act_ref,sl_ref,sp_ref,wt_ref,lt_ref,s_ref,t_ref,ext,ee_ref=rest[-10:]
    ck_ref=par_ref
    i=pl.program_id(0)
    @pl.when(i==0)
    def _():
        ee_ref[...]=spread_matrix(ee_ref.shape)
        if c0:
            s_ref[...]=rest[0][...]; t_ref[...]=rest[1][...]
        else:
            s_ref[...]=jnp.zeros_like(s_ref); t_ref[...]=jnp.zeros_like(t_ref)
    c=c0+i
    start=(first_ref[c//(SPAN//Q)]==1)&(c%(SPAN//Q)==0)
    @pl.when(start)
    def _():
        s_ref[...]=jnp.zeros_like(s_ref); t_ref[...]=jnp.zeros_like(t_ref)
    ext[0:8,:]=t_ref[...]
    x=raw_ref[:,:CW]
    ext[8:8+Q,:]=x
    t_ref[...]=raw_ref[Q-8:Q,:CW]
    pre=par_ref[4:5,:]+ck_ref[3:4,:]*x
    for j in (1,2,3):
        pre=pre+ck_ref[3-j:4-j,:]*ext[8-j:8-j+Q,:]
    sg=sig(pre)
    act=pre*sg
    act_ref[...]=act
    sl_ref[...]=sg*(1.0+pre-act)
    v=act[:,:VW]; b=act[:,VW:VW+NS].astype(bf16); cc=act[:,VW+NS:].astype(bf16)
    dt=softplus(raw_ref[:,CW:]+par_ref[5:6,:128])
    a=-dt*jnp.exp(par_ref[6:7,:128])
    row,col=iotas()
    low=row>=col; up=row<=col
    tri=jnp.where(low,1.0,0.0).astype(bf16)
    cum=tri_sum(tri,a)
    cum_t=cum.T
    last=cum[Q-1:Q,:]
    ee=ee_ref[...]
    sprd=spread(jnp.concatenate([dt,jnp.exp(cum),jnp.exp(last-cum)],axis=0),ee)
    dte,ecum,etail=sprd[:Q],sprd[Q:2*Q],sprd[2*Q:]
    x=v*dte
    g=mm(cc,b,1,1)
    gt=mm(b,cc,1,1)
    parts=[]
    for p in range(VW//128):
        ws=[]
        for h in (2*p,2*p+1):
            d=jnp.where(low,cum[:,h:h+1]-cum_t[h:h+1,:],NEG)
            ws.append((jnp.exp(d)*g).astype(bf16))
            lt=jnp.exp(jnp.where(up,cum_t[h:h+1,:]-cum[:,h:h+1],NEG))
            lt_ref[:,h*Q:(h+1)*Q]=lt
            wt_ref[:,h*Q:(h+1)*Q]=(lt*gt).astype(bf16)
        parts.append(mm(jnp.concatenate(ws,axis=1),halves(x[:,128*p:128*p+128])))
    s=s_ref[...]
    sp_ref[0]=s
    y_ref[...]=jnp.concatenate(parts,axis=1)+ecum*mm(cc,s.astype(bf16))+par_ref[7:8,:VW]*v
    s_ref[...]=ecum[Q-1:Q,:]*s+mm(b,(x*etail).astype(bf16),0,0)

def bwd_kernel(c0,nc,nall,first_ref,raw_ref,act_ref,sl_ref,y_ref,dy_ref,sp_ref,wt_ref,lt_ref,par_ref,*rest):
    out_ref,ds_ref,sn_ref,h_ref,acc_ref,acs_ref,ext,ee_ref,hh_ref=rest[-9:]
    ck_ref=par_ref
    i=pl.program_id(0)
    @pl.when(i==0)
    def _():
        ee_ref[...]=spread_matrix(ee_ref.shape)
        hh_ref[...]=sum_matrix(hh_ref.shape)
        for k,ref in enumerate((ds_ref,sn_ref,h_ref,acc_ref,acs_ref)):
            ref[...]=jnp.zeros_like(ref) if c0+nc==nall else rest[k][...]
    c=c0+nc-1-i
    nxt=jnp.minimum(c+1,nall-1)
    start=(first_ref[nxt//(SPAN//Q)]==1)&(nxt%(SPAN//Q)==0)
    @pl.when(start)
    def _():
        ds_ref[...]=jnp.zeros_like(ds_ref); h_ref[...]=jnp.zeros_like(h_ref)
    act=act_ref[...]
    v=act[:,:VW]; bf=act[:,VW:VW+NS]; cf=act[:,VW+NS:]
    b=bf.astype(bf16); cc=cf.astype(bf16)
    z=raw_ref[:,CW:]+par_ref[5:6,:128]
    dt=softplus(z)
    edl=jnp.exp(par_ref[6:7,:128])
    a=-dt*edl
    row,col=iotas()
    low=row>=col; up=row<=col
    cum=tri_sum(jnp.where(low,1.0,0.0).astype(bf16),a)
    last=cum[Q-1:Q,:]
    ee=ee_ref[...]
    sprd=spread(jnp.concatenate([dt,jnp.exp(cum),jnp.exp(last-cum)],axis=0),ee)
    dte,ecum,etail=sprd[:Q],sprd[Q:2*Q],sprd[2*Q:]
    x=v*dte
    xb=x.astype(bf16)
    dy=dy_ref[...].astype(f32)
    dyb=dy.astype(bf16)
    dgt=jnp.zeros((Q,Q),f32)
    parts=[]
    for p in range(VW//128):
        cols=slice(128*p,128*p+128)
        dyh,dyl=split2(dy[:,cols])
        xh,xl=halves2(x[:,cols])
        dw=mm(jnp.concatenate([xh,xl,xh],axis=1),jnp.concatenate([dyh,dyh,dyl],axis=1),1,1)
        for k in (0,1):
            h=2*p+k
            dgt=dgt+lt_ref[:,h*Q:(h+1)*Q]*dw[k*Q:(k+1)*Q]
        parts.append(mm(wt_ref[:,2*Q*p:2*Q*(p+1)],halves(dy[:,cols])))
    ds=ds_ref[...]
    dsb=ds.astype(bf16)
    s=sp_ref[0]
    dxd=jnp.concatenate(parts,axis=1)
    bds=mm(b,dsb)
    dx=dxd+etail*bds
    xe=(x*etail).astype(bf16)
    dye=dy*ecum
    db=mm3(dgt,cf)+mm3(x*etail,ds,1,1)
    dc=mm3(dgt,bf,0,0)+mm3(dye,s,1,1)
    kk=jnp.sum(dsb.astype(f32)*sn_ref[...],axis=0,keepdims=True)
    rh,rl=split2(dyb.astype(f32)*(y_ref[...]-par_ref[7:8,:VW]*v)-xb.astype(f32)*dxd-xe.astype(f32)*bds)
    kh,kl=split2(jnp.concatenate([kk,jnp.zeros((7,VW),f32)],axis=0))
    hs=mm(jnp.concatenate([rh,rl,(v*dx).astype(bf16),jnp.concatenate([kh,kl],axis=0)],axis=0),hh_ref[...])
    dcum,q,k0=hs[:Q]+hs[Q:2*Q],hs[2*Q:3*Q],hs[3*Q:3*Q+1]+hs[3*Q+8:3*Q+9]
    da=k0+tri_sum(jnp.where(up,1.0,0.0).astype(bf16),dcum)
    dst=(q-da*edl)*sig(z)
    ds_ref[...]=ecum[Q-1:Q,:]*ds+mm3(cf,dye,0,0)
    sn_ref[...]=s
    acs_ref[0:1,:]+=jnp.sum(da*a,axis=0,keepdims=True)
    acs_ref[1:2,:]+=jnp.sum(dst,axis=0,keepdims=True)
    dv=dte*dx+par_ref[7:8,:VW]*dy
    acc_ref[5:6,:VW]+=jnp.sum(dy*v,axis=0,keepdims=True)
    dpre=jnp.concatenate([dv,db,dc],axis=1)*sl_ref[...]
    ext[0:Q,:]=dpre
    ext[Q:Q+8,:]=h_ref[...]
    h_ref[...]=dpre[0:8,:]
    xr=raw_ref[:,:CW]
    draw=ck_ref[3:4,:]*dpre
    acc_ref[3:4,:]+=jnp.sum(dpre*xr,axis=0,keepdims=True)
    acc_ref[4:5,:]+=jnp.sum(dpre,axis=0,keepdims=True)
    for j in (1,2,3):
        sh=ext[j:j+Q,:]
        draw=draw+ck_ref[3-j:4-j,:]*sh
        acc_ref[3-j:4-j,:]+=jnp.sum(sh*xr,axis=0,keepdims=True)
    out_ref[:,:CW]=draw.astype(bf16)
    out_ref[:,CW:]=dst.astype(bf16)

def sd(shape,dt=f32): return jax.ShapeDtypeStruct(shape,dt)

def hbm(shape,dt=f32): return pltpu.HBM(shape,dt)

def vmem(shape,dt=f32): return pltpu.VMEM(shape,dt)

def near_by(x): return pltpu.with_memory_space_constraint(x,pltpu.VMEM)

def stay(x): return pltpu.with_memory_space_constraint(x,pltpu.HBM)

def whole(shape): return pl.BlockSpec(shape,lambda i,*_: (0,)*len(shape))

def once(shape): return pl.BlockSpec(shape,lambda i,*_: (0,)*len(shape),pipeline_mode=pl.Buffered(1))

HL=VW//HW

def ssd_fwd(c0,nc,nall,first,raw,par,carry):
    rb=lambda w: pl.BlockSpec((Q,w),lambda i,*_: (c0+i,0))
    any_spec=pl.BlockSpec(memory_space=pl.ANY)
    held=[whole((NS,VW)),whole((8,CW))]
    return pl.pallas_call(partial(fwd_kernel,c0,nc),
        out_shape=(vmem((nall*Q,VW)),hbm((nall*Q,CW)),hbm((nall*Q,CW)),hbm((nall,NS,VW)),hbm((nall*Q,HL*Q),bf16),hbm((nall*Q,HL*Q)),sd((NS,VW)),sd((8,CW))),
        grid_spec=pltpu.PrefetchScalarGridSpec(num_scalar_prefetch=1,grid=(nc,),
            in_specs=[rb(RW),once((8,CW))]+(held+[any_spec]*6 if carry else []),
            out_specs=(rb(VW),rb(CW),rb(CW),pl.BlockSpec((1,NS,VW),lambda i,*_: (c0+i,0,0)),rb(HL*Q),rb(HL*Q),*held),
            scratch_shapes=[pltpu.VMEM((Q+8,CW),f32),pltpu.VMEM((256,VW),bf16)]),
        input_output_aliases={5+k:k for k in range(6)} if carry else {},
        compiler_params=pltpu.CompilerParams(vmem_limit_bytes=FWD_LIMIT),
        cost_estimate=pl.CostEstimate(flops=int(1.5e9*nc/8),bytes_accessed=30_000_000*nc//8,transcendentals=3_000_000*nc//8),
        name=f"ssd_forward_{c0}")(first,stay(raw),par,*(carry[6:]+(near_by(carry[0]),)+tuple(stay(x) for x in carry[1:6]) if carry else ()))

def ssd_bwd(c0,nc,nall,first,raw,act,sl,y,dy,sp,wt,lt,par,carry):
    rv=lambda w: pl.BlockSpec((Q,w),lambda i,*_: (c0+nc-1-i,0))
    any_spec=pl.BlockSpec(memory_space=pl.ANY)
    held=[whole((NS,VW)),whole((NS,VW)),whole((8,CW)),whole((8,CW)),whole((8,128))]
    return pl.pallas_call(partial(bwd_kernel,c0,nc,nall),
        out_shape=(vmem((nall*Q,RW),bf16),hbm((NS,VW)),hbm((NS,VW)),sd((8,CW)),sd((8,CW)),sd((8,128))),
        grid_spec=pltpu.PrefetchScalarGridSpec(num_scalar_prefetch=1,grid=(nc,),
            in_specs=[rv(RW),rv(CW),rv(CW),rv(VW),rv(VW),pl.BlockSpec((1,NS,VW),lambda i,*_: (c0+nc-1-i,0,0)),rv(HL*Q),rv(HL*Q),once((8,CW))]
                     +(held+[any_spec] if carry else []),
            out_specs=(rv(RW),*held),
            scratch_shapes=[pltpu.VMEM((Q+8,CW),f32),pltpu.VMEM((256,VW),bf16),pltpu.VMEM((VW,128),bf16)]),
        input_output_aliases={15:0} if carry else {},
        compiler_params=pltpu.CompilerParams(vmem_limit_bytes=BACK_LIMIT),
        cost_estimate=pl.CostEstimate(flops=int(3e9*nc/8),bytes_accessed=60_000_000*nc//8,transcendentals=4_000_000*nc//8),
        name=f"ssd_backward_{c0}")(first,stay(raw),stay(act),stay(sl),near_by(y),near_by(dy),stay(sp),stay(wt),stay(lt),par,*((stay(carry[1]),stay(carry[2]))+carry[3:]+(near_by(carry[0]),) if carry else ()))


D = 1536
H = 48
E = 3072
TOK_DEV = 1024
SEQ_DEV = 4
EPSILON = 1e-05
FWD_PARTS = ((0, 4), (4, 4))
BACK_PARTS = ((5, 3), (2, 3), (0, 2))


def contract(left, right, left_dim, right_dim, out=f32):
    return lax.dot_general(
        left, right, (((left_dim,), (right_dim,)), ((), ())), preferred_element_type=f32
    ).astype(out)


def span_layout(seq_lengths, seq_device, seq_offset, device):
    span_index = jnp.arange(SEQ_DEV, dtype=jnp.int32)
    needed = (seq_lengths + SPAN - 1) // SPAN
    owned_seq = (seq_device == device) & (seq_lengths > 0)
    relative = span_index[None, :] - seq_offset[:, None]
    inside = owned_seq[:, None] & (relative >= 0) & (relative < needed[:, None])
    live_rows = jnp.sum(
        jnp.where(inside, jnp.clip(seq_lengths[:, None] - relative * SPAN, 0, SPAN), 0), axis=0
    )
    seq_first = jnp.any(inside & (relative == 0), axis=0)
    return live_rows, seq_first.astype(jnp.int32)


def ring_order(count):
    if count == 8:
        return [0, 2, 4, 6, 7, 5, 3, 1]
    return list(range(count))


def lay(cols, rows, off_ref, refs, out):
    for k, (c0, w) in enumerate(cols):
        out[pl.ds(pl.multiple_of(off_ref[k] * rows, 16), rows), c0 : c0 + w] = refs[k][...]


def row_sums(x):
    a, b = split2(x)
    ones = jnp.ones((8, x.shape[1]), bf16)
    return mm(ones, a, 1, 1) + mm(ones, b, 1, 1)


def project_kernel(cols, rows, nx, off_ref, *refs):
    n = len(cols)
    xs = refs[n : n + nx]
    w_ref, x_ref, xt_ref, raw_ref = refs[n + nx :]
    i = pl.program_id(0)

    @pl.when(i == 0)
    def _():
        lay(cols, rows, off_ref, refs, w_ref)

    for k in range(nx):

        @pl.when(i == k)
        def _(k=k):
            x_ref[...] = xs[k][...]

    xt_ref[...] = x_ref[...].T
    raw_ref[...] = mm(x_ref[...], w_ref[...])


def project(pieces, offsets, xs, total):
    rows, n = pieces[0][0].shape[0], len(pieces)
    cols = [(c0, x.shape[1]) for x, c0 in pieces]
    width = max(c0 + w for c0, w in cols)
    q, depth = xs[0].shape
    nx = len(xs)
    at = lambda w: pl.BlockSpec((q, w), lambda i, off: (off[n + i], 0))
    return pl.pallas_call(
        partial(project_kernel, cols, rows, nx),
        out_shape=(hbm((total, width), bf16), sd((q * nx, depth), bf16), sd((depth, q * nx), bf16), hbm((q * nx, width))),
        grid_spec=pltpu.PrefetchScalarGridSpec(
            num_scalar_prefetch=1,
            grid=(nx,),
            in_specs=[once(x.shape) for x, _ in pieces] + [once(x.shape) for x in xs],
            out_specs=(whole((total, width)), at(depth), pl.BlockSpec((depth, q), lambda i, off: (0, off[n + i])), at(width)),
        ),
        compiler_params=pltpu.CompilerParams(vmem_limit_bytes=22 << 20),
        cost_estimate=pl.CostEstimate(flops=2 * q * nx * total * width, bytes_accessed=30_000_000, transcendentals=0),
        name="project",
    )(offsets, *[x for x, _ in pieces], *xs)


def cotangent_kernel(cols, rows, nx, off_ref, *refs):
    n = len(cols)
    xs = refs[n : n + nx]
    normed_ref, ssd_ref, gain_ref, w_ref, gr_ref, by_ref, sum_ref, yr_ref, x_ref = refs[n + nx :]
    i = pl.program_id(0)

    @pl.when(i == 0)
    def _():
        lay(cols, rows, off_ref, refs, w_ref)

    for k in range(nx):

        @pl.when(i == k)
        def _(k=k):
            x_ref[...] = xs[k][...]

    by = mm(x_ref[...], w_ref[:, VW:])
    gr = mm(normed_ref[...], w_ref[:, :VW])
    by_ref[...] = by
    gr_ref[...] = gr
    gated = ssd_ref[...] * (gr * sig(gr))
    scaled = gated * gain_ref[...]
    yr_ref[...] = scaled.astype(bf16)
    square = row_sums(gated * gated)
    cross = row_sums(by * scaled)
    top = lax.broadcasted_iota(jnp.int32, square.shape, 0) == 0
    sum_ref[0] = jnp.where(top, square, cross)


def cotangent(pieces, offsets, xs, normed, ssd, gain, total):
    rows, n = pieces[0][0].shape[0], len(pieces)
    cols = [(c0, x.shape[1]) for x, c0 in pieces]
    width = max(c0 + w for c0, w in cols)
    q, depth = xs[0].shape
    nx = len(xs)
    at = lambda w: pl.BlockSpec((q, w), lambda i, off: (off[n + i], 0))
    return pl.pallas_call(
        partial(cotangent_kernel, cols, rows, nx),
        out_shape=(
            vmem((total, width), bf16),
            sd((q * nx, VW)),
            sd((q * nx, VW)),
            sd((nx, 8, q)),
            sd((q * nx, VW), bf16),
        ),
        grid_spec=pltpu.PrefetchScalarGridSpec(
            num_scalar_prefetch=1,
            grid=(nx,),
            in_specs=[once(x.shape) for x, _ in pieces]
            + [once(x.shape) for x in xs]
            + [at(depth), at(VW), once((1, VW))],
            out_specs=(
                whole((total, width)),
                at(VW),
                at(VW),
                pl.BlockSpec((1, 8, q), lambda i, off: (off[n + i], 0, 0)),
                at(VW),
            ),
            scratch_shapes=[pltpu.VMEM((q, depth), bf16)],
        ),
        compiler_params=pltpu.CompilerParams(vmem_limit_bytes=30 << 20),
        cost_estimate=pl.CostEstimate(flops=2 * q * nx * total * width, bytes_accessed=30_000_000, transcendentals=800_000),
        name="cotangent",
    )(offsets, *[x for x, _ in pieces], *xs, normed, near_by(ssd), gain)


def turn_kernel(nx, off_ref, *refs):
    i = pl.program_id(0)
    for k in range(nx):

        @pl.when(i == k)
        def _(k=k):
            refs[nx][...] = refs[k][...].T


def turn(offsets, xs):
    q, depth = xs[0].shape
    nx = len(xs)
    n = offsets.shape[0] - nx
    return pl.pallas_call(
        partial(turn_kernel, nx),
        out_shape=sd((depth, q * nx), bf16),
        grid_spec=pltpu.PrefetchScalarGridSpec(
            num_scalar_prefetch=1,
            grid=(nx,),
            in_specs=[once(x.shape) for x in xs],
            out_specs=pl.BlockSpec((depth, q), lambda i, off: (0, off[n + i])),
        ),
        compiler_params=pltpu.CompilerParams(vmem_limit_bytes=8 << 20),
        cost_estimate=pl.CostEstimate(flops=0, bytes_accessed=10_000_000, transcendentals=0),
        name="turn",
    )(offsets, *xs)


def gate_kernel(sum_ref, by_ref, gr_ref, ssd_ref, gain_ref, ny_ref, bg_ref, dy_ref, gg_ref):
    @pl.when(pl.program_id(0) == 0)
    def _():
        gg_ref[...] = jnp.zeros_like(gg_ref)

    sums = sum_ref[0].T
    inv = lax.rsqrt(sums[:, 0:1] / E + EPSILON)
    gr, ssd, by, gain = gr_ref[...], ssd_ref[...], by_ref[...], gain_ref[...]
    sg = sig(gr)
    gate = gr * sg
    unit = ssd * gate * inv
    ny_ref[...] = (unit * gain).astype(bf16)
    gg_ref[0:1, :] += jnp.sum(by * unit, axis=0, keepdims=True)
    back = inv * (by * gain - unit * (inv * sums[:, 1:2] / E))
    bg_ref[...] = (back * ssd * (sg * (1.0 + gr - gate))).astype(bf16)
    dy_ref[...] = back * gate


def gate_back(sums, by, gate_raw, ssd, gain):
    t, width = by.shape
    n, _, q = sums.shape
    rb = pl.BlockSpec((q, width), lambda i: (i, 0))
    return pl.pallas_call(
        gate_kernel,
        out_shape=(sd((t, width), bf16), sd((t, width), bf16), vmem((t, width)), sd((8, width))),
        grid=(n,),
        in_specs=[pl.BlockSpec((1, 8, q), lambda i: (i, 0, 0)), rb, rb, rb, once((1, width))],
        out_specs=(rb, rb, rb, whole((8, width))),
        compiler_params=pltpu.CompilerParams(vmem_limit_bytes=12 << 20),
        cost_estimate=pl.CostEstimate(flops=20_000_000, bytes_accessed=15_000_000, transcendentals=800_000),
        name="gate_back",
    )(sums, by, gate_raw, near_by(ssd), gain)


def normed_kernel(
    half, at_ref, first_ref, gate_ref, w_ref, g_ref, x_ref, h_ref, m_ref, s_ref, mk_ref, mn_ref, ma_ref, mb_ref, away_ref, keep_ref, ng_ref, o_ref, scale_ref
):
    i = pl.program_id(0)

    @pl.when(i == 0)
    def _():
        ng_ref[...] = jnp.zeros_like(ng_ref)
        inv = lax.rsqrt(s_ref[0, 0:1, :] / E + EPSILON) * m_ref[...]
        scale_ref[...] = jnp.broadcast_to(inv, (8, inv.shape[1])).T

    n = o_ref.shape[0]
    scale = scale_ref[pl.ds(pl.multiple_of(i * n, 8), n), 0:1]
    far = jnp.where(i < half, ma_ref[...].astype(f32), mb_ref[...].astype(f32))
    mixed = mk_ref[0].astype(f32) + mn_ref[0].astype(f32) + far
    o_ref[...] = h_ref[...] + scale * mixed
    back = mm(first_ref[...], w_ref[...], 1, 1) + mm(gate_ref[...], g_ref[...], 1, 1)
    ng_ref[0:1, :] += jnp.sum(back * x_ref[...].astype(f32), axis=0, keepdims=True)

    @pl.when(i < half)
    def _():
        away_ref[0] = back.astype(bf16)

    @pl.when(i >= half)
    def _():
        keep_ref[0] = back.astype(bf16)


def back_normed_rows(at, q, first, gate, w, gate_w, normed, hidden, mask, sums, keep, near, far):
    depth = normed.shape[1]
    n = at.shape[0]
    half = n // 2
    rb = lambda c: pl.BlockSpec((q, c), lambda i, at: (at[i], 0))
    part = lambda c: pl.BlockSpec((q // n, c), lambda i, at: (i, 0))
    second = pl.BlockSpec((1, q // n, depth), lambda i, at: (1, i, 0))
    return pl.pallas_call(
        partial(normed_kernel, half),
        out_shape=(sd((half, q, depth), bf16), sd((half, q, depth), bf16), sd((8, depth)), sd((q, depth))),
        grid_spec=pltpu.PrefetchScalarGridSpec(
            num_scalar_prefetch=1,
            grid=(n,),
            in_specs=[rb(RW), rb(VW), once(w.shape), once((depth, VW)), rb(depth)]
            + [part(depth), whole((1, q)), pl.BlockSpec((1, 8, q), lambda i, at: (at[n - 1], 0, 0)), second, second]
            + [
                pl.BlockSpec((q // n, depth), lambda i, at: (jnp.minimum(i, half - 1), 0)),
                pl.BlockSpec((q // n, depth), lambda i, at: (jnp.maximum(i - half, 0), 0)),
            ],
            out_specs=(
                pl.BlockSpec((1, q, depth), lambda i, at: (jnp.minimum(i, half - 1), 0, 0)),
                pl.BlockSpec((1, q, depth), lambda i, at: (jnp.maximum(i - half, 0), 0, 0)),
                whole((8, depth)),
                part(depth),
            ),
            scratch_shapes=[pltpu.VMEM((q, 8), f32)],
        ),
        compiler_params=pltpu.CompilerParams(vmem_limit_bytes=22 << 20),
        cost_estimate=pl.CostEstimate(flops=2 * n * q * depth * (RW + VW), bytes_accessed=60_000_000, transcendentals=0),
        name="back_normed",
    )(at, near_by(first), gate, w, near_by(gate_w), normed, hidden, mask, sums, keep, near, *far)


def mixer_kernel(half, at_ref, x_ref, w_ref, away_ref, keep_ref):
    r = mm(x_ref[...], w_ref[...], 1, 1).astype(bf16)
    i = pl.program_id(0)

    @pl.when(i < half)
    def _():
        away_ref[0] = r

    @pl.when(i >= half)
    def _():
        keep_ref[0] = r


def mixer_blocks(at, q, x, w):
    n, depth, width = at.shape[0], w.shape[0], x.shape[1]
    half = n // 2
    return pl.pallas_call(
        partial(mixer_kernel, half),
        out_shape=(sd((half, q, depth), bf16), sd((half, q, depth), bf16)),
        grid_spec=pltpu.PrefetchScalarGridSpec(
            num_scalar_prefetch=1,
            grid=(n,),
            in_specs=[
                pl.BlockSpec((q, width), lambda i, at: (at[i], 0)),
                pl.BlockSpec((depth, width), lambda i, at: (0, 1), pipeline_mode=pl.Buffered(1)),
            ],
            out_specs=(
                pl.BlockSpec((1, q, depth), lambda i, at: (jnp.minimum(i, half - 1), 0, 0)),
                pl.BlockSpec((1, q, depth), lambda i, at: (jnp.maximum(i - half, 0), 0, 0)),
            ),
        ),
        compiler_params=pltpu.CompilerParams(vmem_limit_bytes=12 << 20),
        cost_estimate=pl.CostEstimate(flops=2 * n * q * depth * width, bytes_accessed=20_000_000, transcendentals=0),
        name="mixer_rows",
    )(at, x, near_by(w))


def grad_kernel(per, rows, at_ref, xt_ref, back_ref, out_ref):
    i = pl.program_id(0)
    r = mm(xt_ref[...], back_ref[...]).astype(bf16)
    for d in range(per):
        out_ref[pl.ds(at_ref[i * per + d], 1)] = r[d * rows : (d + 1) * rows][None]


def weight_grad(at, xt, back, n_dp):
    depth, t = xt.shape
    rows, width = depth // n_dp, back.shape[1]
    steps = 2
    return pl.pallas_call(
        partial(grad_kernel, n_dp // steps, rows),
        out_shape=sd((n_dp, rows, width), bf16),
        grid_spec=pltpu.PrefetchScalarGridSpec(
            num_scalar_prefetch=1,
            grid=(steps,),
            in_specs=[pl.BlockSpec((depth // steps, t), lambda i, at: (i, 0)), once(back.shape)],
            out_specs=whole((n_dp, rows, width)),
        ),
        compiler_params=pltpu.CompilerParams(vmem_limit_bytes=20 << 20),
        cost_estimate=pl.CostEstimate(flops=2 * depth * t * width, bytes_accessed=8_000_000, transcendentals=0),
        name="weight_grad",
    )(at, xt, near_by(back))


def far_pair_kernel(at_ref, xt_ref, back_ref, zt_ref, y_ref, f_ref, b_ref):
    f_ref[...] = mm(xt_ref[...], back_ref[...]).astype(bf16)
    b_ref[...] = mm(zt_ref[...], y_ref[...]).astype(bf16)


def far_value_kernel(mid, at_ref, xt_ref, back_ref, f_ref, b_ref):
    r = mm(xt_ref[...], back_ref[...]).astype(bf16)
    f_ref[...] = r[:, :mid]
    b_ref[...] = r[:, mid:]


def far_grad(at, rows, pairs, mid=0):
    depth, t = pairs[0][0].shape
    block = pl.BlockSpec((rows, t), lambda i, at: (at[0], 0))
    specs, args = [], []
    for xt, back in pairs:
        specs += [block, once(back.shape)]
        args += [xt, back]
    widths = (mid, pairs[0][1].shape[1] - mid) if mid else tuple(b.shape[1] for _, b in pairs)
    return pl.pallas_call(
        partial(far_value_kernel, mid) if mid else far_pair_kernel,
        out_shape=tuple(sd((rows, w), bf16) for w in widths),
        grid_spec=pltpu.PrefetchScalarGridSpec(
            num_scalar_prefetch=1,
            grid=(1,),
            in_specs=specs,
            out_specs=tuple(whole((rows, w)) for w in widths),
        ),
        compiler_params=pltpu.CompilerParams(vmem_limit_bytes=12 << 20),
        cost_estimate=pl.CostEstimate(flops=2 * rows * t * sum(widths), bytes_accessed=4_000_000, transcendentals=0),
        name="far_grad",
    )(at, *args)


def pair_grad_kernel(per, rows, at_ref, xt_ref, back_ref, zt_ref, y_ref, out_ref):
    i = pl.program_id(0)
    for k, r in enumerate((mm(xt_ref[...], back_ref[...]), mm(zt_ref[...], y_ref[...]))):
        r = r.astype(bf16)
        for d in range(per):
            out_ref[pl.ds(at_ref[i * per + d], 1), :, k * VW : (k + 1) * VW] = r[d * rows : (d + 1) * rows][None]


def pair_grad(at, xt, back, zt, y, n_dp):
    depth, t = xt.shape
    rows, steps = depth // n_dp, 4
    rb = pl.BlockSpec((depth // steps, t), lambda i, at: (i, 0))
    return pl.pallas_call(
        partial(pair_grad_kernel, n_dp // steps, rows),
        out_shape=sd((n_dp, rows, 2 * VW), bf16),
        grid_spec=pltpu.PrefetchScalarGridSpec(
            num_scalar_prefetch=1,
            grid=(steps,),
            in_specs=[rb, once(back.shape), rb, once(y.shape)],
            out_specs=whole((n_dp, rows, 2 * VW)),
        ),
        compiler_params=pltpu.CompilerParams(vmem_limit_bytes=22 << 20),
        cost_estimate=pl.CostEstimate(flops=4 * depth * t * VW, bytes_accessed=14_000_000, transcendentals=0),
        name="pair_grad",
    )(at, xt, back, zt, y)


def finish_kernel(
    x_ref, f_ref, b_ref, g_ref, small_ref, gv_ref, steps_ref, taps_ref, bias_ref, gain_ref, sb_ref, dl_ref, skip_ref
):
    value = x_ref[...].astype(f32) + f_ref[...].astype(f32) + b_ref[...].astype(f32)
    gv_ref[:, 0, :] = g_ref[...]
    gv_ref[:, 1, :] = value[:, :VW]
    heads = sb_ref.shape[0]
    steps_ref[...] = value[:, CW:].T[:heads, :]
    taps_ref[...] = small_ref[0:4, :VW]
    bias_ref[...] = small_ref[4, :VW]
    gain_ref[...] = small_ref[6, :VW]
    dl_ref[...] = small_ref[6, VW : VW + heads]
    sb_ref[...] = small_ref[6, VW + 128 : VW + 128 + heads]
    parts = jnp.concatenate(split3(small_ref[0:8, :VW]), axis=0)
    sums = mm(parts, sum_matrix((VW, 128)))
    skip_ref[...] = (sums[5:6] + sums[13:14] + sums[21:22])[0, :heads]


def finish(x, f, b, pair_out, small, heads):
    rows, width = x.shape
    full = whole((rows, width))
    outs = ((rows, 2, VW), (heads, rows), (4, VW), (VW,), (VW,), (heads,), (heads,), (heads,))
    return pl.pallas_call(
        finish_kernel,
        out_shape=tuple(sd(o) for o in outs),
        grid=(1,),
        in_specs=[full, full, full, pl.BlockSpec((rows, VW), lambda i: (0, 0)), whole(small.shape)],
        out_specs=tuple(whole(o) for o in outs),
        compiler_params=pltpu.CompilerParams(vmem_limit_bytes=16 << 20),
        cost_estimate=pl.CostEstimate(flops=1_000_000, bytes_accessed=5_000_000, transcendentals=0),
        name="finish",
    )(x, stay(f), stay(b), pair_out, small)


class Ring:
    def __init__(self, count):
        self.count = count
        self.half = count // 2
        self.order = ring_order(count)
        at = {d: i for i, d in enumerate(self.order)}
        self.table = [[self.order[(at[d] + k) % count] for k in range(count)] for d in range(count)]
        self.ahead = [(self.order[i], self.order[(i + 1) % count]) for i in range(count)]
        self.back = [(b, a) for a, b in self.ahead]

    def rows_of(self, table):
        return jnp.asarray(table, jnp.int32)[lax.axis_index("dp")]

    def hop(self, f, b):
        return lax.ppermute(f, "dp", self.ahead), lax.ppermute(b, "dp", self.back)


class Gather:
    def __init__(self, ring, x, c0=0):
        self.ring, self.mid, self.c0 = ring, x.shape[1] // 2 // 128 * 128, c0
        self.pieces, self.f, self.b, self.s = [(x, c0)], x, x, 0

    def ready(self):
        if self.s == self.ring.half - 1:
            return [self.f[:, : self.mid], self.b[:, self.mid :]]
        return [self.f, self.b]

    def step(self, f, b):
        self.s += 1
        self.f, self.b = self.ring.hop(f, b)
        self.pieces += [(self.f, self.c0), (self.b, self.c0 + (self.mid if self.s == self.ring.half else 0))]

    @staticmethod
    def offsets(ring):
        ahead = [0]
        for s in range(1, ring.half + 1):
            ahead += [ring.count - s, s]
        return [[ring.table[d][k] for k in ahead] for d in range(ring.count)]


class Scatter:
    def __init__(self, ring, first):
        self.ring, self.first, self.x, self.s = ring, list(first), None, ring.half

    def ready(self):
        x, s = self.x, self.s
        if s == self.ring.half:
            return self.first
        f, b = self.f, self.b
        if s == self.ring.half - 1:
            f = jnp.pad(f, ((0, 0), (0, x.shape[2] - f.shape[1])))
            b = jnp.pad(b, ((0, 0), (x.shape[2] - b.shape[1], 0)))
        f = x[s].astype(f32) + f.astype(f32)
        b = x[self.ring.count - s].astype(f32) + b.astype(f32)
        return [f.astype(bf16), b.astype(bf16)]

    def step(self, f, b):
        self.f, self.b = self.ring.hop(f, b)
        self.s -= 1

    def total(self, columns=slice(None)):
        return self.x[0, :, columns].astype(f32) + self.f[:, columns].astype(f32) + self.b[:, columns].astype(f32)


def swap(x, axis, count, bits):
    return lax.ppermute(x, axis, [(i, i ^ bits) for i in range(count)])


def tensor_order(count):
    keys = [0]
    bit = count // 2
    while bit:
        keys += [k ^ bit for k in keys]
        bit //= 2
    return keys


def pick(x, index, axis=0):
    return lax.dynamic_index_in_dim(x, index, axis, keepdims=False)


def groups_of(count):
    bits = [1 << k for k in range(count.bit_length() - 1)]
    first = len(bits) % 2
    return ([bits[:first]] if first else []) + [bits[k : k + 2] for k in range(first, len(bits), 2)]


def others(bits):
    return [bits[0]] if len(bits) == 1 else [bits[0], bits[1], bits[0] | bits[1]]


class Spread:
    def __init__(self, x, axis, count):
        self.x, self.axis, self.count, self.groups = x, axis, count, groups_of(count)

    def step(self, x):
        bits = self.groups.pop(0)
        self.x = sum((swap(x, self.axis, self.count, k) for k in others(bits)), x)


def together(*lists):
    flat = lax.optimization_barrier(tuple(x for xs in lists for x in xs))
    out, at = [], 0
    for xs in lists:
        out.append(list(flat[at : at + len(xs)]))
        at += len(xs)
    return out


def body(
    n_dp,
    n_tensor,
    hidden_in,
    norm_gain,
    gate_value_weight,
    state_proj_weight,
    step_weight,
    conv_value_kernel,
    conv_value_bias,
    conv_state_kernel,
    conv_state_bias,
    step_bias,
    decay_log,
    skip_scale,
    gate_norm_gain,
    out_weight,
    out_cotangent,
    seq_lengths,
    seq_device,
    seq_offset,
):
    quarter = hidden_in.shape[0]
    heads = step_weight.shape[1]
    rows = gate_value_weight.shape[0]
    me, dp = lax.axis_index("tensor"), lax.axis_index("dp")
    ring = Ring(n_dp)
    ring_at = ring.rows_of([[ring.table[d].index(k) for k in range(n_dp)] for d in range(n_dp)])
    far_at = ring.rows_of([[ring.table[d][ring.half]] for d in range(n_dp)])
    order = me ^ jnp.asarray([3, 1, 2, 0], jnp.int32)
    offsets = jnp.concatenate([ring.rows_of(Gather.offsets(ring)), me ^ jnp.asarray(tensor_order(n_tensor), jnp.int32)])
    to_core = lambda x: swap(x, "tensor", n_tensor, 1)
    to_far = lambda x: swap(x, "tensor", n_tensor, 2)

    live_rows, seq_first = span_layout(seq_lengths, seq_device, seq_offset, dp)
    row = me * quarter + jnp.arange(quarter, dtype=jnp.int32)
    local_live = jnp.sum(
        jnp.where((row // SPAN)[:, None] == jnp.arange(SEQ_DEV)[None, :], live_rows[None, :], 0), axis=1
    )
    local_mask = (row % SPAN < local_live).astype(f32)

    pad_to = lambda x, w: jnp.pad(x, (0, w - x.shape[0]))[None]
    params = jnp.concatenate(
        [
            jnp.concatenate([conv_value_kernel, conv_state_kernel], axis=0).T,
            jnp.concatenate([conv_value_bias, conv_state_bias])[None],
            pad_to(step_bias, CW),
            pad_to(decay_log, CW),
            pad_to(jnp.repeat(skip_scale, HW), CW),
        ],
        axis=0,
    )
    gain = gate_norm_gain[None]
    zeros = lambda *s: jnp.zeros(s, f32)

    first_own = jnp.concatenate(
        [gate_value_weight[:, 1, :], state_proj_weight, jnp.pad(step_weight, ((0, 0), (0, 128 - heads)))], axis=1
    )
    first_own, hidden, later = lax.optimization_barrier((first_own, hidden_in, gate_value_weight))
    inv_rms = lax.rsqrt(jnp.mean(hidden * hidden, axis=-1) + EPSILON)
    scaled = hidden * inv_rms[:, None]
    normed_local = (scaled * norm_gain[None, :]).astype(bf16)
    first = Gather(ring, first_own)
    first.step(*first.ready())
    far = to_far(normed_local)
    out_own = jnp.concatenate([later[:, 0, :], out_weight], axis=1)
    back_local = (local_mask[:, None] * out_cotangent).astype(bf16)
    (out_own, offsets, ring_at, far_at, order, seq_first, params, back_local) = lax.optimization_barrier(
        (out_own, offsets, ring_at, far_at, order, seq_first, params, back_local)
    )
    out = Gather(ring, out_own)
    for s in range(1, ring.half):
        extra = []
        if s == min(2, ring.half - 1):
            extra = [[normed_local, far]]
        elif s == ring.half - 1:
            extra = [[back_local] + normed_parts[2:]]
        sends = together(first.ready(), *extra)
        first.step(*sends.pop(0))
        if s == min(2, ring.half - 1):
            [a, far] = sends.pop(0)
            normed_parts = [a, far, to_core(a), to_core(far)]
        elif s == ring.half - 1:
            [back_local, *normed_parts[2:]] = sends.pop(0)
            back_far = to_far(back_local)
    ps, os = together([x for x, _ in first.pieces] + normed_parts, out.ready())
    out.step(*os)
    n = len(first.pieces)
    first_w, normed, normed_t, raw = project(
        [(x, c0) for x, (_, c0) in zip(ps, first.pieces)], offsets, ps[n:], D
    )
    chunks = TOK_DEV // Q
    carry = ()
    for k, (c0, n) in enumerate(FWD_PARTS):
        held, os, bs = together([carry[6]] if carry else [raw], out.ready(), [back_local, back_far] if k == 0 else [])
        out.step(*os)
        if k:
            carry = carry[:6] + (held[0],) + carry[7:]
        else:
            raw = held[0]
            back_parts = bs + [to_core(x) for x in bs]
        carry = tuple(ssd_fwd(c0, n, chunks, seq_first, raw, params, carry))
    held, os, back_parts = together([carry[0]], out.ready(), back_parts)
    carry = (held[0],) + carry[1:]
    out.step(*os)
    back_t = turn(offsets, back_parts)
    while out.s < ring.half:
        out.step(*out.ready())
    ssd, act, slope, states, weights_t, decays_t = carry[:6]

    out_w, gate_raw, back_y, sums, gated = cotangent(
        out.pieces, offsets, back_parts, normed, ssd, gain, D
    )
    total = Spread(sums, "tensor", n_tensor)
    while total.groups:
        total.step(total.x)
    sums = total.x
    mixer = mixer_blocks(order, quarter, gated, out_w)
    sums, mixer_away, mixer_keep = lax.optimization_barrier((sums, *mixer))
    normed_y, back_gate, back_ssd, gain_grad = gate_back(sums, back_y, gate_raw, ssd, gain)
    pair_sum = Scatter(ring, far_grad(far_at, rows, [(normed_t, back_gate), (back_t, normed_y)]))
    ps, [away, mixer_keep, back_gate, normed_y] = together(
        pair_sum.ready(), [mixer_away, mixer_keep, back_gate, normed_y]
    )
    pair_sum.step(*ps)
    mixer_near = to_core(away)
    pair_sum.x = pair_grad(ring_at, normed_t, back_gate, back_t, normed_y, n_dp)
    [pair_sum.f, pair_sum.b, pair_sum.x, mixer_near], = together([pair_sum.f, pair_sum.b, pair_sum.x, mixer_near])

    half_rows = quarter // 2
    away = (mixer_keep[0].astype(f32) + mixer_near[0].astype(f32)).astype(bf16)
    away = [away[:half_rows], away[half_rows:]]
    carry, held, mixer_far = (), [back_ssd], []
    for k, (c0, n) in enumerate(BACK_PARTS):
        ps = pair_sum.ready() if pair_sum.s else []
        held, ps, ms = together(held, ps, away[k : k + 1])
        if carry:
            carry = carry[:1] + (held[0],) + carry[2:]
        else:
            back_ssd = held[0]
        if pair_sum.s:
            pair_sum.step(*ps)
        ms = [to_far(x) for x in ms]
        carry = tuple(
            ssd_bwd(
                c0, n, chunks, seq_first, raw, act, slope, ssd, back_ssd, states, weights_t, decays_t, params, carry
            )
        )
        last = k == len(BACK_PARTS) - 1
        held, [pair_sum.f, pair_sum.b], ms = together([carry[0 if last else 1]], [pair_sum.f, pair_sum.b], ms)
        mixer_far += ms
    carry = (held[0],) + carry[1:]
    while pair_sum.s:
        pair_sum.step(*pair_sum.ready())
    back_first, _, _, _, acc, acs = carry
    value_sum = Scatter(ring, far_grad(far_at, rows, [(normed_t, back_first)], RW // 2 // 128 * 128))
    vs, [back_first] = together(value_sum.ready(), [back_first])
    value_sum.step(*vs)
    value_sum.x = weight_grad(ring_at, normed_t, back_first, n_dp)
    [value_sum.f, value_sum.b, value_sum.x, back_first], = together(
        [value_sum.f, value_sum.b, value_sum.x, back_first]
    )
    vs, [back_first] = together(value_sum.ready(), [back_first])
    value_sum.step(*vs)
    away, keep, ng, output = back_normed_rows(
        order, quarter, back_first, back_gate, first_w, out_w, normed, hidden_in, local_mask[None], sums, mixer_keep, mixer_near, mixer_far
    )
    [value_sum.f, value_sum.b, away, keep, ng], = together([value_sum.f, value_sum.b, away, keep, ng])
    shared = jnp.concatenate([acc[:5, VW:], (ng[0] / norm_gain).reshape(6, 256), zeros(5, 256)], axis=0)
    shared = Spread(shared, "tensor", n_tensor)
    vs, cs, ps = together(value_sum.ready(), [away], [shared.x])
    value_sum.step(*vs)
    near = to_core(cs[0])
    away = (keep[0].astype(f32) + near[0].astype(f32)).astype(bf16)
    got = to_far(away[:half_rows])
    shared.step(ps[0])
    [value_sum.f, value_sum.b, near, away, got, shared.x], = together(
        [value_sum.f, value_sum.b, near, away, got, shared.x]
    )
    own = jnp.concatenate(
        [acc[:6], jnp.concatenate([gain_grad[0], acs[0], acs[1]])[None], zeros(1, CW)], axis=0
    )
    while shared.groups:
        shared.step(shared.x)
    small = Spread(jnp.concatenate([own, shared.x.reshape(4, CW)], axis=0), "dp", n_dp)
    vs, cs, ps = together(value_sum.ready(), [away[half_rows:]], [small.x])
    value_sum.step(*vs)
    cs = [got, to_far(cs[0])]
    small.step(ps[0])
    while value_sum.s:
        value_sum.step(*value_sum.ready())
    [value_sum.f, value_sum.b, small.x], cs = together([value_sum.f, value_sum.b, small.x], cs)
    state_grad = value_sum.total(slice(VW, CW)).reshape(n_tensor, rows // n_tensor, 2 * NS)
    ps, ss = together([small.x], [pick(state_grad, me ^ k) for k in range(n_tensor)])
    state_out = sum((swap(ss[k], "tensor", n_tensor, k) for k in range(1, n_tensor)), ss[0])
    small.x = ps[0]
    while small.groups:
        small.step(small.x)
    small = small.x
    pair_out = pair_sum.total()
    gv_out, step_out, taps, bias, gains, steps, decays, skips = finish(
        value_sum.x[0], value_sum.f, value_sum.b, pair_out, small, heads
    )
    back_rows = keep[1].astype(f32) + near[1].astype(f32) + jnp.concatenate(cs, axis=0).astype(f32)
    back_scaled = back_rows * norm_gain[None, :]
    hidden_gradient = out_cotangent + inv_rms[:, None] * (
        back_scaled - scaled * jnp.mean(back_scaled * scaled, axis=-1)[:, None]
    )
    shared = small[8:].reshape(16, 256)
    index = dp * n_tensor + me
    all_count = n_dp * n_tensor
    kern_share = 2 * NS // all_count
    state_kernel_out = lax.dynamic_slice(shared, (0, index * kern_share), (5, kern_share))
    norm_out = lax.dynamic_slice(shared[5:11].reshape(D), (index * (D // all_count),), (D // all_count,))
    return (
        output,
        hidden_gradient,
        norm_out,
        gv_out,
        state_out,
        step_out.T,
        taps.T,
        bias,
        state_kernel_out[:4].T,
        state_kernel_out[4],
        steps,
        decays,
        skips,
        gains,
        pair_out[:, VW:],
    )


def solution(mesh):
    in_specs = (
        P(("dp", "tensor"), None),
        P(),
        P("dp", None, "tensor"),
        P("dp", None),
        P("dp", "tensor"),
        P("tensor", None),
        P("tensor"),
        P(),
        P(),
        P("tensor"),
        P("tensor"),
        P("tensor"),
        P("tensor"),
        P("dp", "tensor"),
        P(("dp", "tensor"), None),
        P(),
        P(),
        P(),
    )
    out_specs = (
        P(("dp", "tensor"), None),
        P(("dp", "tensor"), None),
        P(("dp", "tensor")),
        P("dp", None, "tensor"),
        P(("dp", "tensor"), None),
        P("dp", "tensor"),
        P("tensor", None),
        P("tensor"),
        P(("dp", "tensor"), None),
        P(("dp", "tensor")),
        P("tensor"),
        P("tensor"),
        P("tensor"),
        P("tensor"),
        P("dp", "tensor"),
    )
    return jax.shard_map(
        partial(body, mesh.shape["dp"], mesh.shape["tensor"]),
        mesh=mesh,
        in_specs=in_specs,
        out_specs=out_specs,
        check_vma=False,
    )
```

profile of v0, /device:TPU:0, one launch (start us, length us, event | category | flops | bytes accessed | tf_op | source)
XLA Modules:
  0.0 256.2 jit_solution(17061856062335336573)
XLA Ops:
  0.7 1.8 slice.141
  2.8 3.1 %collective-permute-start = (bf16[192,1152]{1,0:T(8,128)(2,1)S(1)}, bf16[192,1152]{1,0:T(8,128)(2,1)}, u32[]{:S(2)}, u32[]{:S(2)}) collective-permute-start(bf16[192,1152]{1,0:T(8,128)(2,1)S(1)} %fusion.15.refs_0_), channel_id=1, source_target_pairs={{0,8},{8,16},{16,24},{24,28},{28,20},{20,12},{12,4},{4,0},{1,9},{9... | collective-permute-start | bytes 1327112 | tf_op jit(solution)/shard_map/ppermute | solution.py:706
  6.4 2.0 collective-permute-start.4
  11.2 4.9 %collective-permute-done.refs_1_ = bf16[192,1152]{1,0:T(8,128)(2,1)} collective-permute-done((bf16[192,1152]{1,0:T(8,128)(2,1)S(1)}, bf16[192,1152]{1,0:T(8,128)(2,1)}, u32[]{:S(2)}, u32[]{:S(2)}) %collective-permute-start) | collective-permute-done | bytes 442400 | tf_op jit(solution)/shard_map/ppermute | solution.py:706
  16.1 1.5 collective-permute-done.1.refs_2_
  17.6 1.6 collective-permute-start.2
  19.6 1.7 slice_bitcast_fusion.4
  21.3 4.3 %collective-permute-done.4.refs_10_ = bf16[256,1536]{1,0:T(8,128)(2,1)} collective-permute-done((bf16[256,1536]{1,0:T(8,128)(2,1)S(1)}, bf16[256,1536]{1,0:T(8,128)(2,1)}, u32[]{:S(2)}, u32[]{:S(2)}) %collective-permute-start.4) | collective-permute-done | bytes 786464 | tf_op jit(solution)/shard_map/ppermute | solution.py:757
  25.6 2.9 %collective-permute-done.2.refs_3_ = bf16[192,1152]{1,0:T(8,128)(2,1)S(1)} collective-permute-done((bf16[192,1152]{1,0:T(8,128)(2,1)}, bf16[192,1152]{1,0:T(8,128)(2,1)S(1)}, u32[]{:S(2)}, u32[]{:S(2)}) %collective-permute-start.2) | collective-permute-done | bytes 442400 | tf_op jit(solution)/shard_map/ppermute | solution.py:706
  28.5 1.3 collective-permute-done.3.refs_4_
  30.6 1.2 constant_dynamic-slice_fusion.1
  33.6 1.6 collective-permute-start.5
  35.2 1.6 multiply_convert_fusion.1.refs_9_.refs_0_
  36.7 8.5 %collective-permute-done.6.refs_6_ = bf16[192,1152]{1,0:T(8,128)(2,1)S(1)} collective-permute-done((bf16[192,1152]{1,0:T(8,128)(2,1)}, bf16[192,1152]{1,0:T(8,128)(2,1)S(1)}, u32[]{:S(2)}, u32[]{:S(2)}) %collective-permute-start.6) | collective-permute-done | bytes 442400 | tf_op jit(solution)/shard_map/ppermute | solution.py:706
  45.9 1.5 collective-permute-start.9
  47.4 1.5 collective-permute-start.13
  48.9 2.7 %collective-permute-done.9.refs_7_ = bf16[192,512]{1,0:T(8,128)(2,1)S(1)} collective-permute-done((bf16[192,512]{1,0:T(8,128)(2,1)S(1)}, bf16[192,512]{1,0:T(8,128)(2,1)S(1)}, u32[]{:S(2)}, u32[]{:S(2)}) %collective-permute-start.9) | collective-permute-done | bytes 196640 | tf_op jit(solution)/shard_map/ppermute | solution.py:706
  52.2 1.6 collective-permute-start.11
  54.3 10.2 %project.1 = (bf16[1536,1152]{1,0:T(8,128)(2,1)}, bf16[1024,1536]{1,0:T(8,128)(2,1)S(1)}, bf16[1536,1024]{1,0:T(8,128)(2,1)S(1)}, f32[1024,1152]{1,0:T(8,128)}) custom-call(s32[13]{0:T(128)S(1)} %pad_add_fusion.off_ref, bf16[192,1152]{1,0:T(8,128)(2,1)S(1)} %fusion.15.refs_0_, bf16[192,1152]{1,0:T(8,128)(2,1)} %collective-permute-done.refs_1_, ...), custom_call_target="tpu_custom_call" | custom-call | flops 3623878656 | bytes 30000000 | tf_op jit(solution)/shard_map/project/pallas_call | solution.py:330
  64.4 1.7 copy-done.10
  66.8 1.5 collective-permute-start.14
  69.3 8.5 %ssd_forward_0.1 = (f32[1024,768]{1,0:T(8,128)S(1)}, f32[1024,1024]{1,0:T(8,128)}, f32[1024,1024]{1,0:T(8,128)}, f32[8,128,768]{2,1,0:T(8,128)}, bf16[1024,1536]...) custom-call(s32[4]{0:T(128)S(1)} %convert_element_type.245.first_ref, ...), custom_call_target="tpu_custom_call" | custom-call | flops 750000000 | bytes 15000000 | tf_op jit(solution)/shard_map/ssd_forward_0/pallas_call | solution.py:229
  78.9 1.3 collective-permute-done.15.refs_4_
  80.1 1.5 collective-permute-start.16
  82.2 8.9 %ssd_forward_4.1 = (f32[1024,768]{1,0:T(8,128)S(1)}, f32[1024,1024]{1,0:T(8,128)}, f32[1024,1024]{1,0:T(8,128)}, f32[8,128,768]{2,1,0:T(8,128)}, bf16[1024,1536]...) custom-call(s32[4]{0:T(128)S(1)} %convert_element_type.245.first_ref, ...), custom_call_target="tpu_custom_call", output_to_operand_aliasing={{0}: (5, {}), {1}: (6, {}), {2}: (7, {}), {3}: (8, {}), {4}... | custom-call | flops 750000000 | bytes 15000000 | tf_op jit(solution)/shard_map/ssd_forward_4/pallas_call | solution.py:229
  91.0 2.1 collective-permute-done.16.refs_5_
  93.2 1.2 collective-permute-done.17.refs_6_
  96.6 2.1 turn.1.zt_ref
  98.7 2.6 %collective-permute-done.20.refs_7_ = bf16[192,768]{1,0:T(8,128)(2,1)S(1)} collective-permute-done((bf16[192,768]{1,0:T(8,128)(2,1)S(1)}, bf16[192,768]{1,0:T(8,128)(2,1)S(1)}, u32[]{:S(2)}, u32[]{:S(2)}) %collective-permute-start.20) | collective-permute-done | bytes 294944 | tf_op jit(solution)/shard_map/ppermute | solution.py:706
  102.2 10.1 %cotangent.1 = (bf16[1536,1536]{1,0:T(8,128)(2,1)S(1)}, f32[1024,768]{1,0:T(8,128)S(1)}, f32[1024,768]{1,0:T(8,128)S(1)}, f32[4,8,256]{2,1,0:T(8,128)S(1)}, bf16[1024,768]{1,0:T(8,128)(2,1)S(1)}) custom-call(s32[13]{0:T(128)S(1)} %pad_add_fusion.off_ref, bf16[192,1536]{1,0:T(8,128)(2,1)S(1)} %pad_maximum_fusion.1.refs_0_, ...), custom_call_target="tpu_custom_call" | custom-call | flops 4831838208 | bytes 30000000 | tf_op jit(solution)/shard_map/cotangent/pallas_call | solution.py:381
  112.3 1.6 collective-permute-start.23
  114.2 4.3 %mixer_rows.1 = (bf16[2,256,1536]{2,1,0:T(8,128)(2,1)S(1)}, bf16[2,256,1536]{2,1,0:T(8,128)(2,1)S(1)}) custom-call(s32[4]{0:T(128)S(1)} %get-tuple-element.202.at_ref, bf16[1024,768]{1,0:T(8,128)(2,1)S(1)} %get-tuple-element.267.x_ref, bf16[1536,1536]{1,0:T(8,128)(2,1)S(1)} %get-tuple-element.268.w_ref.g_ref), custom_call_target="tpu_custom_call" | custom-call | flops 2415919104 | bytes 20000000 | tf_op jit(solution)/shard_map/mixer_rows/pallas_call | solution.py:550
  118.5 3.2 %gate_back.1 = (bf16[1024,768]{1,0:T(8,128)(2,1)S(1)}, bf16[1024,768]{1,0:T(8,128)(2,1)S(1)}, f32[1024,768]{1,0:T(8,128)S(1)}, f32[8,768]{1,0:T(8,128)S(1)}) custom-call(f32[4,8,256]{2,1,0:T(8,128)S(1)} %add_add_fusion.2.sum_ref.s_ref, f32[1024,768]{1,0:T(8,128)S(1)} %get-tuple-element.272.by_ref, f32[1024,768]{1,0:T(8,128)S(1)} %get-tuple-element.273.gr_ref, ...), custom_call_target="tpu_custom_call" | custom-call | flops 20000000 | bytes 15000000 | tf_op jit(solution)/shard_map/gate_back/pallas_call | solution.py:461
  121.7 1.4 far_grad.2
  123.6 1.2 collective-permute-start.25
  125.6 6.3 %pair_grad.1 = bf16[8,192,1536]{2,1,0:T(8,128)(2,1)S(1)} custom-call(s32[8]{0:T(128)S(1)} %fusion.27.at_ref, bf16[1536,1024]{1,0:T(8,128)(2,1)S(1)} %copy-done.2, bf16[1024,768]{1,0:T(8,128)(2,1)S(1)} %get-tuple-element.284.back_ref.gate_ref, bf16[1536,1024]{1,0:T(8,128)(2,1)S(1)} %turn.1.zt_ref, bf16[1024,768]{1,0:T(8,128)(2,1)S(1)} %get-tuple-element.285.y_ref), custom_call_target="tpu_custom_call" | custom-call | flops 4831838208 | bytes 14000000 | tf_op jit(solution)/shard_map/pair_grad/pallas_call | solution.py:643
  134.0 1.3 collective-permute-start.28
  136.0 1.5 collective-permute-start.30
  137.5 12.2 %ssd_backward_5.1 = (bf16[1024,1152]{1,0:T(8,128)(2,1)S(1)}, f32[128,768]{1,0:T(8,128)}, f32[128,768]{1,0:T(8,128)}, f32[8,1024]{1,0:T(8,128)S(1)}, f32[8,1024]{1,0:T(8,128)S(1)}, /*index=5*/f32[8,128]{1,0:T(8,128)S(1)}) custom-call(s32[4]{0:T(128)S(1)} %convert_element_type.245.first_ref, f32[1024,1152]{1,0:T(8,128)} %get-tuple-element.238.raw_ref, ...), custom_call_target="tpu_custom_call" | custom-call | flops 1124999936 | bytes 22500000 | tf_op jit(solution)/shard_map/ssd_backward_5/pallas_call | solution.py:244
  150.1 1.3 collective-permute-start.31
  153.1 12.7 %ssd_backward_2.1 = (bf16[1024,1152]{1,0:T(8,128)(2,1)S(1)}, f32[128,768]{1,0:T(8,128)}, f32[128,768]{1,0:T(8,128)}, f32[8,1024]{1,0:T(8,128)S(1)}, f32[8,1024]{1,0:T(8,128)S(1)}, /*index=5*/f32[8,128]{1,0:T(8,128)S(1)}) custom-call(s32[4]{0:T(128)S(1)} %convert_element_type.245.first_ref, ...), custom_call_target="tpu_custom_call", output_to_operand_aliasing={{0}: (15, {})} | custom-call | flops 1124999936 | bytes 22500000 | tf_op jit(solution)/shard_map/ssd_backward_2/pallas_call | solution.py:244
  167.0 1.2 collective-permute-start.35
  168.2 9.8 %ssd_backward_0.1 = (bf16[1024,1152]{1,0:T(8,128)(2,1)S(1)}, f32[128,768]{1,0:T(8,128)}, f32[128,768]{1,0:T(8,128)}, f32[8,1024]{1,0:T(8,128)}, f32[8,1024]{1,0:T(8,128)S(1)}, /*index=5*/f32[8,128]{1,0:T(8,128)S(1)}) custom-call(s32[4]{0:T(128)S(1)} %convert_element_type.245.first_ref, ...), custom_call_target="tpu_custom_call", output_to_operand_aliasing={{0}: (15, {})} | custom-call | flops 750000000 | bytes 15000000 | tf_op jit(solution)/shard_map/ssd_backward_0/pallas_call | solution.py:244
  179.2 1.3 far_grad.3
  182.7 5.0 %weight_grad.1 = bf16[8,192,1152]{2,1,0:T(8,128)(2,1)S(1)} custom-call(s32[8]{0:T(128)S(1)} %fusion.27.at_ref, bf16[1536,1024]{1,0:T(8,128)(2,1)S(1)} %copy-done.2, bf16[1024,1152]{1,0:T(8,128)(2,1)S(1)} %get-tuple-element.335.back_ref.first_ref), custom_call_target="tpu_custom_call" | custom-call | flops 3623878656 | bytes 8000000 | tf_op jit(solution)/shard_map/weight_grad/pallas_call | solution.py:582
  188.7 1.5 collective-permute-start.38
  190.7 10.1 %back_normed.1 = (bf16[2,256,1536]{2,1,0:T(8,128)(2,1)}, bf16[2,256,1536]{2,1,0:T(8,128)(2,1)S(1)}, f32[8,1536]{1,0:T(8,128)S(1)}, f32[256,1536]{1,0:T(8,128)}) custom-call(s32[4]{0:T(128)S(1)} %get-tuple-element.202.at_ref, bf16[1024,1152]{1,0:T(8,128)(2,1)S(1)} %get-tuple-element.335.back_ref.first_ref, ...), custom_call_target="tpu_custom_call" | custom-call | flops 6039797760 | bytes 60000000 | tf_op jit(solution)/shard_map/back_normed/pallas_call | solution.py:508
  201.8 2.6 %fusion.10 = (bf16[192,1152]{1,0:T(8,128)(2,1)}, bf16[192,1152]{1,0:T(8,128)(2,1)}) fusion(bf16[192,1152]{1,0:T(8,128)(2,1)} %copy-done.22, bf16[8,192,1152]{2,1,0:T(8,128)(2,1)} %copy-done.6, bf16[192,1152]{1,0:T(8,128)(2,1)} %copy-done.21), kind=kLoop, calls=%fused_computation.29 | loop fusion | flops 1769472 | bytes 2654208 | tf_op jit(solution)/shard_map/convert_element_type | solution.py:746
  206.6 1.6 collective-permute-start.40
  208.2 1.2 collective-permute-start.41
  209.4 1.3 add_convert_fusion
  211.8 1.3 fusion.1.g_ref
  213.9 5.8 %collective-permute-done.40 = bf16[192,1152]{1,0:T(8,128)(2,1)} collective-permute-done((bf16[192,1152]{1,0:T(8,128)(2,1)}, bf16[192,1152]{1,0:T(8,128)(2,1)}, u32[]{:S(2)}, u32[]{:S(2)}) %collective-permute-start.40) | collective-permute-done | bytes 442400 | tf_op jit(solution)/shard_map/ppermute | solution.py:706
  219.7 1.2 collective-permute-done.41
  222.9 1.6 fusion.8
  226.3 1.3 collective-permute-start.48
  229.8 6.9 %collective-permute-done.50 = bf16[128,1536]{1,0:T(8,128)(2,1)S(1)} collective-permute-done((bf16[128,1536]{1,0:T(8,128)(2,1)S(1)}, bf16[128,1536]{1,0:T(8,128)(2,1)S(1)}, u32[]{:S(2)}, u32[]{:S(2)}) %collective-permute-start.50) | collective-permute-done | bytes 393248 | tf_op jit(solution)/shard_map/ppermute | solution.py:757
  239.6 2.2 collective-permute-start.52
  241.8 1.4 collective-permute-start.53
  243.2 1.3 collective-permute-start.55
  244.4 1.8 multiply_reduce_fusion
  246.3 3.0 %multiply_add_fusion = f32[256,1536]{1,0:T(8,128)} fusion(f32[256,1536]{1,0:T(8,128)S(1)} %copy-done.12, f32[256,1536]{1,0:T(8,128)S(1)} %copy-done, f32[256]{0:T(256)S(1)} %broadcast_multiply_fusion, f32[1536]{0:T(1024)S(1)} %copy-done.23, f32[256]{0:T(256)S(1)} %add_rsqrt_fusion, bf16[2,256,1536]{2,1,0:T(8,128)(2,1)} %collective-permute-done.42, ...), kind=kLoop, calls=%fused_computation.2 | loop fusion | flops 5505024 | bytes 7086080 | tf_op jit(solution)/shard_map/add | solution.py:1006
  251.7 3.0 %finish.1 = (f32[192,2,768]{2,1,0:T(2,128)}, f32[12,192]{1,0:T(8,128)}, f32[4,768]{1,0:T(4,128)}, f32[768]{0:T(1024)}, f32[768]{0:T(1024)}, /*index=5*/f32[12]{0:T(128)}, f32[12]{0:T(128)}, f32[12]{0:T(128)}) custom-call(bf16[192,1152]{1,0:T(8,128)(2,1)S(1)} %slice_bitcast_fusion.x_ref, bf16[192,1152]{1,0:T(8,128)(2,1)} %copy-done.15, ...), custom_call_target="tpu_custom_call" | custom-call | flops 1000000 | bytes 5000000 | tf_op jit(solution)/shard_map/finish/pallas_call | solution.py:680
  254.8 1.5 add_add_fusion.1
  (227 shorter events, 43.0 us)
Async XLA Ops:
  2.8 13.3 %collective-permute-start = (bf16[192,1152]{1,0:T(8,128)(2,1)S(1)}, bf16[192,1152]{1,0:T(8,128)(2,1)}, u32[]{:S(2)}, u32[]{:S(2)}) collective-permute-start(bf16[192,1152]{1,0:T(8,128)(2,1)S(1)} %fusion.15.refs_0_), channel_id=1, source_target_pairs={{0,8},{8,16},{16,24},{24,28},{28,20},{20,12},{12,4},{4,0},{1,9},{9... | collective-permute-start | bytes 1327112 | tf_op jit(solution)/shard_map/ppermute | solution.py:706
  5.8 11.7 %collective-permute-start.1 = (bf16[192,1152]{1,0:T(8,128)(2,1)S(1)}, bf16[192,1152]{1,0:T(8,128)(2,1)}, u32[]{:S(2)}, u32[]{:S(2)}) collective-permute-start(bf16[192,1152]{1,0:T(8,128)(2,1)S(1)} %fusion.15.refs_0_), channel_id=1, source_target_pairs={{8,0},{16,8},{24,16},{28,24},{20,28},{12,20},{4,12},{0,4},{9,1},{1... | collective-permute-start | bytes 1327112 | tf_op jit(solution)/shard_map/ppermute | solution.py:706
  6.2 25.6 %copy-start.33 = (f32[12]{0:T(128)S(1)}, f32[12]{0:T(128)}, u32[]{:S(2)}) copy-start(f32[12]{0:T(128)} %param.34) | copy-start | bytes 148
  6.2 25.7 %copy-start.34 = (f32[12]{0:T(128)S(1)}, f32[12]{0:T(128)}, u32[]{:S(2)}) copy-start(f32[12]{0:T(128)} %param.32) | copy-start | bytes 148
  6.2 25.7 %copy-start.35 = (f32[12]{0:T(128)S(1)}, f32[12]{0:T(128)}, u32[]{:S(2)}) copy-start(f32[12]{0:T(128)} %param.33) | copy-start | bytes 148
  6.4 19.2 %collective-permute-start.4 = (bf16[256,1536]{1,0:T(8,128)(2,1)S(1)}, bf16[256,1536]{1,0:T(8,128)(2,1)}, u32[]{:S(2)}, u32[]{:S(2)}) collective-permute-start(bf16[256,1536]{1,0:T(8,128)(2,1)S(1)} %multiply_convert_fusion.refs_9_), channel_id=1, source_target_pairs={{0,2},{1,3},{2,0},{3,1},{4,6},{5,7},{6,4},{7,5},{8,10},{9,11},{10,... | collective-permute-start | bytes 2359304 | tf_op jit(solution)/shard_map/ppermute | solution.py:757
  17.6 10.9 %collective-permute-start.2 = (bf16[192,1152]{1,0:T(8,128)(2,1)}, bf16[192,1152]{1,0:T(8,128)(2,1)S(1)}, u32[]{:S(2)}, u32[]{:S(2)}) collective-permute-start(bf16[192,1152]{1,0:T(8,128)(2,1)} %collective-permute-done.refs_1_), channel_id=1, source_target_pairs={{0,8},{8,16},{16,24},{24,28},{28,20},{20,12},{12,4},{4,0},{1,9},{9... | collective-permute-start | bytes 1327112 | tf_op jit(solution)/shard_map/ppermute | solution.py:706
  19.2 10.6 %collective-permute-start.3 = (bf16[192,1152]{1,0:T(8,128)(2,1)}, bf16[192,1152]{1,0:T(8,128)(2,1)S(1)}, u32[]{:S(2)}, u32[]{:S(2)}) collective-permute-start(bf16[192,1152]{1,0:T(8,128)(2,1)} %collective-permute-done.1.refs_2_), channel_id=1, source_target_pairs={{8,0},{16,8},{24,16},{28,24},{20,28},{12,20},{4,12},{0,4},{9,1},{1... | collective-permute-start | bytes 1327112 | tf_op jit(solution)/shard_map/ppermute | solution.py:706
  29.8 15.5 %collective-permute-start.7 = (bf16[256,1536]{1,0:T(8,128)(2,1)S(1)}, bf16[256,1536]{1,0:T(8,128)(2,1)}, u32[]{:S(2)}, u32[]{:S(2)}) collective-permute-start(bf16[256,1536]{1,0:T(8,128)(2,1)S(1)} %multiply_convert_fusion.refs_9_), channel_id=1, source_target_pairs={{0,1},{1,0},{2,3},{3,2},{4,5},{5,4},{6,7},{7,6},{8,9},{9,8},{10,11... | collective-permute-start | bytes 2359304 | tf_op jit(solution)/shard_map/ppermute | solution.py:757
  29.8 15.5 %collective-permute-start.8 = (bf16[256,1536]{1,0:T(8,128)(2,1)}, bf16[256,1536]{1,0:T(8,128)(2,1)}, u32[]{:S(2)}, u32[]{:S(2)}) collective-permute-start(bf16[256,1536]{1,0:T(8,128)(2,1)} %collective-permute-done.4.refs_10_), channel_id=1, source_target_pairs={{0,1},{1,0},{2,3},{3,2},{4,5},{5,4},{6,7},{7,6},{8,9},{9,8},{10,11... | collective-permute-start | bytes 2359304 | tf_op jit(solution)/shard_map/ppermute | solution.py:757
  33.1 21.2 %copy-start.8 = (bf16[192,1152]{1,0:T(8,128)(2,1)S(1)}, bf16[192,1152]{1,0:T(8,128)(2,1)}, u32[]{:S(2)}) copy-start(bf16[192,1152]{1,0:T(8,128)(2,1)} %copy-done.7) | copy-start | bytes 1327108
  33.1 12.2 %collective-permute-start.6 = (bf16[192,1152]{1,0:T(8,128)(2,1)}, bf16[192,1152]{1,0:T(8,128)(2,1)S(1)}, u32[]{:S(2)}, u32[]{:S(2)}) collective-permute-start(bf16[192,1152]{1,0:T(8,128)(2,1)} %copy-done.7), channel_id=1, source_target_pairs={{8,0},{16,8},{24,16},{28,24},{20,28},{12,20},{4,12},{0,4},{9,1},{1... | collective-permute-start | bytes 1327112 | tf_op jit(solution)/shard_map/ppermute | solution.py:706
  33.6 11.7 %collective-permute-start.5 = (bf16[192,1152]{1,0:T(8,128)(2,1)S(1)}, bf16[192,1152]{1,0:T(8,128)(2,1)S(1)}, u32[]{:S(2)}, u32[]{:S(2)}) collective-permute-start(bf16[192,1152]{1,0:T(8,128)(2,1)S(1)} %collective-permute-done.2.refs_3_), channel_id=1, source_target_pairs={{0,8},{8,16},{16,24},{24,28},{28,20},{20,12},{12,4},{4,0},{1,9},{9... | collective-permute-start | bytes 1327112 | tf_op jit(solution)/shard_map/ppermute | solution.py:706
  45.4 6.9 %collective-permute-start.10 = (bf16[192,640]{1,0:T(8,128)(2,1)S(1)}, bf16[192,640]{1,0:T(8,128)(2,1)S(1)}, u32[]{:S(2)}, u32[]{:S(2)}) collective-permute-start(bf16[192,640]{1,0:T(8,128)(2,1)S(1)} %slice.190), channel_id=1, source_target_pairs={{8,0},{16,8},{24,16},{28,24},{20,28},{12,20},{4,12},{0,4},{9,1},{1... | collective-permute-start | bytes 737288 | tf_op jit(solution)/shard_map/ppermute | solution.py:706
  45.9 5.7 %collective-permute-start.9 = (bf16[192,512]{1,0:T(8,128)(2,1)S(1)}, bf16[192,512]{1,0:T(8,128)(2,1)S(1)}, u32[]{:S(2)}, u32[]{:S(2)}) collective-permute-start(bf16[192,512]{1,0:T(8,128)(2,1)S(1)} %slice.189), channel_id=1, source_target_pairs={{0,8},{8,16},{16,24},{24,28},{28,20},{20,12},{12,4},{4,0},{1,9},{9... | collective-permute-start | bytes 589832 | tf_op jit(solution)/shard_map/ppermute | solution.py:706
  47.4 18.7 %collective-permute-start.13 = (bf16[256,1536]{1,0:T(8,128)(2,1)S(1)}, bf16[256,1536]{1,0:T(8,128)(2,1)S(1)}, u32[]{:S(2)}, u32[]{:S(2)}) collective-permute-start(bf16[256,1536]{1,0:T(8,128)(2,1)S(1)} %multiply_convert_fusion.1.refs_9_.refs_0_), channel_id=1, source_target_pairs={{0,2},{1,3},{2,0},{3,1},{4,6},{5,7},{6,4},{7,5},{8,10},{9,11},{10,... | collective-permute-start | bytes 2359304 | tf_op jit(solution)/shard_map/ppermute | solution.py:757
  52.2 13.9 %collective-permute-start.11 = (bf16[192,1536]{1,0:T(8,128)(2,1)S(1)}, bf16[192,1536]{1,0:T(8,128)(2,1)S(1)}, u32[]{:S(2)}, u32[]{:S(2)}) collective-permute-start(bf16[192,1536]{1,0:T(8,128)(2,1)S(1)} %pad_maximum_fusion.1.refs_0_), channel_id=1, source_target_pairs={{0,8},{8,16},{16,24},{24,28},{28,20},{20,12},{12,4},{4,0},{1,9},{9... | collective-permute-start | bytes 1769480 | tf_op jit(solution)/shard_map/ppermute | solution.py:706
  53.8 13.0 %collective-permute-start.12 = (bf16[192,1536]{1,0:T(8,128)(2,1)S(1)}, bf16[192,1536]{1,0:T(8,128)(2,1)S(1)}, u32[]{:S(2)}, u32[]{:S(2)}) collective-permute-start(bf16[192,1536]{1,0:T(8,128)(2,1)S(1)} %pad_maximum_fusion.1.refs_0_), channel_id=1, source_target_pairs={{8,0},{16,8},{24,16},{28,24},{20,28},{12,20},{4,12},{0,4},{9,1},{1... | collective-permute-start | bytes 1769480 | tf_op jit(solution)/shard_map/ppermute | solution.py:706
  66.8 12.1 %collective-permute-start.14 = (bf16[192,1536]{1,0:T(8,128)(2,1)S(1)}, bf16[192,1536]{1,0:T(8,128)(2,1)S(1)}, u32[]{:S(2)}, u32[]{:S(2)}) collective-permute-start(bf16[192,1536]{1,0:T(8,128)(2,1)S(1)} %collective-permute-done.11.refs_1_), channel_id=1, source_target_pairs={{0,8},{8,16},{16,24},{24,28},{28,20},{20,12},{12,4},{4,0},{1,9},{9... | collective-permute-start | bytes 1769480 | tf_op jit(solution)/shard_map/ppermute | solution.py:706
  68.3 11.8 %collective-permute-start.15 = (bf16[192,1536]{1,0:T(8,128)(2,1)S(1)}, bf16[192,1536]{1,0:T(8,128)(2,1)S(1)}, u32[]{:S(2)}, u32[]{:S(2)}) collective-permute-start(bf16[192,1536]{1,0:T(8,128)(2,1)S(1)} %collective-permute-done.12.refs_2_), channel_id=1, source_target_pairs={{8,0},{16,8},{24,16},{28,24},{20,28},{12,20},{4,12},{0,4},{9,1},{1... | collective-permute-start | bytes 1769480 | tf_op jit(solution)/shard_map/ppermute | solution.py:706
  68.8 25.6 %collective-permute-start.18 = (bf16[256,1536]{1,0:T(8,128)(2,1)S(1)}, bf16[256,1536]{1,0:T(8,128)(2,1)S(1)}, u32[]{:S(2)}, u32[]{:S(2)}) collective-permute-start(bf16[256,1536]{1,0:T(8,128)(2,1)S(1)} %multiply_convert_fusion.1.refs_9_.refs_0_), channel_id=1, source_target_pairs={{0,1},{1,0},{2,3},{3,2},{4,5},{5,4},{6,7},{7,6},{8,9},{9,8},{10,11... | collective-permute-start | bytes 2359304 | tf_op jit(solution)/shard_map/ppermute | solution.py:757
  68.8 25.6 %collective-permute-start.19 = (bf16[256,1536]{1,0:T(8,128)(2,1)S(1)}, bf16[256,1536]{1,0:T(8,128)(2,1)S(1)}, u32[]{:S(2)}, u32[]{:S(2)}) collective-permute-start(bf16[256,1536]{1,0:T(8,128)(2,1)S(1)} %collective-permute-done.13.refs_10_.refs_1_), channel_id=1, source_target_pairs={{0,1},{1,0},{2,3},{3,2},{4,5},{5,4},{6,7},{7,6},{8,9},{9,8},{10,11... | collective-permute-start | bytes 2359304 | tf_op jit(solution)/shard_map/ppermute | solution.py:757
  80.1 13.1 %collective-permute-start.16 = (bf16[192,1536]{1,0:T(8,128)(2,1)S(1)}, bf16[192,1536]{1,0:T(8,128)(2,1)S(1)}, u32[]{:S(2)}, u32[]{:S(2)}) collective-permute-start(bf16[192,1536]{1,0:T(8,128)(2,1)S(1)} %collective-permute-done.14.refs_3_), channel_id=1, source_target_pairs={{0,8},{8,16},{16,24},{24,28},{28,20},{20,12},{12,4},{4,0},{1,9},{9... | collective-permute-start | bytes 1769480 | tf_op jit(solution)/shard_map/ppermute | solution.py:706
  81.7 12.8 %collective-permute-start.17 = (bf16[192,1536]{1,0:T(8,128)(2,1)S(1)}, bf16[192,1536]{1,0:T(8,128)(2,1)S(1)}, u32[]{:S(2)}, u32[]{:S(2)}) collective-permute-start(bf16[192,1536]{1,0:T(8,128)(2,1)S(1)} %collective-permute-done.15.refs_4_), channel_id=1, source_target_pairs={{8,0},{16,8},{24,16},{28,24},{20,28},{12,20},{4,12},{0,4},{9,1},{1... | collective-permute-start | bytes 1769480 | tf_op jit(solution)/shard_map/ppermute | solution.py:706
  82.2 14.4 %copy-start.27 = (f32[768]{0:T(1024)S(1)}, f32[768]{0:T(1024)}, u32[]{:S(2)}) copy-start(f32[768]{0:T(1024)} %param.35) | copy-start | bytes 9220
  94.5 6.8 %collective-permute-start.20 = (bf16[192,768]{1,0:T(8,128)(2,1)S(1)}, bf16[192,768]{1,0:T(8,128)(2,1)S(1)}, u32[]{:S(2)}, u32[]{:S(2)}) collective-permute-start(bf16[192,768]{1,0:T(8,128)(2,1)S(1)} %slice.191), channel_id=1, source_target_pairs={{0,8},{8,16},{16,24},{24,28},{28,20},{20,12},{12,4},{4,0},{1,9},{9... | collective-permute-start | bytes 884744 | tf_op jit(solution)/shard_map/ppermute | solution.py:706
  95.5 6.7 %collective-permute-start.21 = (bf16[192,768]{1,0:T(8,128)(2,1)S(1)}, bf16[192,768]{1,0:T(8,128)(2,1)S(1)}, u32[]{:S(2)}, u32[]{:S(2)}) collective-permute-start(bf16[192,768]{1,0:T(8,128)(2,1)S(1)} %slice.192), channel_id=1, source_target_pairs={{8,0},{16,8},{24,16},{28,24},{20,28},{12,20},{4,12},{0,4},{9,1},{1... | collective-permute-start | bytes 884744 | tf_op jit(solution)/shard_map/ppermute | solution.py:706
  112.3 6.2 %collective-permute-start.22 = (f32[4,8,256]{2,1,0:T(8,128)S(1)}, f32[4,8,256]{2,1,0:T(8,128)S(1)}, u32[]{:S(2)}, u32[]{:S(2)}) collective-permute-start(f32[4,8,256]{2,1,0:T(8,128)S(1)} %get-tuple-element.266), channel_id=1, source_target_pairs={{0,1},{1,0},{2,3},{3,2},{4,5},{5,4},{6,7},{7,6},{8,9},{9,8},{10,11... | collective-permute-start | bytes 98312 | tf_op jit(solution)/shard_map/ppermute | solution.py:757
  112.3 6.2 %collective-permute-start.23 = (f32[4,8,256]{2,1,0:T(8,128)S(1)}, f32[4,8,256]{2,1,0:T(8,128)S(1)}, u32[]{:S(2)}, u32[]{:S(2)}) collective-permute-start(f32[4,8,256]{2,1,0:T(8,128)S(1)} %get-tuple-element.266), channel_id=1, source_target_pairs={{0,2},{1,3},{2,0},{3,1},{4,6},{5,7},{6,4},{7,5},{8,10},{9,11},{10,... | collective-permute-start | bytes 98312 | tf_op jit(solution)/shard_map/ppermute | solution.py:757
  113.9 4.6 %collective-permute-start.24 = (f32[4,8,256]{2,1,0:T(8,128)S(1)}, f32[4,8,256]{2,1,0:T(8,128)S(1)}, u32[]{:S(2)}, u32[]{:S(2)}) collective-permute-start(f32[4,8,256]{2,1,0:T(8,128)S(1)} %get-tuple-element.266), channel_id=1, source_target_pairs={{0,3},{1,2},{2,1},{3,0},{4,7},{5,6},{6,5},{7,4},{8,11},{9,10},{10,... | collective-permute-start | bytes 98312 | tf_op jit(solution)/shard_map/ppermute | solution.py:757
  123.2 10.4 %collective-permute-start.27 = (bf16[2,256,1536]{2,1,0:T(8,128)(2,1)S(1)}, bf16[2,256,1536]{2,1,0:T(8,128)(2,1)S(1)}, u32[]{:S(2)}, u32[]{:S(2)}) collective-permute-start(bf16[2,256,1536]{2,1,0:T(8,128)(2,1)S(1)} %get-tuple-element.286), channel_id=1, source_target_pairs={{0,1},{1,0},{2,3},{3,2},{4,5},{5,4},{6,7},{7,6},{8,9},{9,8},{10,11... | collective-permute-start | bytes 4718600 | tf_op jit(solution)/shard_map/ppermute | solution.py:757
  123.6 9.1 %collective-permute-start.25 = (bf16[192,768]{1,0:T(8,128)(2,1)S(1)}, bf16[192,768]{1,0:T(8,128)(2,1)S(1)}, u32[]{:S(2)}, u32[]{:S(2)}) collective-permute-start(bf16[192,768]{1,0:T(8,128)(2,1)S(1)} %get-tuple-element.281), channel_id=1, source_target_pairs={{0,8},{8,16},{16,24},{24,28},{28,20},{20,12},{12,4},{4,0},{1,9},{9... | collective-permute-start | bytes 884744 | tf_op jit(solution)/shard_map/ppermute | solution.py:706
  124.7 8.8 %collective-permute-start.26 = (bf16[192,768]{1,0:T(8,128)(2,1)S(1)}, bf16[192,768]{1,0:T(8,128)(2,1)S(1)}, u32[]{:S(2)}, u32[]{:S(2)}) collective-permute-start(bf16[192,768]{1,0:T(8,128)(2,1)S(1)} %get-tuple-element.282), channel_id=1, source_target_pairs={{8,0},{16,8},{24,16},{28,24},{20,28},{12,20},{4,12},{0,4},{9,1},{1... | collective-permute-start | bytes 884744 | tf_op jit(solution)/shard_map/ppermute | solution.py:706
  131.9 33.9 %copy-start.3 = (bf16[8,192,1536]{2,1,0:T(8,128)(2,1)}, bf16[8,192,1536]{2,1,0:T(8,128)(2,1)S(1)}, u32[]{:S(2)}) copy-start(bf16[8,192,1536]{2,1,0:T(8,128)(2,1)S(1)} %pair_grad.1) | copy-start | bytes 14155780
  134.0 15.8 %collective-permute-start.28 = (bf16[192,1536]{1,0:T(8,128)(2,1)S(1)}, bf16[192,1536]{1,0:T(8,128)(2,1)S(1)}, u32[]{:S(2)}, u32[]{:S(2)}) collective-permute-start(bf16[192,1536]{1,0:T(8,128)(2,1)S(1)} %get-tuple-element.297), channel_id=1, source_target_pairs={{0,8},{8,16},{16,24},{24,28},{28,20},{20,12},{12,4},{4,0},{1,9},{9... | collective-permute-start | bytes 1769480 | tf_op jit(solution)/shard_map/ppermute | solution.py:706
  135.2 14.6 %collective-permute-start.29 = (bf16[192,1536]{1,0:T(8,128)(2,1)S(1)}, bf16[192,1536]{1,0:T(8,128)(2,1)S(1)}, u32[]{:S(2)}, u32[]{:S(2)}) collective-permute-start(bf16[192,1536]{1,0:T(8,128)(2,1)S(1)} %get-tuple-element.298), channel_id=1, source_target_pairs={{8,0},{16,8},{24,16},{28,24},{20,28},{12,20},{4,12},{0,4},{9,1},{1... | collective-permute-start | bytes 1769480 | tf_op jit(solution)/shard_map/ppermute | solution.py:706
  136.0 13.7 %collective-permute-start.30 = (bf16[128,1536]{1,0:T(8,128)(2,1)S(1)}, bf16[128,1536]{1,0:T(8,128)(2,1)S(1)}, u32[]{:S(2)}, u32[]{:S(2)}) collective-permute-start(bf16[128,1536]{1,0:T(8,128)(2,1)S(1)} %get-tuple-element.299), channel_id=1, source_target_pairs={{0,2},{1,3},{2,0},{3,1},{4,6},{5,7},{6,4},{7,5},{8,10},{9,11},{10,... | collective-permute-start | bytes 1179656 | tf_op jit(solution)/shard_map/ppermute | solution.py:757
  150.1 15.7 %collective-permute-start.31 = (bf16[192,1536]{1,0:T(8,128)(2,1)S(1)}, bf16[192,1536]{1,0:T(8,128)(2,1)S(1)}, u32[]{:S(2)}, u32[]{:S(2)}) collective-permute-start(bf16[192,1536]{1,0:T(8,128)(2,1)S(1)} %get-tuple-element.310), channel_id=1, source_target_pairs={{0,8},{8,16},{16,24},{24,28},{28,20},{20,12},{12,4},{4,0},{1,9},{9... | collective-permute-start | bytes 1769480 | tf_op jit(solution)/shard_map/ppermute | solution.py:706
  151.4 14.4 %collective-permute-start.32 = (bf16[192,1536]{1,0:T(8,128)(2,1)S(1)}, bf16[192,1536]{1,0:T(8,128)(2,1)S(1)}, u32[]{:S(2)}, u32[]{:S(2)}) collective-permute-start(bf16[192,1536]{1,0:T(8,128)(2,1)S(1)} %get-tuple-element.311), channel_id=1, source_target_pairs={{8,0},{16,8},{24,16},{28,24},{20,28},{12,20},{4,12},{0,4},{9,1},{1... | collective-permute-start | bytes 1769480 | tf_op jit(solution)/shard_map/ppermute | solution.py:706
  152.2 13.6 %collective-permute-start.33 = (bf16[128,1536]{1,0:T(8,128)(2,1)S(1)}, bf16[128,1536]{1,0:T(8,128)(2,1)S(1)}, u32[]{:S(2)}, u32[]{:S(2)}) collective-permute-start(bf16[128,1536]{1,0:T(8,128)(2,1)S(1)} %get-tuple-element.312), channel_id=1, source_target_pairs={{0,2},{1,3},{2,0},{3,1},{4,6},{5,7},{6,4},{7,5},{8,10},{9,11},{10,... | collective-permute-start | bytes 1179656 | tf_op jit(solution)/shard_map/ppermute | solution.py:757
  166.1 12.3 %collective-permute-start.34 = (bf16[192,1536]{1,0:T(8,128)(2,1)S(1)}, bf16[192,1536]{1,0:T(8,128)(2,1)S(1)}, u32[]{:S(2)}, u32[]{:S(2)}) collective-permute-start(bf16[192,1536]{1,0:T(8,128)(2,1)S(1)} %get-tuple-element.323), channel_id=1, source_target_pairs={{0,8},{8,16},{16,24},{24,28},{28,20},{20,12},{12,4},{4,0},{1,9},{9... | collective-permute-start | bytes 1769480 | tf_op jit(solution)/shard_map/ppermute | solution.py:706
  167.0 12.3 %collective-permute-start.35 = (bf16[192,1536]{1,0:T(8,128)(2,1)S(1)}, bf16[192,1536]{1,0:T(8,128)(2,1)S(1)}, u32[]{:S(2)}, u32[]{:S(2)}) collective-permute-start(bf16[192,1536]{1,0:T(8,128)(2,1)S(1)} %get-tuple-element.324), channel_id=1, source_target_pairs={{8,0},{16,8},{24,16},{28,24},{20,28},{12,20},{4,12},{0,4},{9,1},{1... | collective-permute-start | bytes 1769480 | tf_op jit(solution)/shard_map/ppermute | solution.py:706
  180.6 7.9 %collective-permute-start.37 = (bf16[192,640]{1,0:T(8,128)(2,1)S(1)}, bf16[192,640]{1,0:T(8,128)(2,1)S(1)}, u32[]{:S(2)}, u32[]{:S(2)}) collective-permute-start(bf16[192,640]{1,0:T(8,128)(2,1)S(1)} %get-tuple-element.329), channel_id=1, source_target_pairs={{8,0},{16,8},{24,16},{28,24},{20,28},{12,20},{4,12},{0,4},{9,1},{1... | collective-permute-start | bytes 737288 | tf_op jit(solution)/shard_map/ppermute | solution.py:706
  181.6 6.9 %collective-permute-start.36 = (bf16[192,512]{1,0:T(8,128)(2,1)S(1)}, bf16[192,512]{1,0:T(8,128)(2,1)S(1)}, u32[]{:S(2)}, u32[]{:S(2)}) collective-permute-start(bf16[192,512]{1,0:T(8,128)(2,1)S(1)} %get-tuple-element.328), channel_id=1, source_target_pairs={{0,8},{8,16},{16,24},{24,28},{28,20},{20,12},{12,4},{4,0},{1,9},{9... | collective-permute-start | bytes 589832 | tf_op jit(solution)/shard_map/ppermute | solution.py:706
  188.7 12.2 %collective-permute-start.38 = (bf16[192,1152]{1,0:T(8,128)(2,1)S(1)}, bf16[192,1152]{1,0:T(8,128)(2,1)S(1)}, u32[]{:S(2)}, u32[]{:S(2)}) collective-permute-start(bf16[192,1152]{1,0:T(8,128)(2,1)S(1)} %get-tuple-element.340), channel_id=1, source_target_pairs={{0,8},{8,16},{16,24},{24,28},{28,20},{20,12},{12,4},{4,0},{1,9},{9... | collective-permute-start | bytes 1327112 | tf_op jit(solution)/shard_map/ppermute | solution.py:706
  190.2 10.7 %collective-permute-start.39 = (bf16[192,1152]{1,0:T(8,128)(2,1)S(1)}, bf16[192,1152]{1,0:T(8,128)(2,1)S(1)}, u32[]{:S(2)}, u32[]{:S(2)}) collective-permute-start(bf16[192,1152]{1,0:T(8,128)(2,1)S(1)} %get-tuple-element.341), channel_id=1, source_target_pairs={{8,0},{16,8},{24,16},{28,24},{20,28},{12,20},{4,12},{0,4},{9,1},{1... | collective-permute-start | bytes 1327112 | tf_op jit(solution)/shard_map/ppermute | solution.py:706
  204.4 3.8 %collective-permute-start.42 = (bf16[2,256,1536]{2,1,0:T(8,128)(2,1)}, bf16[2,256,1536]{2,1,0:T(8,128)(2,1)}, u32[]{:S(2)}, u32[]{:S(2)}) collective-permute-start(bf16[2,256,1536]{2,1,0:T(8,128)(2,1)} %get-tuple-element.353), channel_id=1, source_target_pairs={{0,1},{1,0},{2,3},{3,2},{4,5},{5,4},{6,7},{7,6},{8,9},{9,8},{10,11... | collective-permute-start | bytes 4718600 | tf_op jit(solution)/shard_map/ppermute | solution.py:757
  204.6 6.1 %collective-permute-start.44 = (f32[16,256]{1,0:T(8,128)S(1)}, f32[16,256]{1,0:T(8,128)S(1)}, u32[]{:S(2)}, u32[]{:S(2)}) collective-permute-start(f32[16,256]{1,0:T(8,128)S(1)} %maximum_maximum_fusion), channel_id=1, source_target_pairs={{0,1},{1,0},{2,3},{3,2},{4,5},{5,4},{6,7},{7,6},{8,9},{9,8},{10,11... | collective-permute-start | bytes 49160 | tf_op jit(solution)/shard_map/ppermute | solution.py:757
  205.2 8.8 %collective-permute-start.45 = (f32[16,256]{1,0:T(8,128)S(1)}, f32[16,256]{1,0:T(8,128)S(1)}, u32[]{:S(2)}, u32[]{:S(2)}) collective-permute-start(f32[16,256]{1,0:T(8,128)S(1)} %maximum_maximum_fusion), channel_id=1, source_target_pairs={{0,2},{1,3},{2,0},{3,1},{4,6},{5,7},{6,4},{7,5},{8,10},{9,11},{10,... | collective-permute-start | bytes 49160 | tf_op jit(solution)/shard_map/ppermute | solution.py:757
  206.3 7.6 %collective-permute-start.46 = (f32[16,256]{1,0:T(8,128)S(1)}, f32[16,256]{1,0:T(8,128)S(1)}, u32[]{:S(2)}, u32[]{:S(2)}) collective-permute-start(f32[16,256]{1,0:T(8,128)S(1)} %maximum_maximum_fusion), channel_id=1, source_target_pairs={{0,3},{1,2},{2,1},{3,0},{4,7},{5,6},{6,5},{7,4},{8,11},{9,10},{10,... | collective-permute-start | bytes 49160 | tf_op jit(solution)/shard_map/ppermute | solution.py:757
  206.6 13.1 %collective-permute-start.40 = (bf16[192,1152]{1,0:T(8,128)(2,1)}, bf16[192,1152]{1,0:T(8,128)(2,1)}, u32[]{:S(2)}, u32[]{:S(2)}) collective-permute-start(bf16[192,1152]{1,0:T(8,128)(2,1)} %get-tuple-element.351), channel_id=1, source_target_pairs={{0,8},{8,16},{16,24},{24,28},{28,20},{20,12},{12,4},{4,0},{1,9},{9... | collective-permute-start | bytes 1327112 | tf_op jit(solution)/shard_map/ppermute | solution.py:706
  208.2 12.7 %collective-permute-start.41 = (bf16[192,1152]{1,0:T(8,128)(2,1)}, bf16[192,1152]{1,0:T(8,128)(2,1)}, u32[]{:S(2)}, u32[]{:S(2)}) collective-permute-start(bf16[192,1152]{1,0:T(8,128)(2,1)} %get-tuple-element.352), channel_id=1, source_target_pairs={{8,0},{16,8},{24,16},{28,24},{20,28},{12,20},{4,12},{0,4},{9,1},{1... | collective-permute-start | bytes 1327112 | tf_op jit(solution)/shard_map/ppermute | solution.py:706
  210.8 11.0 %collective-permute-start.43 = (bf16[128,1536]{1,0:T(8,128)(2,1)S(1)}, bf16[128,1536]{1,0:T(8,128)(2,1)}, u32[]{:S(2)}, u32[]{:S(2)}) collective-permute-start(bf16[128,1536]{1,0:T(8,128)(2,1)S(1)} %slice_bitcast_fusion.1), channel_id=1, source_target_pairs={{0,2},{1,3},{2,0},{3,1},{4,6},{5,7},{6,4},{7,5},{8,10},{9,11},{10,... | collective-permute-start | bytes 1179656 | tf_op jit(solution)/shard_map/ppermute | solution.py:757
  224.5 19.9 %copy-start.5 = (bf16[2,256,1536]{2,1,0:T(8,128)(2,1)S(1)}, bf16[2,256,1536]{2,1,0:T(8,128)(2,1)}, u32[]{:S(2)}) copy-start(bf16[2,256,1536]{2,1,0:T(8,128)(2,1)} %copy-done.4) | copy-start | bytes 4718596
  224.6 5.2 %collective-permute-start.49 = (f32[12,1024]{1,0:T(8,128)S(1)}, f32[12,1024]{1,0:T(8,128)S(1)}, u32[]{:S(2)}, u32[]{:S(2)}) collective-permute-start(f32[12,1024]{1,0:T(8,128)S(1)} %pad_maximum_fusion.2), channel_id=1, source_target_pairs={{0,4},{4,0},{8,12},{12,8},{16,20},{20,16},{24,28},{28,24},{1,5},{5... | collective-permute-start | bytes 147464 | tf_op jit(solution)/shard_map/ppermute | solution.py:757
  225.6 11.5 %collective-permute-start.47 = (bf16[192,1152]{1,0:T(8,128)(2,1)S(1)}, bf16[192,1152]{1,0:T(8,128)(2,1)S(1)}, u32[]{:S(2)}, u32[]{:S(2)}) collective-permute-start(bf16[192,1152]{1,0:T(8,128)(2,1)S(1)} %get-tuple-element.362), channel_id=1, source_target_pairs={{0,8},{8,16},{16,24},{24,28},{28,20},{20,12},{12,4},{4,0},{1,9},{9... | collective-permute-start | bytes 1327112 | tf_op jit(solution)/shard_map/ppermute | solution.py:706
  226.3 10.8 %collective-permute-start.48 = (bf16[192,1152]{1,0:T(8,128)(2,1)S(1)}, bf16[192,1152]{1,0:T(8,128)(2,1)S(1)}, u32[]{:S(2)}, u32[]{:S(2)}) collective-permute-start(bf16[192,1152]{1,0:T(8,128)(2,1)S(1)} %get-tuple-element.363), channel_id=1, source_target_pairs={{8,0},{16,8},{24,16},{28,24},{20,28},{12,20},{4,12},{0,4},{9,1},{1... | collective-permute-start | bytes 1327112 | tf_op jit(solution)/shard_map/ppermute | solution.py:706
  227.6 9.2 %collective-permute-start.50 = (bf16[128,1536]{1,0:T(8,128)(2,1)S(1)}, bf16[128,1536]{1,0:T(8,128)(2,1)S(1)}, u32[]{:S(2)}, u32[]{:S(2)}) collective-permute-start(bf16[128,1536]{1,0:T(8,128)(2,1)S(1)} %slice.173), channel_id=1, source_target_pairs={{0,2},{1,3},{2,0},{3,1},{4,6},{5,7},{6,4},{7,5},{8,10},{9,11},{10,... | collective-permute-start | bytes 1179656 | tf_op jit(solution)/shard_map/ppermute | solution.py:757
  238.8 10.5 %collective-permute-start.51 = (f32[12,1024]{1,0:T(8,128)S(1)}, f32[12,1024]{1,0:T(8,128)S(1)}, u32[]{:S(2)}, u32[]{:S(2)}) collective-permute-start(f32[12,1024]{1,0:T(8,128)S(1)} %add.245), channel_id=1, source_target_pairs={{0,8},{4,12},{8,0},{12,4},{16,24},{20,28},{24,16},{28,20},{1,9},{5... | collective-permute-start | bytes 147464 | tf_op jit(solution)/shard_map/ppermute | solution.py:757
  239.6 10.3 %collective-permute-start.52 = (f32[12,1024]{1,0:T(8,128)S(1)}, f32[12,1024]{1,0:T(8,128)S(1)}, u32[]{:S(2)}, u32[]{:S(2)}) collective-permute-start(f32[12,1024]{1,0:T(8,128)S(1)} %add.245), channel_id=1, source_target_pairs={{0,16},{4,20},{8,24},{12,28},{16,0},{20,4},{24,8},{28,12},{1,17},{... | collective-permute-start | bytes 147464 | tf_op jit(solution)/shard_map/ppermute | solution.py:757
  241.8 8.1 %collective-permute-start.53 = (f32[12,1024]{1,0:T(8,128)S(1)}, f32[12,1024]{1,0:T(8,128)S(1)}, u32[]{:S(2)}, u32[]{:S(2)}) collective-permute-start(f32[12,1024]{1,0:T(8,128)S(1)} %add.245), channel_id=1, source_target_pairs={{0,24},{4,28},{8,16},{12,20},{16,8},{20,12},{24,0},{28,4},{1,25},{... | collective-permute-start | bytes 147464 | tf_op jit(solution)/shard_map/ppermute | solution.py:757
  243.1 11.6 %collective-permute-start.54 = (f32[48,256]{1,0:T(8,128)}, f32[48,256]{1,0:T(8,128)}, u32[]{:S(2)}, u32[]{:S(2)}) collective-permute-start(f32[48,256]{1,0:T(8,128)} %get-tuple-element.377), channel_id=1, source_target_pairs={{0,1},{1,0},{2,3},{3,2},{4,5},{5,4},{6,7},{7,6},{8,9},{9,8},{10,11... | collective-permute-start | bytes 147464 | tf_op jit(solution)/shard_map/ppermute | solution.py:757
  243.2 11.6 %collective-permute-start.55 = (f32[48,256]{1,0:T(8,128)S(1)}, f32[48,256]{1,0:T(8,128)}, u32[]{:S(2)}, u32[]{:S(2)}) collective-permute-start(f32[48,256]{1,0:T(8,128)S(1)} %get-tuple-element.378), channel_id=1, source_target_pairs={{0,2},{1,3},{2,0},{3,1},{4,6},{5,7},{6,4},{7,5},{8,10},{9,11},{10,... | collective-permute-start | bytes 147464 | tf_op jit(solution)/shard_map/ppermute | solution.py:757
  249.3 5.5 %collective-permute-start.56 = (f32[48,256]{1,0:T(8,128)S(1)}, f32[48,256]{1,0:T(8,128)S(1)}, u32[]{:S(2)}, u32[]{:S(2)}) collective-permute-start(f32[48,256]{1,0:T(8,128)S(1)} %get-tuple-element.379), channel_id=1, source_target_pairs={{0,3},{1,2},{2,1},{3,0},{4,7},{5,6},{6,5},{7,4},{8,11},{9,10},{10,... | collective-permute-start | bytes 147464 | tf_op jit(solution)/shard_map/ppermute | solution.py:757
  (32 other events, 143.2 us)
where the time goes:
time: 257 us; the launch traced here: 256 us
  Pallas kernels  109 us (42%)
  waiting for transfers between devices  55.5 us (22%)
  starting transfers between devices  55.2 us (21%)
  other arithmetic  18.9 us (7%)
  local copies, waits for them, and re-layouts  16 us (6%)
    ppermute x32, waiting for transfers between devices, hop(): return (lax.ppermute(f, 'dp', self.ahead), lax.ppermute(b, 'dp', self.back))  43.3 us
    pallas_call x3, Pallas kernels, ssd_bwd(): pl.pallas_call(partial(bwd_kernel, c0, nc, nall), out_shape=(vmem((nall *...  34.7 us
    ppermute x32, starting transfers between devices, hop(): return (lax.ppermute(f, 'dp', self.ahead), lax.ppermute(b, 'dp', self.back))  34.6 us
    ppermute x25, starting transfers between devices, swap(): return lax.ppermute(x, axis, [(i, i ^ bits) for i in range(count)])  20.6 us
    pallas_call x2, Pallas kernels, ssd_fwd(): pl.pallas_call(partial(fwd_kernel, c0, nc), out_shape=(vmem((nall * Q, VW...  17.4 us
    ppermute x25, waiting for transfers between devices, swap(): return lax.ppermute(x, axis, [(i, i ^ bits) for i in range(count)])  12.3 us
    pallas_call x1, Pallas kernels, project(): pl.pallas_call(partial(project_kernel, cols, rows, nx), out_shape=(hbm((t...  10.2 us
    pallas_call x1, Pallas kernels, cotangent(): pl.pallas_call(partial(cotangent_kernel, cols, rows, nx), out_shape=(vmem...  10.1 us
  transfers between devices with their start and end apart: 57, of which 25 were waited for; matrix products, arithmetic and copies ran while one was open for 8% of the time, Pallas kernels for 36%

commit v1 on v0

--- a/solution.py
+++ b/solution.py
@@ -13,8 +13,8 @@
 CW=1024
 RW=1152
 SPAN=256
-FWD_LIMIT=14<<20
-BACK_LIMIT=18<<20
+FWD_LIMIT=12<<20
+BACK_LIMIT=16<<20
 NEG=-1e30
 
 def mm(a,b,ca=1,cb=0):
@@ -308,6 +308,7 @@
 
     @pl.when(i == 0)
     def _():
+        w_ref[:, CW:] = jnp.zeros((w_ref.shape[0], RW - CW), bf16)
         lay(cols, rows, off_ref, refs, w_ref)
 
     for k in range(nx):
@@ -323,7 +324,7 @@
 def project(pieces, offsets, xs, total):
     rows, n = pieces[0][0].shape[0], len(pieces)
     cols = [(c0, x.shape[1]) for x, c0 in pieces]
-    width = max(c0 + w for c0, w in cols)
+    width = RW
     q, depth = xs[0].shape
     nx = len(xs)
     at = lambda w: pl.BlockSpec((q, w), lambda i, off: (off[n + i], 0))
@@ -686,7 +687,7 @@
         compiler_params=pltpu.CompilerParams(vmem_limit_bytes=16 << 20),
         cost_estimate=pl.CostEstimate(flops=1_000_000, bytes_accessed=5_000_000, transcendentals=0),
         name="finish",
-    )(x, stay(f), stay(b), pair_out, small)
+    )(stay(x), stay(f), stay(b), stay(pair_out), small)
 
 
 class Ring:
@@ -825,10 +826,14 @@
     rows = gate_value_weight.shape[0]
     me, dp = lax.axis_index("tensor"), lax.axis_index("dp")
     ring = Ring(n_dp)
-    ring_at = ring.rows_of([[ring.table[d].index(k) for k in range(n_dp)] for d in range(n_dp)])
-    far_at = ring.rows_of([[ring.table[d][ring.half]] for d in range(n_dp)])
+    plan = [
+        [ring.table[d].index(k) for k in range(n_dp)] + [ring.table[d][ring.half]] + Gather.offsets(ring)[d]
+        for d in range(n_dp)
+    ]
+    plan = ring.rows_of(plan)
+    ring_at, far_at = plan[:n_dp], plan[n_dp : n_dp + 1]
     order = me ^ jnp.asarray([3, 1, 2, 0], jnp.int32)
-    offsets = jnp.concatenate([ring.rows_of(Gather.offsets(ring)), me ^ jnp.asarray(tensor_order(n_tensor), jnp.int32)])
+    offsets = jnp.concatenate([plan[n_dp + 1 :], me ^ jnp.asarray(tensor_order(n_tensor), jnp.int32)])
     to_core = lambda x: swap(x, "tensor", n_tensor, 1)
     to_far = lambda x: swap(x, "tensor", n_tensor, 2)
 
@@ -854,7 +859,7 @@
     zeros = lambda *s: jnp.zeros(s, f32)
 
     first_own = jnp.concatenate(
-        [gate_value_weight[:, 1, :], state_proj_weight, jnp.pad(step_weight, ((0, 0), (0, 128 - heads)))], axis=1
+        [gate_value_weight[:, 1, :], state_proj_weight, jnp.pad(step_weight, ((0, 0), (0, 16 - heads)))], axis=1
     )
     first_own, hidden, later = lax.optimization_barrier((first_own, hidden_in, gate_value_weight))
     inv_rms = lax.rsqrt(jnp.mean(hidden * hidden, axis=-1) + EPSILON)

time: 257 us -> 255 us (level)
  transfers between devices with their start and end apart: 57 -> 57, of which waited for: 25 -> 27; matrix products, arithmetic and copies ran while one was open for 8% -> 8% of each run, Pallas kernels for 36% -> 37%
where the time goes in v1:
time: 255 us; the launch traced here: 254 us
  Pallas kernels  109 us (43%)
  waiting for transfers between devices  55.1 us (22%)
  starting transfers between devices  54.8 us (21%)
  other arithmetic  18 us (7%)
  local copies, waits for them, and re-layouts  15.2 us (6%)
    ppermute x32, waiting for transfers between devices, hop(): return (lax.ppermute(f, 'dp', self.ahead), lax.ppermute(b, 'dp', self.back))  43.4 us
    pallas_call x3, Pallas kernels, ssd_bwd(): pl.pallas_call(partial(bwd_kernel, c0, nc, nall), out_shape=(vmem((nall *...  34.7 us
    ppermute x32, starting transfers between devices, hop(): return (lax.ppermute(f, 'dp', self.ahead), lax.ppermute(b, 'dp', self.back))  34 us
    ppermute x25, starting transfers between devices, swap(): return lax.ppermute(x, axis, [(i, i ^ bits) for i in range(count)])  20.8 us
    pallas_call x2, Pallas kernels, ssd_fwd(): pl.pallas_call(partial(fwd_kernel, c0, nc), out_shape=(vmem((nall * Q, VW...  17.4 us
    ppermute x25, waiting for transfers between devices, swap(): return lax.ppermute(x, axis, [(i, i ^ bits) for i in range(count)])  11.7 us
    pallas_call x1, Pallas kernels, project(): pl.pallas_call(partial(project_kernel, cols, rows, nx), out_shape=(hbm((t...  10.2 us
    pallas_call x1, Pallas kernels, cotangent(): pl.pallas_call(partial(cotangent_kernel, cols, rows, nx), out_shape=(vmem...  10.1 us
  transfers between devices with their start and end apart: 57, of which 27 were waited for; matrix products, arithmetic and copies ran while one was open for 8% of the time, Pallas kernels for 37%

profile of v1, /device:TPU:0, one launch (start us, length us, event | category | flops | bytes accessed | tf_op | source)
XLA Modules:
  0.0 254.1 jit_solution(18328727645735310741)
XLA Ops:
  0.7 1.8 slice.159
  2.8 3.1 %collective-permute-start = (bf16[192,1040]{1,0:T(8,128)(2,1)S(1)}, bf16[192,1040]{1,0:T(8,128)(2,1)}, u32[]{:S(2)}, u32[]{:S(2)}) collective-permute-start(bf16[192,1040]{1,0:T(8,128)(2,1)S(1)} %fusion.15.refs_0_), channel_id=1, source_target_pairs={{0,8},{8,16},{16,24},{24,28},{28,20},{20,12},{12,4},{4,0},{1,9},{9... | collective-permute-start | bytes 1198088 | tf_op jit(solution)/shard_map/ppermute | solution.py:707
  6.4 2.0 collective-permute-start.4
  9.6 6.4 %collective-permute-done.refs_1_ = bf16[192,1040]{1,0:T(8,128)(2,1)} collective-permute-done((bf16[192,1040]{1,0:T(8,128)(2,1)S(1)}, bf16[192,1040]{1,0:T(8,128)(2,1)}, u32[]{:S(2)}, u32[]{:S(2)}) %collective-permute-start) | collective-permute-done | bytes 399392 | tf_op jit(solution)/shard_map/ppermute | solution.py:707
  16.1 1.5 collective-permute-done.1.refs_2_
  17.6 1.6 collective-permute-start.2
  19.6 1.1 copy.49
  21.5 4.1 %collective-permute-done.4.refs_10_ = bf16[256,1536]{1,0:T(8,128)(2,1)} collective-permute-done((bf16[256,1536]{1,0:T(8,128)(2,1)S(1)}, bf16[256,1536]{1,0:T(8,128)(2,1)}, u32[]{:S(2)}, u32[]{:S(2)}) %collective-permute-start.4) | collective-permute-done | bytes 786464 | tf_op jit(solution)/shard_map/ppermute | solution.py:758
  25.6 2.9 %collective-permute-done.2.refs_3_ = bf16[192,1040]{1,0:T(8,128)(2,1)S(1)} collective-permute-done((bf16[192,1040]{1,0:T(8,128)(2,1)}, bf16[192,1040]{1,0:T(8,128)(2,1)S(1)}, u32[]{:S(2)}, u32[]{:S(2)}) %collective-permute-start.2) | collective-permute-done | bytes 399392 | tf_op jit(solution)/shard_map/ppermute | solution.py:707
  28.5 1.3 collective-permute-done.3.refs_4_
  31.4 1.1 pad_maximum_fusion.1.refs_0_
  33.0 1.6 collective-permute-start.5
  34.6 1.6 multiply_convert_fusion.1.refs_9_.refs_0_
  36.1 8.5 %collective-permute-done.6.refs_6_ = bf16[192,1040]{1,0:T(8,128)(2,1)S(1)} collective-permute-done((bf16[192,1040]{1,0:T(8,128)(2,1)}, bf16[192,1040]{1,0:T(8,128)(2,1)S(1)}, u32[]{:S(2)}, u32[]{:S(2)}) %collective-permute-start.6) | collective-permute-done | bytes 399392 | tf_op jit(solution)/shard_map/ppermute | solution.py:707
  45.3 1.5 collective-permute-start.9
  46.8 1.5 collective-permute-start.13
  48.3 2.7 %collective-permute-done.9.refs_7_ = bf16[192,512]{1,0:T(8,128)(2,1)S(1)} collective-permute-done((bf16[192,512]{1,0:T(8,128)(2,1)S(1)}, bf16[192,512]{1,0:T(8,128)(2,1)S(1)}, u32[]{:S(2)}, u32[]{:S(2)}) %collective-permute-start.9) | collective-permute-done | bytes 196640 | tf_op jit(solution)/shard_map/ppermute | solution.py:707
  51.6 1.6 collective-permute-start.11
  53.6 10.2 %project.1 = (bf16[1536,1152]{1,0:T(8,128)(2,1)}, bf16[1024,1536]{1,0:T(8,128)(2,1)S(1)}, bf16[1536,1024]{1,0:T(8,128)(2,1)S(1)}, f32[1024,1152]{1,0:T(8,128)}) custom-call(s32[13]{0:T(128)S(1)} %pad_add_fusion.off_ref, bf16[192,1040]{1,0:T(8,128)(2,1)S(1)} %fusion.15.refs_0_, bf16[192,1040]{1,0:T(8,128)(2,1)} %collective-permute-done.refs_1_, ...), custom_call_target="tpu_custom_call" | custom-call | flops 3623878656 | bytes 30000000 | tf_op jit(solution)/shard_map/project/pallas_call | solution.py:331
  63.8 1.7 copy-done.8
  66.2 1.5 collective-permute-start.14
  68.7 8.5 %ssd_forward_0.1 = (f32[1024,768]{1,0:T(8,128)S(1)}, f32[1024,1024]{1,0:T(8,128)}, f32[1024,1024]{1,0:T(8,128)}, f32[8,128,768]{2,1,0:T(8,128)}, bf16[1024,1536]...) custom-call(s32[4]{0:T(128)S(1)} %convert_element_type.245.first_ref, ...), custom_call_target="tpu_custom_call" | custom-call | flops 750000000 | bytes 15000000 | tf_op jit(solution)/shard_map/ssd_forward_0/pallas_call | solution.py:229
  78.3 1.3 collective-permute-done.15.refs_4_
  79.6 1.5 collective-permute-start.16
  81.6 8.9 %ssd_forward_4.1 = (f32[1024,768]{1,0:T(8,128)S(1)}, f32[1024,1024]{1,0:T(8,128)}, f32[1024,1024]{1,0:T(8,128)}, f32[8,128,768]{2,1,0:T(8,128)}, bf16[1024,1536]...) custom-call(s32[4]{0:T(128)S(1)} %convert_element_type.245.first_ref, ...), custom_call_target="tpu_custom_call", output_to_operand_aliasing={{0}: (5, {}), {1}: (6, {}), {2}: (7, {}), {3}: (8, {}), {4}... | custom-call | flops 750000000 | bytes 15000000 | tf_op jit(solution)/shard_map/ssd_forward_4/pallas_call | solution.py:229
  90.5 2.0 collective-permute-done.16.refs_5_
  92.5 1.2 collective-permute-done.17.refs_6_
  95.9 2.1 turn.1.zt_ref
  98.0 2.6 %collective-permute-done.20.refs_7_ = bf16[192,768]{1,0:T(8,128)(2,1)S(1)} collective-permute-done((bf16[192,768]{1,0:T(8,128)(2,1)S(1)}, bf16[192,768]{1,0:T(8,128)(2,1)S(1)}, u32[]{:S(2)}, u32[]{:S(2)}) %collective-permute-start.20) | collective-permute-done | bytes 294944 | tf_op jit(solution)/shard_map/ppermute | solution.py:707
  101.6 10.1 %cotangent.1 = (bf16[1536,1536]{1,0:T(8,128)(2,1)S(1)}, f32[1024,768]{1,0:T(8,128)S(1)}, f32[1024,768]{1,0:T(8,128)S(1)}, f32[4,8,256]{2,1,0:T(8,128)S(1)}, bf16[1024,768]{1,0:T(8,128)(2,1)S(1)}) custom-call(s32[13]{0:T(128)S(1)} %pad_add_fusion.off_ref, bf16[192,1536]{1,0:T(8,128)(2,1)S(1)} %pad_maximum_fusion.1.refs_0_, ...), custom_call_target="tpu_custom_call" | custom-call | flops 4831838208 | bytes 30000000 | tf_op jit(solution)/shard_map/cotangent/pallas_call | solution.py:382
  111.7 1.6 collective-permute-start.23
  113.6 4.3 %mixer_rows.1 = (bf16[2,256,1536]{2,1,0:T(8,128)(2,1)S(1)}, bf16[2,256,1536]{2,1,0:T(8,128)(2,1)S(1)}) custom-call(s32[4]{0:T(128)S(1)} %get-tuple-element.202.at_ref, bf16[1024,768]{1,0:T(8,128)(2,1)S(1)} %get-tuple-element.267.x_ref, bf16[1536,1536]{1,0:T(8,128)(2,1)S(1)} %get-tuple-element.268.w_ref.g_ref), custom_call_target="tpu_custom_call" | custom-call | flops 2415919104 | bytes 20000000 | tf_op jit(solution)/shard_map/mixer_rows/pallas_call | solution.py:551
  117.9 3.2 %gate_back.1 = (bf16[1024,768]{1,0:T(8,128)(2,1)S(1)}, bf16[1024,768]{1,0:T(8,128)(2,1)S(1)}, f32[1024,768]{1,0:T(8,128)S(1)}, f32[8,768]{1,0:T(8,128)S(1)}) custom-call(f32[4,8,256]{2,1,0:T(8,128)S(1)} %add_add_fusion.2.sum_ref.s_ref, f32[1024,768]{1,0:T(8,128)S(1)} %get-tuple-element.272.by_ref, f32[1024,768]{1,0:T(8,128)S(1)} %get-tuple-element.273.gr_ref, ...), custom_call_target="tpu_custom_call" | custom-call | flops 20000000 | bytes 15000000 | tf_op jit(solution)/shard_map/gate_back/pallas_call | solution.py:462
  121.1 1.4 far_grad.2
  123.0 1.2 collective-permute-start.25
  125.0 6.2 %pair_grad.1 = bf16[8,192,1536]{2,1,0:T(8,128)(2,1)S(1)} custom-call(s32[8]{0:T(128)S(1)} %slice_bitcast_fusion.9.at_ref, bf16[1536,1024]{1,0:T(8,128)(2,1)S(1)} %copy-done.2, bf16[1024,768]{1,0:T(8,128)(2,1)S(1)} %get-tuple-element.284.back_ref.gate_ref, bf16[1536,1024]{1,0:T(8,128)(2,1)S(1)} %turn.1.zt_ref, bf16[1024,768]{1,0:T(8,128)(2,1)S(1)} %get-tuple-element.285.y_ref), custom_call_target="tpu_custom_call" | custom-call | flops 4831838208 | bytes 14000000 | tf_op jit(solution)/shard_map/pair_grad/pallas_call | solution.py:644
  133.4 1.2 collective-permute-start.28
  135.5 1.5 collective-permute-start.30
  137.0 12.2 %ssd_backward_5.1 = (bf16[1024,1152]{1,0:T(8,128)(2,1)S(1)}, f32[128,768]{1,0:T(8,128)}, f32[128,768]{1,0:T(8,128)}, f32[8,1024]{1,0:T(8,128)S(1)}, f32[8,1024]{1,0:T(8,128)S(1)}, /*index=5*/f32[8,128]{1,0:T(8,128)S(1)}) custom-call(s32[4]{0:T(128)S(1)} %convert_element_type.245.first_ref, f32[1024,1152]{1,0:T(8,128)} %get-tuple-element.238.raw_ref, ...), custom_call_target="tpu_custom_call" | custom-call | flops 1124999936 | bytes 22500000 | tf_op jit(solution)/shard_map/ssd_backward_5/pallas_call | solution.py:244
  149.5 1.2 collective-permute-start.31
  152.5 12.7 %ssd_backward_2.1 = (bf16[1024,1152]{1,0:T(8,128)(2,1)S(1)}, f32[128,768]{1,0:T(8,128)}, f32[128,768]{1,0:T(8,128)}, f32[8,1024]{1,0:T(8,128)S(1)}, f32[8,1024]{1,0:T(8,128)S(1)}, /*index=5*/f32[8,128]{1,0:T(8,128)S(1)}) custom-call(s32[4]{0:T(128)S(1)} %convert_element_type.245.first_ref, ...), custom_call_target="tpu_custom_call", output_to_operand_aliasing={{0}: (15, {})} | custom-call | flops 1124999936 | bytes 22500000 | tf_op jit(solution)/shard_map/ssd_backward_2/pallas_call | solution.py:244
  166.3 1.2 collective-permute-start.35
  167.6 9.8 %ssd_backward_0.1 = (bf16[1024,1152]{1,0:T(8,128)(2,1)S(1)}, f32[128,768]{1,0:T(8,128)}, f32[128,768]{1,0:T(8,128)}, f32[8,1024]{1,0:T(8,128)}, f32[8,1024]{1,0:T(8,128)S(1)}, /*index=5*/f32[8,128]{1,0:T(8,128)S(1)}) custom-call(s32[4]{0:T(128)S(1)} %convert_element_type.245.first_ref, ...), custom_call_target="tpu_custom_call", output_to_operand_aliasing={{0}: (15, {})} | custom-call | flops 750000000 | bytes 15000000 | tf_op jit(solution)/shard_map/ssd_backward_0/pallas_call | solution.py:244
  178.6 1.3 far_grad.3
  180.9 1.2 collective-permute-start.36
  182.1 5.0 %weight_grad.1 = bf16[8,192,1152]{2,1,0:T(8,128)(2,1)S(1)} custom-call(s32[8]{0:T(128)S(1)} %slice_bitcast_fusion.9.at_ref, bf16[1536,1024]{1,0:T(8,128)(2,1)S(1)} %copy-done.2, bf16[1024,1152]{1,0:T(8,128)(2,1)S(1)} %get-tuple-element.335.back_ref.first_ref), custom_call_target="tpu_custom_call" | custom-call | flops 3623878656 | bytes 8000000 | tf_op jit(solution)/shard_map/weight_grad/pallas_call | solution.py:583
  189.8 10.1 %back_normed.1 = (bf16[2,256,1536]{2,1,0:T(8,128)(2,1)}, bf16[2,256,1536]{2,1,0:T(8,128)(2,1)S(1)}, f32[8,1536]{1,0:T(8,128)S(1)}, f32[256,1536]{1,0:T(8,128)}) custom-call(s32[4]{0:T(128)S(1)} %get-tuple-element.202.at_ref, bf16[1024,1152]{1,0:T(8,128)(2,1)S(1)} %get-tuple-element.335.back_ref.first_ref, ...), custom_call_target="tpu_custom_call" | custom-call | flops 6039797760 | bytes 60000000 | tf_op jit(solution)/shard_map/back_normed/pallas_call | solution.py:509
  200.9 2.6 %fusion.10 = (bf16[192,1152]{1,0:T(8,128)(2,1)}, bf16[192,1152]{1,0:T(8,128)(2,1)}) fusion(bf16[192,1152]{1,0:T(8,128)(2,1)} %copy-done.20, bf16[8,192,1152]{2,1,0:T(8,128)(2,1)} %copy-done.4, bf16[192,1152]{1,0:T(8,128)(2,1)} %copy-done.19), kind=kLoop, calls=%fused_computation.29 | loop fusion | flops 1769472 | bytes 2654208 | tf_op jit(solution)/shard_map/convert_element_type | solution.py:747
  204.2 1.3 collective-permute-start.45
  207.2 1.1 collective-permute-start.41
  208.3 1.3 add_convert_fusion
  209.7 1.3 collective-permute-start.43
  211.0 1.3 fusion.1.g_ref
  214.2 4.6 %collective-permute-done.40 = bf16[192,1152]{1,0:T(8,128)(2,1)} collective-permute-done((bf16[192,1152]{1,0:T(8,128)(2,1)}, bf16[192,1152]{1,0:T(8,128)(2,1)}, u32[]{:S(2)}, u32[]{:S(2)}) %collective-permute-start.40) | collective-permute-done | bytes 442400 | tf_op jit(solution)/shard_map/ppermute | solution.py:707
  221.8 1.6 fusion.8
  224.3 1.3 collective-permute-start.47
  226.3 1.3 collective-permute-start.50
  227.6 1.8 slice_bitcast_fusion.x_ref
  229.5 6.0 %collective-permute-done.50 = bf16[128,1536]{1,0:T(8,128)(2,1)S(1)} collective-permute-done((bf16[128,1536]{1,0:T(8,128)(2,1)S(1)}, bf16[128,1536]{1,0:T(8,128)(2,1)S(1)}, u32[]{:S(2)}, u32[]{:S(2)}) %collective-permute-start.50) | collective-permute-done | bytes 393248 | tf_op jit(solution)/shard_map/ppermute | solution.py:758
  238.0 2.9 %collective-permute-start.52 = (f32[12,1024]{1,0:T(8,128)S(1)}, f32[12,1024]{1,0:T(8,128)S(1)}, u32[]{:S(2)}, u32[]{:S(2)}) collective-permute-start(f32[12,1024]{1,0:T(8,128)S(1)} %add.243), channel_id=1, source_target_pairs={{0,16},{4,20},{8,24},{12,28},{16,0},{20,4},{24,8},{28,12},{1,17},{... | collective-permute-start | bytes 147464 | tf_op jit(solution)/shard_map/ppermute | solution.py:758
  241.6 1.1 collective-permute-start.55
  242.8 1.8 multiply_reduce_fusion
  244.6 3.0 %multiply_add_fusion = f32[256,1536]{1,0:T(8,128)} fusion(f32[256,1536]{1,0:T(8,128)S(1)} %copy-done.11, f32[256,1536]{1,0:T(8,128)S(1)} %copy-done, f32[256]{0:T(256)S(1)} %broadcast_multiply_fusion, f32[1536]{0:T(1024)S(1)} %copy-done.21, f32[256]{0:T(256)S(1)} %add_rsqrt_fusion, bf16[2,256,1536]{2,1,0:T(8,128)(2,1)} %collective-permute-done.42, ...), kind=kLoop, calls=%fused_computation.2 | loop fusion | flops 5505024 | bytes 7086080 | tf_op jit(solution)/shard_map/add | solution.py:1011
  250.1 3.3 %finish.1 = (f32[192,2,768]{2,1,0:T(2,128)}, f32[12,192]{1,0:T(8,128)}, f32[4,768]{1,0:T(4,128)}, f32[768]{0:T(1024)}, f32[768]{0:T(1024)}, /*index=5*/f32[12]{0:T(128)}, f32[12]{0:T(128)}, f32[12]{0:T(128)}) custom-call(bf16[192,1152]{1,0:T(8,128)(2,1)} %slice_bitcast_fusion.x_ref, bf16[192,1152]{1,0:T(8,128)(2,1)} %copy-done.13, ...), custom_call_target="tpu_custom_call" | custom-call | flops 1000000 | bytes 5000000 | tf_op jit(solution)/shard_map/finish/pallas_call | solution.py:681
  (224 shorter events, 42.2 us)
Async XLA Ops:
  2.8 13.3 %collective-permute-start = (bf16[192,1040]{1,0:T(8,128)(2,1)S(1)}, bf16[192,1040]{1,0:T(8,128)(2,1)}, u32[]{:S(2)}, u32[]{:S(2)}) collective-permute-start(bf16[192,1040]{1,0:T(8,128)(2,1)S(1)} %fusion.15.refs_0_), channel_id=1, source_target_pairs={{0,8},{8,16},{16,24},{24,28},{28,20},{20,12},{12,4},{4,0},{1,9},{9... | collective-permute-start | bytes 1198088 | tf_op jit(solution)/shard_map/ppermute | solution.py:707
  5.8 11.7 %collective-permute-start.1 = (bf16[192,1040]{1,0:T(8,128)(2,1)S(1)}, bf16[192,1040]{1,0:T(8,128)(2,1)}, u32[]{:S(2)}, u32[]{:S(2)}) collective-permute-start(bf16[192,1040]{1,0:T(8,128)(2,1)S(1)} %fusion.15.refs_0_), channel_id=1, source_target_pairs={{8,0},{16,8},{24,16},{28,24},{20,28},{12,20},{4,12},{0,4},{9,1},{1... | collective-permute-start | bytes 1198088 | tf_op jit(solution)/shard_map/ppermute | solution.py:707
  6.1 14.6 %copy-start.23 = (f32[768,4]{0,1:T(4,128)S(1)}, f32[768,4]{0,1:T(4,128)}, u32[]{:S(2)}) copy-start(f32[768,4]{0,1:T(4,128)} %param.26) | copy-start | bytes 36868
  6.2 14.6 %copy-start.27 = (f32[256,4]{0,1:T(4,128)S(1)}, f32[256,4]{0,1:T(4,128)}, u32[]{:S(2)}) copy-start(f32[256,4]{0,1:T(4,128)} %param.28) | copy-start | bytes 12292
  6.2 25.0 %copy-start.31 = (f32[12]{0:T(128)S(1)}, f32[12]{0:T(128)}, u32[]{:S(2)}) copy-start(f32[12]{0:T(128)} %param.32) | copy-start | bytes 148
  6.2 25.1 %copy-start.32 = (f32[12]{0:T(128)S(1)}, f32[12]{0:T(128)}, u32[]{:S(2)}) copy-start(f32[12]{0:T(128)} %param.30) | copy-start | bytes 148
  6.2 25.1 %copy-start.33 = (f32[12]{0:T(128)S(1)}, f32[12]{0:T(128)}, u32[]{:S(2)}) copy-start(f32[12]{0:T(128)} %param.31) | copy-start | bytes 148
  6.4 19.2 %collective-permute-start.4 = (bf16[256,1536]{1,0:T(8,128)(2,1)S(1)}, bf16[256,1536]{1,0:T(8,128)(2,1)}, u32[]{:S(2)}, u32[]{:S(2)}) collective-permute-start(bf16[256,1536]{1,0:T(8,128)(2,1)S(1)} %multiply_convert_fusion.refs_9_), channel_id=1, source_target_pairs={{0,2},{1,3},{2,0},{3,1},{4,6},{5,7},{6,4},{7,5},{8,10},{9,11},{10,... | collective-permute-start | bytes 2359304 | tf_op jit(solution)/shard_map/ppermute | solution.py:758
  17.6 10.9 %collective-permute-start.2 = (bf16[192,1040]{1,0:T(8,128)(2,1)}, bf16[192,1040]{1,0:T(8,128)(2,1)S(1)}, u32[]{:S(2)}, u32[]{:S(2)}) collective-permute-start(bf16[192,1040]{1,0:T(8,128)(2,1)} %collective-permute-done.refs_1_), channel_id=1, source_target_pairs={{0,8},{8,16},{16,24},{24,28},{28,20},{20,12},{12,4},{4,0},{1,9},{9... | collective-permute-start | bytes 1198088 | tf_op jit(solution)/shard_map/ppermute | solution.py:707
  19.2 10.6 %collective-permute-start.3 = (bf16[192,1040]{1,0:T(8,128)(2,1)}, bf16[192,1040]{1,0:T(8,128)(2,1)S(1)}, u32[]{:S(2)}, u32[]{:S(2)}) collective-permute-start(bf16[192,1040]{1,0:T(8,128)(2,1)} %collective-permute-done.1.refs_2_), channel_id=1, source_target_pairs={{8,0},{16,8},{24,16},{28,24},{20,28},{12,20},{4,12},{0,4},{9,1},{1... | collective-permute-start | bytes 1198088 | tf_op jit(solution)/shard_map/ppermute | solution.py:707
  29.8 14.9 %collective-permute-start.7 = (bf16[256,1536]{1,0:T(8,128)(2,1)S(1)}, bf16[256,1536]{1,0:T(8,128)(2,1)}, u32[]{:S(2)}, u32[]{:S(2)}) collective-permute-start(bf16[256,1536]{1,0:T(8,128)(2,1)S(1)} %multiply_convert_fusion.refs_9_), channel_id=1, source_target_pairs={{0,1},{1,0},{2,3},{3,2},{4,5},{5,4},{6,7},{7,6},{8,9},{9,8},{10,11... | collective-permute-start | bytes 2359304 | tf_op jit(solution)/shard_map/ppermute | solution.py:758
  29.8 14.9 %collective-permute-start.8 = (bf16[256,1536]{1,0:T(8,128)(2,1)}, bf16[256,1536]{1,0:T(8,128)(2,1)}, u32[]{:S(2)}, u32[]{:S(2)}) collective-permute-start(bf16[256,1536]{1,0:T(8,128)(2,1)} %collective-permute-done.4.refs_10_), channel_id=1, source_target_pairs={{0,1},{1,0},{2,3},{3,2},{4,5},{5,4},{6,7},{7,6},{8,9},{9,8},{10,11... | collective-permute-start | bytes 2359304 | tf_op jit(solution)/shard_map/ppermute | solution.py:758
  32.5 21.2 %copy-start.6 = (bf16[192,1040]{1,0:T(8,128)(2,1)S(1)}, bf16[192,1040]{1,0:T(8,128)(2,1)}, u32[]{:S(2)}) copy-start(bf16[192,1040]{1,0:T(8,128)(2,1)} %copy-done.5) | copy-start | bytes 1198084
  32.5 12.2 %collective-permute-start.6 = (bf16[192,1040]{1,0:T(8,128)(2,1)}, bf16[192,1040]{1,0:T(8,128)(2,1)S(1)}, u32[]{:S(2)}, u32[]{:S(2)}) collective-permute-start(bf16[192,1040]{1,0:T(8,128)(2,1)} %copy-done.5), channel_id=1, source_target_pairs={{8,0},{16,8},{24,16},{28,24},{20,28},{12,20},{4,12},{0,4},{9,1},{1... | collective-permute-start | bytes 1198088 | tf_op jit(solution)/shard_map/ppermute | solution.py:707
  33.0 11.7 %collective-permute-start.5 = (bf16[192,1040]{1,0:T(8,128)(2,1)S(1)}, bf16[192,1040]{1,0:T(8,128)(2,1)S(1)}, u32[]{:S(2)}, u32[]{:S(2)}) collective-permute-start(bf16[192,1040]{1,0:T(8,128)(2,1)S(1)} %collective-permute-done.2.refs_3_), channel_id=1, source_target_pairs={{0,8},{8,16},{16,24},{24,28},{28,20},{20,12},{12,4},{4,0},{1,9},{9... | collective-permute-start | bytes 1198088 | tf_op jit(solution)/shard_map/ppermute | solution.py:707
  44.7 6.9 %collective-permute-start.10 = (bf16[192,528]{1,0:T(8,128)(2,1)S(1)}, bf16[192,528]{1,0:T(8,128)(2,1)S(1)}, u32[]{:S(2)}, u32[]{:S(2)}) collective-permute-start(bf16[192,528]{1,0:T(8,128)(2,1)S(1)} %slice.214), channel_id=1, source_target_pairs={{8,0},{16,8},{24,16},{28,24},{20,28},{12,20},{4,12},{0,4},{9,1},{1... | collective-permute-start | bytes 608264 | tf_op jit(solution)/shard_map/ppermute | solution.py:707
  45.3 5.7 %collective-permute-start.9 = (bf16[192,512]{1,0:T(8,128)(2,1)S(1)}, bf16[192,512]{1,0:T(8,128)(2,1)S(1)}, u32[]{:S(2)}, u32[]{:S(2)}) collective-permute-start(bf16[192,512]{1,0:T(8,128)(2,1)S(1)} %slice.213), channel_id=1, source_target_pairs={{0,8},{8,16},{16,24},{24,28},{28,20},{20,12},{12,4},{4,0},{1,9},{9... | collective-permute-start | bytes 589832 | tf_op jit(solution)/shard_map/ppermute | solution.py:707
  46.8 18.7 %collective-permute-start.13 = (bf16[256,1536]{1,0:T(8,128)(2,1)S(1)}, bf16[256,1536]{1,0:T(8,128)(2,1)S(1)}, u32[]{:S(2)}, u32[]{:S(2)}) collective-permute-start(bf16[256,1536]{1,0:T(8,128)(2,1)S(1)} %multiply_convert_fusion.1.refs_9_.refs_0_), channel_id=1, source_target_pairs={{0,2},{1,3},{2,0},{3,1},{4,6},{5,7},{6,4},{7,5},{8,10},{9,11},{10,... | collective-permute-start | bytes 2359304 | tf_op jit(solution)/shard_map/ppermute | solution.py:758
  51.6 13.9 %collective-permute-start.11 = (bf16[192,1536]{1,0:T(8,128)(2,1)S(1)}, bf16[192,1536]{1,0:T(8,128)(2,1)S(1)}, u32[]{:S(2)}, u32[]{:S(2)}) collective-permute-start(bf16[192,1536]{1,0:T(8,128)(2,1)S(1)} %pad_maximum_fusion.1.refs_0_), channel_id=1, source_target_pairs={{0,8},{8,16},{16,24},{24,28},{28,20},{20,12},{12,4},{4,0},{1,9},{9... | collective-permute-start | bytes 1769480 | tf_op jit(solution)/shard_map/ppermute | solution.py:707
  53.2 13.0 %collective-permute-start.12 = (bf16[192,1536]{1,0:T(8,128)(2,1)S(1)}, bf16[192,1536]{1,0:T(8,128)(2,1)S(1)}, u32[]{:S(2)}, u32[]{:S(2)}) collective-permute-start(bf16[192,1536]{1,0:T(8,128)(2,1)S(1)} %pad_maximum_fusion.1.refs_0_), channel_id=1, source_target_pairs={{8,0},{16,8},{24,16},{28,24},{20,28},{12,20},{4,12},{0,4},{9,1},{1... | collective-permute-start | bytes 1769480 | tf_op jit(solution)/shard_map/ppermute | solution.py:707
  66.2 12.1 %collective-permute-start.14 = (bf16[192,1536]{1,0:T(8,128)(2,1)S(1)}, bf16[192,1536]{1,0:T(8,128)(2,1)S(1)}, u32[]{:S(2)}, u32[]{:S(2)}) collective-permute-start(bf16[192,1536]{1,0:T(8,128)(2,1)S(1)} %collective-permute-done.11.refs_1_), channel_id=1, source_target_pairs={{0,8},{8,16},{16,24},{24,28},{28,20},{20,12},{12,4},{4,0},{1,9},{9... | collective-permute-start | bytes 1769480 | tf_op jit(solution)/shard_map/ppermute | solution.py:707
  67.7 11.9 %collective-permute-start.15 = (bf16[192,1536]{1,0:T(8,128)(2,1)S(1)}, bf16[192,1536]{1,0:T(8,128)(2,1)S(1)}, u32[]{:S(2)}, u32[]{:S(2)}) collective-permute-start(bf16[192,1536]{1,0:T(8,128)(2,1)S(1)} %collective-permute-done.12.refs_2_), channel_id=1, source_target_pairs={{8,0},{16,8},{24,16},{28,24},{20,28},{12,20},{4,12},{0,4},{9,1},{1... | collective-permute-start | bytes 1769480 | tf_op jit(solution)/shard_map/ppermute | solution.py:707
  68.2 25.6 %collective-permute-start.18 = (bf16[256,1536]{1,0:T(8,128)(2,1)S(1)}, bf16[256,1536]{1,0:T(8,128)(2,1)S(1)}, u32[]{:S(2)}, u32[]{:S(2)}) collective-permute-start(bf16[256,1536]{1,0:T(8,128)(2,1)S(1)} %multiply_convert_fusion.1.refs_9_.refs_0_), channel_id=1, source_target_pairs={{0,1},{1,0},{2,3},{3,2},{4,5},{5,4},{6,7},{7,6},{8,9},{9,8},{10,11... | collective-permute-start | bytes 2359304 | tf_op jit(solution)/shard_map/ppermute | solution.py:758
  68.2 25.6 %collective-permute-start.19 = (bf16[256,1536]{1,0:T(8,128)(2,1)S(1)}, bf16[256,1536]{1,0:T(8,128)(2,1)S(1)}, u32[]{:S(2)}, u32[]{:S(2)}) collective-permute-start(bf16[256,1536]{1,0:T(8,128)(2,1)S(1)} %collective-permute-done.13.refs_10_.refs_1_), channel_id=1, source_target_pairs={{0,1},{1,0},{2,3},{3,2},{4,5},{5,4},{6,7},{7,6},{8,9},{9,8},{10,11... | collective-permute-start | bytes 2359304 | tf_op jit(solution)/shard_map/ppermute | solution.py:758
  79.6 12.9 %collective-permute-start.16 = (bf16[192,1536]{1,0:T(8,128)(2,1)S(1)}, bf16[192,1536]{1,0:T(8,128)(2,1)S(1)}, u32[]{:S(2)}, u32[]{:S(2)}) collective-permute-start(bf16[192,1536]{1,0:T(8,128)(2,1)S(1)} %collective-permute-done.14.refs_3_), channel_id=1, source_target_pairs={{0,8},{8,16},{16,24},{24,28},{28,20},{20,12},{12,4},{4,0},{1,9},{9... | collective-permute-start | bytes 1769480 | tf_op jit(solution)/shard_map/ppermute | solution.py:707
  81.1 12.6 %collective-permute-start.17 = (bf16[192,1536]{1,0:T(8,128)(2,1)S(1)}, bf16[192,1536]{1,0:T(8,128)(2,1)S(1)}, u32[]{:S(2)}, u32[]{:S(2)}) collective-permute-start(bf16[192,1536]{1,0:T(8,128)(2,1)S(1)} %collective-permute-done.15.refs_4_), channel_id=1, source_target_pairs={{8,0},{16,8},{24,16},{28,24},{20,28},{12,20},{4,12},{0,4},{9,1},{1... | collective-permute-start | bytes 1769480 | tf_op jit(solution)/shard_map/ppermute | solution.py:707
  93.8 6.8 %collective-permute-start.20 = (bf16[192,768]{1,0:T(8,128)(2,1)S(1)}, bf16[192,768]{1,0:T(8,128)(2,1)S(1)}, u32[]{:S(2)}, u32[]{:S(2)}) collective-permute-start(bf16[192,768]{1,0:T(8,128)(2,1)S(1)} %slice.215), channel_id=1, source_target_pairs={{0,8},{8,16},{16,24},{24,28},{28,20},{20,12},{12,4},{4,0},{1,9},{9... | collective-permute-start | bytes 884744 | tf_op jit(solution)/shard_map/ppermute | solution.py:707
  94.8 6.7 %collective-permute-start.21 = (bf16[192,768]{1,0:T(8,128)(2,1)S(1)}, bf16[192,768]{1,0:T(8,128)(2,1)S(1)}, u32[]{:S(2)}, u32[]{:S(2)}) collective-permute-start(bf16[192,768]{1,0:T(8,128)(2,1)S(1)} %slice.216), channel_id=1, source_target_pairs={{8,0},{16,8},{24,16},{28,24},{20,28},{12,20},{4,12},{0,4},{9,1},{1... | collective-permute-start | bytes 884744 | tf_op jit(solution)/shard_map/ppermute | solution.py:707
  111.7 6.2 %collective-permute-start.22 = (f32[4,8,256]{2,1,0:T(8,128)S(1)}, f32[4,8,256]{2,1,0:T(8,128)S(1)}, u32[]{:S(2)}, u32[]{:S(2)}) collective-permute-start(f32[4,8,256]{2,1,0:T(8,128)S(1)} %get-tuple-element.266), channel_id=1, source_target_pairs={{0,1},{1,0},{2,3},{3,2},{4,5},{5,4},{6,7},{7,6},{8,9},{9,8},{10,11... | collective-permute-start | bytes 98312 | tf_op jit(solution)/shard_map/ppermute | solution.py:758
  111.7 6.2 %collective-permute-start.23 = (f32[4,8,256]{2,1,0:T(8,128)S(1)}, f32[4,8,256]{2,1,0:T(8,128)S(1)}, u32[]{:S(2)}, u32[]{:S(2)}) collective-permute-start(f32[4,8,256]{2,1,0:T(8,128)S(1)} %get-tuple-element.266), channel_id=1, source_target_pairs={{0,2},{1,3},{2,0},{3,1},{4,6},{5,7},{6,4},{7,5},{8,10},{9,11},{10,... | collective-permute-start | bytes 98312 | tf_op jit(solution)/shard_map/ppermute | solution.py:758
  113.3 4.6 %collective-permute-start.24 = (f32[4,8,256]{2,1,0:T(8,128)S(1)}, f32[4,8,256]{2,1,0:T(8,128)S(1)}, u32[]{:S(2)}, u32[]{:S(2)}) collective-permute-start(f32[4,8,256]{2,1,0:T(8,128)S(1)} %get-tuple-element.266), channel_id=1, source_target_pairs={{0,3},{1,2},{2,1},{3,0},{4,7},{5,6},{6,5},{7,4},{8,11},{9,10},{10,... | collective-permute-start | bytes 98312 | tf_op jit(solution)/shard_map/ppermute | solution.py:758
  122.6 10.4 %collective-permute-start.27 = (bf16[2,256,1536]{2,1,0:T(8,128)(2,1)S(1)}, bf16[2,256,1536]{2,1,0:T(8,128)(2,1)S(1)}, u32[]{:S(2)}, u32[]{:S(2)}) collective-permute-start(bf16[2,256,1536]{2,1,0:T(8,128)(2,1)S(1)} %get-tuple-element.286), channel_id=1, source_target_pairs={{0,1},{1,0},{2,3},{3,2},{4,5},{5,4},{6,7},{7,6},{8,9},{9,8},{10,11... | collective-permute-start | bytes 4718600 | tf_op jit(solution)/shard_map/ppermute | solution.py:758
  123.0 9.1 %collective-permute-start.25 = (bf16[192,768]{1,0:T(8,128)(2,1)S(1)}, bf16[192,768]{1,0:T(8,128)(2,1)S(1)}, u32[]{:S(2)}, u32[]{:S(2)}) collective-permute-start(bf16[192,768]{1,0:T(8,128)(2,1)S(1)} %get-tuple-element.281), channel_id=1, source_target_pairs={{0,8},{8,16},{16,24},{24,28},{28,20},{20,12},{12,4},{4,0},{1,9},{9... | collective-permute-start | bytes 884744 | tf_op jit(solution)/shard_map/ppermute | solution.py:707
  124.2 8.8 %collective-permute-start.26 = (bf16[192,768]{1,0:T(8,128)(2,1)S(1)}, bf16[192,768]{1,0:T(8,128)(2,1)S(1)}, u32[]{:S(2)}, u32[]{:S(2)}) collective-permute-start(bf16[192,768]{1,0:T(8,128)(2,1)S(1)} %get-tuple-element.282), channel_id=1, source_target_pairs={{8,0},{16,8},{24,16},{28,24},{20,28},{12,20},{4,12},{0,4},{9,1},{1... | collective-permute-start | bytes 884744 | tf_op jit(solution)/shard_map/ppermute | solution.py:707
  131.3 33.9 %copy-start.3 = (bf16[8,192,1536]{2,1,0:T(8,128)(2,1)}, bf16[8,192,1536]{2,1,0:T(8,128)(2,1)S(1)}, u32[]{:S(2)}) copy-start(bf16[8,192,1536]{2,1,0:T(8,128)(2,1)S(1)} %pair_grad.1) | copy-start | bytes 14155780
  133.4 15.8 %collective-permute-start.28 = (bf16[192,1536]{1,0:T(8,128)(2,1)S(1)}, bf16[192,1536]{1,0:T(8,128)(2,1)S(1)}, u32[]{:S(2)}, u32[]{:S(2)}) collective-permute-start(bf16[192,1536]{1,0:T(8,128)(2,1)S(1)} %get-tuple-element.297), channel_id=1, source_target_pairs={{0,8},{8,16},{16,24},{24,28},{28,20},{20,12},{12,4},{4,0},{1,9},{9... | collective-permute-start | bytes 1769480 | tf_op jit(solution)/shard_map/ppermute | solution.py:707
  134.6 14.6 %collective-permute-start.29 = (bf16[192,1536]{1,0:T(8,128)(2,1)S(1)}, bf16[192,1536]{1,0:T(8,128)(2,1)S(1)}, u32[]{:S(2)}, u32[]{:S(2)}) collective-permute-start(bf16[192,1536]{1,0:T(8,128)(2,1)S(1)} %get-tuple-element.298), channel_id=1, source_target_pairs={{8,0},{16,8},{24,16},{28,24},{20,28},{12,20},{4,12},{0,4},{9,1},{1... | collective-permute-start | bytes 1769480 | tf_op jit(solution)/shard_map/ppermute | solution.py:707
  135.5 13.7 %collective-permute-start.30 = (bf16[128,1536]{1,0:T(8,128)(2,1)S(1)}, bf16[128,1536]{1,0:T(8,128)(2,1)S(1)}, u32[]{:S(2)}, u32[]{:S(2)}) collective-permute-start(bf16[128,1536]{1,0:T(8,128)(2,1)S(1)} %get-tuple-element.299), channel_id=1, source_target_pairs={{0,2},{1,3},{2,0},{3,1},{4,6},{5,7},{6,4},{7,5},{8,10},{9,11},{10,... | collective-permute-start | bytes 1179656 | tf_op jit(solution)/shard_map/ppermute | solution.py:758
  149.5 15.6 %collective-permute-start.31 = (bf16[192,1536]{1,0:T(8,128)(2,1)S(1)}, bf16[192,1536]{1,0:T(8,128)(2,1)S(1)}, u32[]{:S(2)}, u32[]{:S(2)}) collective-permute-start(bf16[192,1536]{1,0:T(8,128)(2,1)S(1)} %get-tuple-element.310), channel_id=1, source_target_pairs={{0,8},{8,16},{16,24},{24,28},{28,20},{20,12},{12,4},{4,0},{1,9},{9... | collective-permute-start | bytes 1769480 | tf_op jit(solution)/shard_map/ppermute | solution.py:707
  150.7 14.4 %collective-permute-start.32 = (bf16[192,1536]{1,0:T(8,128)(2,1)S(1)}, bf16[192,1536]{1,0:T(8,128)(2,1)S(1)}, u32[]{:S(2)}, u32[]{:S(2)}) collective-permute-start(bf16[192,1536]{1,0:T(8,128)(2,1)S(1)} %get-tuple-element.311), channel_id=1, source_target_pairs={{8,0},{16,8},{24,16},{28,24},{20,28},{12,20},{4,12},{0,4},{9,1},{1... | collective-permute-start | bytes 1769480 | tf_op jit(solution)/shard_map/ppermute | solution.py:707
  151.6 13.5 %collective-permute-start.33 = (bf16[128,1536]{1,0:T(8,128)(2,1)S(1)}, bf16[128,1536]{1,0:T(8,128)(2,1)S(1)}, u32[]{:S(2)}, u32[]{:S(2)}) collective-permute-start(bf16[128,1536]{1,0:T(8,128)(2,1)S(1)} %get-tuple-element.312), channel_id=1, source_target_pairs={{0,2},{1,3},{2,0},{3,1},{4,6},{5,7},{6,4},{7,5},{8,10},{9,11},{10,... | collective-permute-start | bytes 1179656 | tf_op jit(solution)/shard_map/ppermute | solution.py:758
  165.5 12.3 %collective-permute-start.34 = (bf16[192,1536]{1,0:T(8,128)(2,1)S(1)}, bf16[192,1536]{1,0:T(8,128)(2,1)S(1)}, u32[]{:S(2)}, u32[]{:S(2)}) collective-permute-start(bf16[192,1536]{1,0:T(8,128)(2,1)S(1)} %get-tuple-element.323), channel_id=1, source_target_pairs={{0,8},{8,16},{16,24},{24,28},{28,20},{20,12},{12,4},{4,0},{1,9},{9... | collective-permute-start | bytes 1769480 | tf_op jit(solution)/shard_map/ppermute | solution.py:707
  166.3 12.3 %collective-permute-start.35 = (bf16[192,1536]{1,0:T(8,128)(2,1)S(1)}, bf16[192,1536]{1,0:T(8,128)(2,1)S(1)}, u32[]{:S(2)}, u32[]{:S(2)}) collective-permute-start(bf16[192,1536]{1,0:T(8,128)(2,1)S(1)} %get-tuple-element.324), channel_id=1, source_target_pairs={{8,0},{16,8},{24,16},{28,24},{20,28},{12,20},{4,12},{0,4},{9,1},{1... | collective-permute-start | bytes 1769480 | tf_op jit(solution)/shard_map/ppermute | solution.py:707
  180.0 7.6 %collective-permute-start.37 = (bf16[192,640]{1,0:T(8,128)(2,1)S(1)}, bf16[192,640]{1,0:T(8,128)(2,1)S(1)}, u32[]{:S(2)}, u32[]{:S(2)}) collective-permute-start(bf16[192,640]{1,0:T(8,128)(2,1)S(1)} %get-tuple-element.329), channel_id=1, source_target_pairs={{8,0},{16,8},{24,16},{28,24},{20,28},{12,20},{4,12},{0,4},{9,1},{1... | collective-permute-start | bytes 737288 | tf_op jit(solution)/shard_map/ppermute | solution.py:707
  180.9 6.7 %collective-permute-start.36 = (bf16[192,512]{1,0:T(8,128)(2,1)S(1)}, bf16[192,512]{1,0:T(8,128)(2,1)S(1)}, u32[]{:S(2)}, u32[]{:S(2)}) collective-permute-start(bf16[192,512]{1,0:T(8,128)(2,1)S(1)} %get-tuple-element.328), channel_id=1, source_target_pairs={{0,8},{8,16},{16,24},{24,28},{28,20},{20,12},{12,4},{4,0},{1,9},{9... | collective-permute-start | bytes 589832 | tf_op jit(solution)/shard_map/ppermute | solution.py:707
  187.7 12.2 %collective-permute-start.38 = (bf16[192,1152]{1,0:T(8,128)(2,1)S(1)}, bf16[192,1152]{1,0:T(8,128)(2,1)S(1)}, u32[]{:S(2)}, u32[]{:S(2)}) collective-permute-start(bf16[192,1152]{1,0:T(8,128)(2,1)S(1)} %get-tuple-element.340), channel_id=1, source_target_pairs={{0,8},{8,16},{16,24},{24,28},{28,20},{20,12},{12,4},{4,0},{1,9},{9... | collective-permute-start | bytes 1327112 | tf_op jit(solution)/shard_map/ppermute | solution.py:707
  188.8 11.2 %collective-permute-start.39 = (bf16[192,1152]{1,0:T(8,128)(2,1)S(1)}, bf16[192,1152]{1,0:T(8,128)(2,1)S(1)}, u32[]{:S(2)}, u32[]{:S(2)}) collective-permute-start(bf16[192,1152]{1,0:T(8,128)(2,1)S(1)} %get-tuple-element.341), channel_id=1, source_target_pairs={{8,0},{16,8},{24,16},{28,24},{20,28},{12,20},{4,12},{0,4},{9,1},{1... | collective-permute-start | bytes 1327112 | tf_op jit(solution)/shard_map/ppermute | solution.py:707
  203.5 3.8 %collective-permute-start.42 = (bf16[2,256,1536]{2,1,0:T(8,128)(2,1)}, bf16[2,256,1536]{2,1,0:T(8,128)(2,1)}, u32[]{:S(2)}, u32[]{:S(2)}) collective-permute-start(bf16[2,256,1536]{2,1,0:T(8,128)(2,1)} %get-tuple-element.353), channel_id=1, source_target_pairs={{0,1},{1,0},{2,3},{3,2},{4,5},{5,4},{6,7},{7,6},{8,9},{9,8},{10,11... | collective-permute-start | bytes 4718600 | tf_op jit(solution)/shard_map/ppermute | solution.py:758
  203.7 6.1 %collective-permute-start.44 = (f32[16,256]{1,0:T(8,128)S(1)}, f32[16,256]{1,0:T(8,128)S(1)}, u32[]{:S(2)}, u32[]{:S(2)}) collective-permute-start(f32[16,256]{1,0:T(8,128)S(1)} %maximum_maximum_fusion), channel_id=1, source_target_pairs={{0,1},{1,0},{2,3},{3,2},{4,5},{5,4},{6,7},{7,6},{8,9},{9,8},{10,11... | collective-permute-start | bytes 49160 | tf_op jit(solution)/shard_map/ppermute | solution.py:758
  204.2 9.9 %collective-permute-start.45 = (f32[16,256]{1,0:T(8,128)S(1)}, f32[16,256]{1,0:T(8,128)S(1)}, u32[]{:S(2)}, u32[]{:S(2)}) collective-permute-start(f32[16,256]{1,0:T(8,128)S(1)} %maximum_maximum_fusion), channel_id=1, source_target_pairs={{0,2},{1,3},{2,0},{3,1},{4,6},{5,7},{6,4},{7,5},{8,10},{9,11},{10,... | collective-permute-start | bytes 49160 | tf_op jit(solution)/shard_map/ppermute | solution.py:758
  205.5 8.6 %collective-permute-start.46 = (f32[16,256]{1,0:T(8,128)S(1)}, f32[16,256]{1,0:T(8,128)S(1)}, u32[]{:S(2)}, u32[]{:S(2)}) collective-permute-start(f32[16,256]{1,0:T(8,128)S(1)} %maximum_maximum_fusion), channel_id=1, source_target_pairs={{0,3},{1,2},{2,1},{3,0},{4,7},{5,6},{6,5},{7,4},{8,11},{9,10},{10,... | collective-permute-start | bytes 49160 | tf_op jit(solution)/shard_map/ppermute | solution.py:758
  205.6 13.1 %collective-permute-start.40 = (bf16[192,1152]{1,0:T(8,128)(2,1)}, bf16[192,1152]{1,0:T(8,128)(2,1)}, u32[]{:S(2)}, u32[]{:S(2)}) collective-permute-start(bf16[192,1152]{1,0:T(8,128)(2,1)} %get-tuple-element.351), channel_id=1, source_target_pairs={{0,8},{8,16},{16,24},{24,28},{28,20},{20,12},{12,4},{4,0},{1,9},{9... | collective-permute-start | bytes 1327112 | tf_op jit(solution)/shard_map/ppermute | solution.py:707
  207.2 12.5 %collective-permute-start.41 = (bf16[192,1152]{1,0:T(8,128)(2,1)}, bf16[192,1152]{1,0:T(8,128)(2,1)}, u32[]{:S(2)}, u32[]{:S(2)}) collective-permute-start(bf16[192,1152]{1,0:T(8,128)(2,1)} %get-tuple-element.352), channel_id=1, source_target_pairs={{8,0},{16,8},{24,16},{28,24},{20,28},{12,20},{4,12},{0,4},{9,1},{1... | collective-permute-start | bytes 1327112 | tf_op jit(solution)/shard_map/ppermute | solution.py:707
  209.7 11.0 %collective-permute-start.43 = (bf16[128,1536]{1,0:T(8,128)(2,1)S(1)}, bf16[128,1536]{1,0:T(8,128)(2,1)}, u32[]{:S(2)}, u32[]{:S(2)}) collective-permute-start(bf16[128,1536]{1,0:T(8,128)(2,1)S(1)} %slice_bitcast_fusion.1), channel_id=1, source_target_pairs={{0,2},{1,3},{2,0},{3,1},{4,6},{5,7},{6,4},{7,5},{8,10},{9,11},{10,... | collective-permute-start | bytes 1179656 | tf_op jit(solution)/shard_map/ppermute | solution.py:758
  223.5 5.9 %collective-permute-start.49 = (f32[12,1024]{1,0:T(8,128)S(1)}, f32[12,1024]{1,0:T(8,128)S(1)}, u32[]{:S(2)}, u32[]{:S(2)}) collective-permute-start(f32[12,1024]{1,0:T(8,128)S(1)} %pad_maximum_fusion.2), channel_id=1, source_target_pairs={{0,4},{4,0},{8,12},{12,8},{16,20},{20,16},{24,28},{28,24},{1,5},{5... | collective-permute-start | bytes 147464 | tf_op jit(solution)/shard_map/ppermute | solution.py:758
  224.3 11.7 %collective-permute-start.47 = (bf16[192,1152]{1,0:T(8,128)(2,1)S(1)}, bf16[192,1152]{1,0:T(8,128)(2,1)S(1)}, u32[]{:S(2)}, u32[]{:S(2)}) collective-permute-start(bf16[192,1152]{1,0:T(8,128)(2,1)S(1)} %get-tuple-element.362), channel_id=1, source_target_pairs={{0,8},{8,16},{16,24},{24,28},{28,20},{20,12},{12,4},{4,0},{1,9},{9... | collective-permute-start | bytes 1327112 | tf_op jit(solution)/shard_map/ppermute | solution.py:707
  225.6 10.5 %collective-permute-start.48 = (bf16[192,1152]{1,0:T(8,128)(2,1)S(1)}, bf16[192,1152]{1,0:T(8,128)(2,1)S(1)}, u32[]{:S(2)}, u32[]{:S(2)}) collective-permute-start(bf16[192,1152]{1,0:T(8,128)(2,1)S(1)} %get-tuple-element.363), channel_id=1, source_target_pairs={{8,0},{16,8},{24,16},{28,24},{20,28},{12,20},{4,12},{0,4},{9,1},{1... | collective-permute-start | bytes 1327112 | tf_op jit(solution)/shard_map/ppermute | solution.py:707
  226.3 9.2 %collective-permute-start.50 = (bf16[128,1536]{1,0:T(8,128)(2,1)S(1)}, bf16[128,1536]{1,0:T(8,128)(2,1)S(1)}, u32[]{:S(2)}, u32[]{:S(2)}) collective-permute-start(bf16[128,1536]{1,0:T(8,128)(2,1)S(1)} %slice.197), channel_id=1, source_target_pairs={{0,2},{1,3},{2,0},{3,1},{4,6},{5,7},{6,4},{7,5},{8,10},{9,11},{10,... | collective-permute-start | bytes 1179656 | tf_op jit(solution)/shard_map/ppermute | solution.py:758
  237.2 10.4 %collective-permute-start.51 = (f32[12,1024]{1,0:T(8,128)S(1)}, f32[12,1024]{1,0:T(8,128)S(1)}, u32[]{:S(2)}, u32[]{:S(2)}) collective-permute-start(f32[12,1024]{1,0:T(8,128)S(1)} %add.243), channel_id=1, source_target_pairs={{0,8},{4,12},{8,0},{12,4},{16,24},{20,28},{24,16},{28,20},{1,9},{5... | collective-permute-start | bytes 147464 | tf_op jit(solution)/shard_map/ppermute | solution.py:758
  238.0 10.3 %collective-permute-start.52 = (f32[12,1024]{1,0:T(8,128)S(1)}, f32[12,1024]{1,0:T(8,128)S(1)}, u32[]{:S(2)}, u32[]{:S(2)}) collective-permute-start(f32[12,1024]{1,0:T(8,128)S(1)} %add.243), channel_id=1, source_target_pairs={{0,16},{4,20},{8,24},{12,28},{16,0},{20,4},{24,8},{28,12},{1,17},{... | collective-permute-start | bytes 147464 | tf_op jit(solution)/shard_map/ppermute | solution.py:758
  240.9 7.4 %collective-permute-start.53 = (f32[12,1024]{1,0:T(8,128)S(1)}, f32[12,1024]{1,0:T(8,128)S(1)}, u32[]{:S(2)}, u32[]{:S(2)}) collective-permute-start(f32[12,1024]{1,0:T(8,128)S(1)} %add.243), channel_id=1, source_target_pairs={{0,24},{4,28},{8,16},{12,20},{16,8},{20,12},{24,0},{28,4},{1,25},{... | collective-permute-start | bytes 147464 | tf_op jit(solution)/shard_map/ppermute | solution.py:758
  241.6 11.8 %collective-permute-start.54 = (f32[48,256]{1,0:T(8,128)S(1)}, f32[48,256]{1,0:T(8,128)S(1)}, u32[]{:S(2)}, u32[]{:S(2)}) collective-permute-start(f32[48,256]{1,0:T(8,128)S(1)} %get-tuple-element.377), channel_id=1, source_target_pairs={{0,1},{1,0},{2,3},{3,2},{4,5},{5,4},{6,7},{7,6},{8,9},{9,8},{10,11... | collective-permute-start | bytes 147464 | tf_op jit(solution)/shard_map/ppermute | solution.py:758
  241.6 11.8 %collective-permute-start.55 = (f32[48,256]{1,0:T(8,128)S(1)}, f32[48,256]{1,0:T(8,128)S(1)}, u32[]{:S(2)}, u32[]{:S(2)}) collective-permute-start(f32[48,256]{1,0:T(8,128)S(1)} %get-tuple-element.378), channel_id=1, source_target_pairs={{0,2},{1,3},{2,0},{3,1},{4,6},{5,7},{6,4},{7,5},{8,10},{9,11},{10,... | collective-permute-start | bytes 147464 | tf_op jit(solution)/shard_map/ppermute | solution.py:758
  247.6 5.9 %collective-permute-start.56 = (f32[48,256]{1,0:T(8,128)S(1)}, f32[48,256]{1,0:T(8,128)S(1)}, u32[]{:S(2)}, u32[]{:S(2)}) collective-permute-start(f32[48,256]{1,0:T(8,128)S(1)} %get-tuple-element.379), channel_id=1, source_target_pairs={{0,3},{1,2},{2,1},{3,0},{4,7},{5,6},{6,5},{7,4},{8,11},{9,10},{10,... | collective-permute-start | bytes 147464 | tf_op jit(solution)/shard_map/ppermute | solution.py:758
  (30 other events, 135.8 us)

commit v2 on v1

--- a/solution.py
+++ b/solution.py
@@ -831,7 +831,7 @@
         for d in range(n_dp)
     ]
     plan = ring.rows_of(plan)
-    ring_at, far_at = plan[:n_dp], plan[n_dp : n_dp + 1]
+    ring_at, far_at = plan, plan[n_dp : n_dp + 1]
     order = me ^ jnp.asarray([3, 1, 2, 0], jnp.int32)
     offsets = jnp.concatenate([plan[n_dp + 1 :], me ^ jnp.asarray(tensor_order(n_tensor), jnp.int32)])
     to_core = lambda x: swap(x, "tensor", n_tensor, 1)

time: 255 us -> 255 us (level)
  no operation moved by 1% of the time
where the time goes in v2:
time: 255 us; the launch traced here: 254 us
  Pallas kernels  109 us (43%)
  waiting for transfers between devices  55.1 us (22%)
  starting transfers between devices  54.8 us (21%)
  other arithmetic  18 us (7%)
  local copies, waits for them, and re-layouts  15.2 us (6%)
    ppermute x32, waiting for transfers between devices, hop(): return (lax.ppermute(f, 'dp', self.ahead), lax.ppermute(b, 'dp', self.back))  43.5 us
    pallas_call x3, Pallas kernels, ssd_bwd(): pl.pallas_call(partial(bwd_kernel, c0, nc, nall), out_shape=(vmem((nall *...  34.7 us
    ppermute x32, starting transfers between devices, hop(): return (lax.ppermute(f, 'dp', self.ahead), lax.ppermute(b, 'dp', self.back))  33.9 us
    ppermute x25, starting transfers between devices, swap(): return lax.ppermute(x, axis, [(i, i ^ bits) for i in range(count)])  21 us
    pallas_call x2, Pallas kernels, ssd_fwd(): pl.pallas_call(partial(fwd_kernel, c0, nc), out_shape=(vmem((nall * Q, VW...  17.4 us
    ppermute x25, waiting for transfers between devices, swap(): return lax.ppermute(x, axis, [(i, i ^ bits) for i in range(count)])  11.6 us
    pallas_call x1, Pallas kernels, project(): pl.pallas_call(partial(project_kernel, cols, rows, nx), out_shape=(hbm((t...  10.2 us
    pallas_call x1, Pallas kernels, cotangent(): pl.pallas_call(partial(cotangent_kernel, cols, rows, nx), out_shape=(vmem...  10.1 us
  transfers between devices with their start and end apart: 57, of which 27 were waited for; matrix products, arithmetic and copies ran while one was open for 8% of the time, Pallas kernels for 37%

profile of v2, /device:TPU:0, one launch (start us, length us, event | category | flops | bytes accessed | tf_op | source)
XLA Modules:
  0.0 254.2 jit_solution(3768427486154481180)
XLA Ops:
  0.7 1.8 slice.153
  2.8 3.1 %collective-permute-start = (bf16[192,1040]{1,0:T(8,128)(2,1)S(1)}, bf16[192,1040]{1,0:T(8,128)(2,1)}, u32[]{:S(2)}, u32[]{:S(2)}) collective-permute-start(bf16[192,1040]{1,0:T(8,128)(2,1)S(1)} %fusion.15.refs_0_), channel_id=1, source_target_pairs={{0,8},{8,16},{16,24},{24,28},{28,20},{20,12},{12,4},{4,0},{1,9},{9... | collective-permute-start | bytes 1198088 | tf_op jit(solution)/shard_map/ppermute | solution.py:707
  6.4 2.0 collective-permute-start.4
  9.6 6.4 %collective-permute-done.refs_1_ = bf16[192,1040]{1,0:T(8,128)(2,1)} collective-permute-done((bf16[192,1040]{1,0:T(8,128)(2,1)S(1)}, bf16[192,1040]{1,0:T(8,128)(2,1)}, u32[]{:S(2)}, u32[]{:S(2)}) %collective-permute-start) | collective-permute-done | bytes 399392 | tf_op jit(solution)/shard_map/ppermute | solution.py:707
  16.1 1.5 collective-permute-done.1.refs_2_
  17.6 1.6 collective-permute-start.2
  19.6 1.1 copy.49
  21.5 4.1 %collective-permute-done.4.refs_10_ = bf16[256,1536]{1,0:T(8,128)(2,1)} collective-permute-done((bf16[256,1536]{1,0:T(8,128)(2,1)S(1)}, bf16[256,1536]{1,0:T(8,128)(2,1)}, u32[]{:S(2)}, u32[]{:S(2)}) %collective-permute-start.4) | collective-permute-done | bytes 786464 | tf_op jit(solution)/shard_map/ppermute | solution.py:758
  25.6 2.9 %collective-permute-done.2.refs_3_ = bf16[192,1040]{1,0:T(8,128)(2,1)S(1)} collective-permute-done((bf16[192,1040]{1,0:T(8,128)(2,1)}, bf16[192,1040]{1,0:T(8,128)(2,1)S(1)}, u32[]{:S(2)}, u32[]{:S(2)}) %collective-permute-start.2) | collective-permute-done | bytes 399392 | tf_op jit(solution)/shard_map/ppermute | solution.py:707
  28.5 1.3 collective-permute-done.3.refs_4_
  31.4 1.1 pad_maximum_fusion.1.refs_0_
  33.0 1.6 collective-permute-start.5
  34.6 1.6 multiply_convert_fusion.1.refs_9_.refs_0_
  36.1 8.5 %collective-permute-done.6.refs_6_ = bf16[192,1040]{1,0:T(8,128)(2,1)S(1)} collective-permute-done((bf16[192,1040]{1,0:T(8,128)(2,1)}, bf16[192,1040]{1,0:T(8,128)(2,1)S(1)}, u32[]{:S(2)}, u32[]{:S(2)}) %collective-permute-start.6) | collective-permute-done | bytes 399392 | tf_op jit(solution)/shard_map/ppermute | solution.py:707
  45.3 1.5 collective-permute-start.9
  46.8 1.5 collective-permute-start.13
  48.3 2.7 %collective-permute-done.9.refs_7_ = bf16[192,512]{1,0:T(8,128)(2,1)S(1)} collective-permute-done((bf16[192,512]{1,0:T(8,128)(2,1)S(1)}, bf16[192,512]{1,0:T(8,128)(2,1)S(1)}, u32[]{:S(2)}, u32[]{:S(2)}) %collective-permute-start.9) | collective-permute-done | bytes 196640 | tf_op jit(solution)/shard_map/ppermute | solution.py:707
  51.6 1.6 collective-permute-start.11
  53.6 10.2 %project.1 = (bf16[1536,1152]{1,0:T(8,128)(2,1)}, bf16[1024,1536]{1,0:T(8,128)(2,1)S(1)}, bf16[1536,1024]{1,0:T(8,128)(2,1)S(1)}, f32[1024,1152]{1,0:T(8,128)}) custom-call(s32[13]{0:T(128)S(1)} %pad_add_fusion.off_ref, bf16[192,1040]{1,0:T(8,128)(2,1)S(1)} %fusion.15.refs_0_, bf16[192,1040]{1,0:T(8,128)(2,1)} %collective-permute-done.refs_1_, ...), custom_call_target="tpu_custom_call" | custom-call | flops 3623878656 | bytes 30000000 | tf_op jit(solution)/shard_map/project/pallas_call | solution.py:331
  63.8 1.7 copy-done.8
  66.2 1.5 collective-permute-start.14
  68.7 8.5 %ssd_forward_0.1 = (f32[1024,768]{1,0:T(8,128)S(1)}, f32[1024,1024]{1,0:T(8,128)}, f32[1024,1024]{1,0:T(8,128)}, f32[8,128,768]{2,1,0:T(8,128)}, bf16[1024,1536]...) custom-call(s32[4]{0:T(128)S(1)} %convert_element_type.245.first_ref, ...), custom_call_target="tpu_custom_call" | custom-call | flops 750000000 | bytes 15000000 | tf_op jit(solution)/shard_map/ssd_forward_0/pallas_call | solution.py:229
  78.3 1.3 collective-permute-done.15.refs_4_
  79.6 1.5 collective-permute-start.16
  81.6 8.9 %ssd_forward_4.1 = (f32[1024,768]{1,0:T(8,128)S(1)}, f32[1024,1024]{1,0:T(8,128)}, f32[1024,1024]{1,0:T(8,128)}, f32[8,128,768]{2,1,0:T(8,128)}, bf16[1024,1536]...) custom-call(s32[4]{0:T(128)S(1)} %convert_element_type.245.first_ref, ...), custom_call_target="tpu_custom_call", output_to_operand_aliasing={{0}: (5, {}), {1}: (6, {}), {2}: (7, {}), {3}: (8, {}), {4}... | custom-call | flops 750000000 | bytes 15000000 | tf_op jit(solution)/shard_map/ssd_forward_4/pallas_call | solution.py:229
  90.5 2.1 collective-permute-done.16.refs_5_
  92.5 1.2 collective-permute-done.17.refs_6_
  95.9 2.1 turn.1.zt_ref
  98.0 2.6 %collective-permute-done.20.refs_7_ = bf16[192,768]{1,0:T(8,128)(2,1)S(1)} collective-permute-done((bf16[192,768]{1,0:T(8,128)(2,1)S(1)}, bf16[192,768]{1,0:T(8,128)(2,1)S(1)}, u32[]{:S(2)}, u32[]{:S(2)}) %collective-permute-start.20) | collective-permute-done | bytes 294944 | tf_op jit(solution)/shard_map/ppermute | solution.py:707
  101.6 10.1 %cotangent.1 = (bf16[1536,1536]{1,0:T(8,128)(2,1)S(1)}, f32[1024,768]{1,0:T(8,128)S(1)}, f32[1024,768]{1,0:T(8,128)S(1)}, f32[4,8,256]{2,1,0:T(8,128)S(1)}, bf16[1024,768]{1,0:T(8,128)(2,1)S(1)}) custom-call(s32[13]{0:T(128)S(1)} %pad_add_fusion.off_ref, bf16[192,1536]{1,0:T(8,128)(2,1)S(1)} %pad_maximum_fusion.1.refs_0_, ...), custom_call_target="tpu_custom_call" | custom-call | flops 4831838208 | bytes 30000000 | tf_op jit(solution)/shard_map/cotangent/pallas_call | solution.py:382
  111.7 1.6 collective-permute-start.23
  113.6 4.3 %mixer_rows.1 = (bf16[2,256,1536]{2,1,0:T(8,128)(2,1)S(1)}, bf16[2,256,1536]{2,1,0:T(8,128)(2,1)S(1)}) custom-call(s32[4]{0:T(128)S(1)} %get-tuple-element.202.at_ref, bf16[1024,768]{1,0:T(8,128)(2,1)S(1)} %get-tuple-element.267.x_ref, bf16[1536,1536]{1,0:T(8,128)(2,1)S(1)} %get-tuple-element.268.w_ref.g_ref), custom_call_target="tpu_custom_call" | custom-call | flops 2415919104 | bytes 20000000 | tf_op jit(solution)/shard_map/mixer_rows/pallas_call | solution.py:551
  117.9 3.2 %gate_back.1 = (bf16[1024,768]{1,0:T(8,128)(2,1)S(1)}, bf16[1024,768]{1,0:T(8,128)(2,1)S(1)}, f32[1024,768]{1,0:T(8,128)S(1)}, f32[8,768]{1,0:T(8,128)S(1)}) custom-call(f32[4,8,256]{2,1,0:T(8,128)S(1)} %add_add_fusion.2.sum_ref.s_ref, f32[1024,768]{1,0:T(8,128)S(1)} %get-tuple-element.272.by_ref, f32[1024,768]{1,0:T(8,128)S(1)} %get-tuple-element.273.gr_ref, ...), custom_call_target="tpu_custom_call" | custom-call | flops 20000000 | bytes 15000000 | tf_op jit(solution)/shard_map/gate_back/pallas_call | solution.py:462
  121.1 1.4 far_grad.2
  123.0 1.2 collective-permute-start.25
  125.0 6.2 %pair_grad.1 = bf16[8,192,1536]{2,1,0:T(8,128)(2,1)S(1)} custom-call(s32[18]{0:T(128)S(1)} %get-tuple-element.283.at_ref, bf16[1536,1024]{1,0:T(8,128)(2,1)S(1)} %copy-done.2, bf16[1024,768]{1,0:T(8,128)(2,1)S(1)} %get-tuple-element.284.back_ref.gate_ref, bf16[1536,1024]{1,0:T(8,128)(2,1)S(1)} %turn.1.zt_ref, bf16[1024,768]{1,0:T(8,128)(2,1)S(1)} %get-tuple-element.285.y_ref), custom_call_target="tpu_custom_call" | custom-call | flops 4831838208 | bytes 14000000 | tf_op jit(solution)/shard_map/pair_grad/pallas_call | solution.py:644
  133.4 1.3 collective-permute-start.28
  135.4 1.5 collective-permute-start.30
  136.9 12.2 %ssd_backward_5.1 = (bf16[1024,1152]{1,0:T(8,128)(2,1)S(1)}, f32[128,768]{1,0:T(8,128)}, f32[128,768]{1,0:T(8,128)}, f32[8,1024]{1,0:T(8,128)S(1)}, f32[8,1024]{1,0:T(8,128)S(1)}, /*index=5*/f32[8,128]{1,0:T(8,128)S(1)}) custom-call(s32[4]{0:T(128)S(1)} %convert_element_type.245.first_ref, f32[1024,1152]{1,0:T(8,128)} %get-tuple-element.238.raw_ref, ...), custom_call_target="tpu_custom_call" | custom-call | flops 1124999936 | bytes 22500000 | tf_op jit(solution)/shard_map/ssd_backward_5/pallas_call | solution.py:244
  149.5 1.3 collective-permute-start.31
  152.5 12.7 %ssd_backward_2.1 = (bf16[1024,1152]{1,0:T(8,128)(2,1)S(1)}, f32[128,768]{1,0:T(8,128)}, f32[128,768]{1,0:T(8,128)}, f32[8,1024]{1,0:T(8,128)S(1)}, f32[8,1024]{1,0:T(8,128)S(1)}, /*index=5*/f32[8,128]{1,0:T(8,128)S(1)}) custom-call(s32[4]{0:T(128)S(1)} %convert_element_type.245.first_ref, ...), custom_call_target="tpu_custom_call", output_to_operand_aliasing={{0}: (15, {})} | custom-call | flops 1124999936 | bytes 22500000 | tf_op jit(solution)/shard_map/ssd_backward_2/pallas_call | solution.py:244
  166.4 1.2 collective-permute-start.35
  167.7 9.8 %ssd_backward_0.1 = (bf16[1024,1152]{1,0:T(8,128)(2,1)S(1)}, f32[128,768]{1,0:T(8,128)}, f32[128,768]{1,0:T(8,128)}, f32[8,1024]{1,0:T(8,128)}, f32[8,1024]{1,0:T(8,128)S(1)}, /*index=5*/f32[8,128]{1,0:T(8,128)S(1)}) custom-call(s32[4]{0:T(128)S(1)} %convert_element_type.245.first_ref, ...), custom_call_target="tpu_custom_call", output_to_operand_aliasing={{0}: (15, {})} | custom-call | flops 750000000 | bytes 15000000 | tf_op jit(solution)/shard_map/ssd_backward_0/pallas_call | solution.py:244
  178.6 1.3 far_grad.3
  180.9 1.2 collective-permute-start.36
  182.1 5.0 %weight_grad.1 = bf16[8,192,1152]{2,1,0:T(8,128)(2,1)S(1)} custom-call(s32[18]{0:T(128)S(1)} %get-tuple-element.283.at_ref, bf16[1536,1024]{1,0:T(8,128)(2,1)S(1)} %copy-done.2, bf16[1024,1152]{1,0:T(8,128)(2,1)S(1)} %get-tuple-element.335.back_ref.first_ref), custom_call_target="tpu_custom_call" | custom-call | flops 3623878656 | bytes 8000000 | tf_op jit(solution)/shard_map/weight_grad/pallas_call | solution.py:583
  188.8 1.1 collective-permute-start.39
  189.9 10.1 %back_normed.1 = (bf16[2,256,1536]{2,1,0:T(8,128)(2,1)}, bf16[2,256,1536]{2,1,0:T(8,128)(2,1)S(1)}, f32[8,1536]{1,0:T(8,128)S(1)}, f32[256,1536]{1,0:T(8,128)}) custom-call(s32[4]{0:T(128)S(1)} %get-tuple-element.202.at_ref, bf16[1024,1152]{1,0:T(8,128)(2,1)S(1)} %get-tuple-element.335.back_ref.first_ref, ...), custom_call_target="tpu_custom_call" | custom-call | flops 6039797760 | bytes 60000000 | tf_op jit(solution)/shard_map/back_normed/pallas_call | solution.py:509
  200.9 2.5 %fusion.10 = (bf16[192,1152]{1,0:T(8,128)(2,1)}, bf16[192,1152]{1,0:T(8,128)(2,1)}) fusion(bf16[192,1152]{1,0:T(8,128)(2,1)} %copy-done.20, bf16[8,192,1152]{2,1,0:T(8,128)(2,1)} %copy-done.4, bf16[192,1152]{1,0:T(8,128)(2,1)} %copy-done.19), kind=kLoop, calls=%fused_computation.29 | loop fusion | flops 1769472 | bytes 2654208 | tf_op jit(solution)/shard_map/convert_element_type | solution.py:747
  204.3 1.2 collective-permute-start.45
  208.3 1.3 add_convert_fusion
  209.7 1.3 collective-permute-start.43
  211.0 1.3 fusion.1.g_ref
  214.2 4.6 %collective-permute-done.40 = bf16[192,1152]{1,0:T(8,128)(2,1)} collective-permute-done((bf16[192,1152]{1,0:T(8,128)(2,1)}, bf16[192,1152]{1,0:T(8,128)(2,1)}, u32[]{:S(2)}, u32[]{:S(2)}) %collective-permute-start.40) | collective-permute-done | bytes 442400 | tf_op jit(solution)/shard_map/ppermute | solution.py:707
  221.8 1.6 fusion.8
  224.3 1.3 collective-permute-start.47
  226.3 1.3 collective-permute-start.50
  227.6 1.8 slice_bitcast_fusion.x_ref
  229.5 6.0 %collective-permute-done.50 = bf16[128,1536]{1,0:T(8,128)(2,1)S(1)} collective-permute-done((bf16[128,1536]{1,0:T(8,128)(2,1)S(1)}, bf16[128,1536]{1,0:T(8,128)(2,1)S(1)}, u32[]{:S(2)}, u32[]{:S(2)}) %collective-permute-start.50) | collective-permute-done | bytes 393248 | tf_op jit(solution)/shard_map/ppermute | solution.py:758
  238.0 2.9 %collective-permute-start.52 = (f32[12,1024]{1,0:T(8,128)S(1)}, f32[12,1024]{1,0:T(8,128)S(1)}, u32[]{:S(2)}, u32[]{:S(2)}) collective-permute-start(f32[12,1024]{1,0:T(8,128)S(1)} %add.243), channel_id=1, source_target_pairs={{0,16},{4,20},{8,24},{12,28},{16,0},{20,4},{24,8},{28,12},{1,17},{... | collective-permute-start | bytes 147464 | tf_op jit(solution)/shard_map/ppermute | solution.py:758
  241.7 1.2 collective-permute-start.55
  242.8 1.8 multiply_reduce_fusion
  244.6 3.0 %multiply_add_fusion = f32[256,1536]{1,0:T(8,128)} fusion(f32[256,1536]{1,0:T(8,128)S(1)} %copy-done.11, f32[256,1536]{1,0:T(8,128)S(1)} %copy-done, f32[256]{0:T(256)S(1)} %broadcast_multiply_fusion, f32[1536]{0:T(1024)S(1)} %copy-done.21, f32[256]{0:T(256)S(1)} %add_rsqrt_fusion, bf16[2,256,1536]{2,1,0:T(8,128)(2,1)} %collective-permute-done.42, ...), kind=kLoop, calls=%fused_computation.2 | loop fusion | flops 5505024 | bytes 7086080 | tf_op jit(solution)/shard_map/add | solution.py:1011
  250.2 3.3 %finish.1 = (f32[192,2,768]{2,1,0:T(2,128)}, f32[12,192]{1,0:T(8,128)}, f32[4,768]{1,0:T(4,128)}, f32[768]{0:T(1024)}, f32[768]{0:T(1024)}, /*index=5*/f32[12]{0:T(128)}, f32[12]{0:T(128)}, f32[12]{0:T(128)}) custom-call(bf16[192,1152]{1,0:T(8,128)(2,1)} %slice_bitcast_fusion.x_ref, bf16[192,1152]{1,0:T(8,128)(2,1)} %copy-done.13, ...), custom_call_target="tpu_custom_call" | custom-call | flops 1000000 | bytes 5000000 | tf_op jit(solution)/shard_map/finish/pallas_call | solution.py:681
  (223 shorter events, 42.1 us)
Async XLA Ops:
  2.8 13.3 %collective-permute-start = (bf16[192,1040]{1,0:T(8,128)(2,1)S(1)}, bf16[192,1040]{1,0:T(8,128)(2,1)}, u32[]{:S(2)}, u32[]{:S(2)}) collective-permute-start(bf16[192,1040]{1,0:T(8,128)(2,1)S(1)} %fusion.15.refs_0_), channel_id=1, source_target_pairs={{0,8},{8,16},{16,24},{24,28},{28,20},{20,12},{12,4},{4,0},{1,9},{9... | collective-permute-start | bytes 1198088 | tf_op jit(solution)/shard_map/ppermute | solution.py:707
  5.8 11.7 %collective-permute-start.1 = (bf16[192,1040]{1,0:T(8,128)(2,1)S(1)}, bf16[192,1040]{1,0:T(8,128)(2,1)}, u32[]{:S(2)}, u32[]{:S(2)}) collective-permute-start(bf16[192,1040]{1,0:T(8,128)(2,1)S(1)} %fusion.15.refs_0_), channel_id=1, source_target_pairs={{8,0},{16,8},{24,16},{28,24},{20,28},{12,20},{4,12},{0,4},{9,1},{1... | collective-permute-start | bytes 1198088 | tf_op jit(solution)/shard_map/ppermute | solution.py:707
  6.1 14.6 %copy-start.23 = (f32[768,4]{0,1:T(4,128)S(1)}, f32[768,4]{0,1:T(4,128)}, u32[]{:S(2)}) copy-start(f32[768,4]{0,1:T(4,128)} %param.26) | copy-start | bytes 36868
  6.2 14.6 %copy-start.27 = (f32[256,4]{0,1:T(4,128)S(1)}, f32[256,4]{0,1:T(4,128)}, u32[]{:S(2)}) copy-start(f32[256,4]{0,1:T(4,128)} %param.28) | copy-start | bytes 12292
  6.2 25.0 %copy-start.31 = (f32[12]{0:T(128)S(1)}, f32[12]{0:T(128)}, u32[]{:S(2)}) copy-start(f32[12]{0:T(128)} %param.32) | copy-start | bytes 148
  6.2 25.1 %copy-start.32 = (f32[12]{0:T(128)S(1)}, f32[12]{0:T(128)}, u32[]{:S(2)}) copy-start(f32[12]{0:T(128)} %param.30) | copy-start | bytes 148
  6.2 25.1 %copy-start.33 = (f32[12]{0:T(128)S(1)}, f32[12]{0:T(128)}, u32[]{:S(2)}) copy-start(f32[12]{0:T(128)} %param.31) | copy-start | bytes 148
  6.4 19.2 %collective-permute-start.4 = (bf16[256,1536]{1,0:T(8,128)(2,1)S(1)}, bf16[256,1536]{1,0:T(8,128)(2,1)}, u32[]{:S(2)}, u32[]{:S(2)}) collective-permute-start(bf16[256,1536]{1,0:T(8,128)(2,1)S(1)} %multiply_convert_fusion.refs_9_), channel_id=1, source_target_pairs={{0,2},{1,3},{2,0},{3,1},{4,6},{5,7},{6,4},{7,5},{8,10},{9,11},{10,... | collective-permute-start | bytes 2359304 | tf_op jit(solution)/shard_map/ppermute | solution.py:758
  17.6 10.9 %collective-permute-start.2 = (bf16[192,1040]{1,0:T(8,128)(2,1)}, bf16[192,1040]{1,0:T(8,128)(2,1)S(1)}, u32[]{:S(2)}, u32[]{:S(2)}) collective-permute-start(bf16[192,1040]{1,0:T(8,128)(2,1)} %collective-permute-done.refs_1_), channel_id=1, source_target_pairs={{0,8},{8,16},{16,24},{24,28},{28,20},{20,12},{12,4},{4,0},{1,9},{9... | collective-permute-start | bytes 1198088 | tf_op jit(solution)/shard_map/ppermute | solution.py:707
  19.2 10.6 %collective-permute-start.3 = (bf16[192,1040]{1,0:T(8,128)(2,1)}, bf16[192,1040]{1,0:T(8,128)(2,1)S(1)}, u32[]{:S(2)}, u32[]{:S(2)}) collective-permute-start(bf16[192,1040]{1,0:T(8,128)(2,1)} %collective-permute-done.1.refs_2_), channel_id=1, source_target_pairs={{8,0},{16,8},{24,16},{28,24},{20,28},{12,20},{4,12},{0,4},{9,1},{1... | collective-permute-start | bytes 1198088 | tf_op jit(solution)/shard_map/ppermute | solution.py:707
  29.8 14.9 %collective-permute-start.7 = (bf16[256,1536]{1,0:T(8,128)(2,1)S(1)}, bf16[256,1536]{1,0:T(8,128)(2,1)}, u32[]{:S(2)}, u32[]{:S(2)}) collective-permute-start(bf16[256,1536]{1,0:T(8,128)(2,1)S(1)} %multiply_convert_fusion.refs_9_), channel_id=1, source_target_pairs={{0,1},{1,0},{2,3},{3,2},{4,5},{5,4},{6,7},{7,6},{8,9},{9,8},{10,11... | collective-permute-start | bytes 2359304 | tf_op jit(solution)/shard_map/ppermute | solution.py:758
  29.8 14.9 %collective-permute-start.8 = (bf16[256,1536]{1,0:T(8,128)(2,1)}, bf16[256,1536]{1,0:T(8,128)(2,1)}, u32[]{:S(2)}, u32[]{:S(2)}) collective-permute-start(bf16[256,1536]{1,0:T(8,128)(2,1)} %collective-permute-done.4.refs_10_), channel_id=1, source_target_pairs={{0,1},{1,0},{2,3},{3,2},{4,5},{5,4},{6,7},{7,6},{8,9},{9,8},{10,11... | collective-permute-start | bytes 2359304 | tf_op jit(solution)/shard_map/ppermute | solution.py:758
  32.5 21.2 %copy-start.6 = (bf16[192,1040]{1,0:T(8,128)(2,1)S(1)}, bf16[192,1040]{1,0:T(8,128)(2,1)}, u32[]{:S(2)}) copy-start(bf16[192,1040]{1,0:T(8,128)(2,1)} %copy-done.5) | copy-start | bytes 1198084
  32.5 12.2 %collective-permute-start.6 = (bf16[192,1040]{1,0:T(8,128)(2,1)}, bf16[192,1040]{1,0:T(8,128)(2,1)S(1)}, u32[]{:S(2)}, u32[]{:S(2)}) collective-permute-start(bf16[192,1040]{1,0:T(8,128)(2,1)} %copy-done.5), channel_id=1, source_target_pairs={{8,0},{16,8},{24,16},{28,24},{20,28},{12,20},{4,12},{0,4},{9,1},{1... | collective-permute-start | bytes 1198088 | tf_op jit(solution)/shard_map/ppermute | solution.py:707
  33.0 11.7 %collective-permute-start.5 = (bf16[192,1040]{1,0:T(8,128)(2,1)S(1)}, bf16[192,1040]{1,0:T(8,128)(2,1)S(1)}, u32[]{:S(2)}, u32[]{:S(2)}) collective-permute-start(bf16[192,1040]{1,0:T(8,128)(2,1)S(1)} %collective-permute-done.2.refs_3_), channel_id=1, source_target_pairs={{0,8},{8,16},{16,24},{24,28},{28,20},{20,12},{12,4},{4,0},{1,9},{9... | collective-permute-start | bytes 1198088 | tf_op jit(solution)/shard_map/ppermute | solution.py:707
  44.7 6.9 %collective-permute-start.10 = (bf16[192,528]{1,0:T(8,128)(2,1)S(1)}, bf16[192,528]{1,0:T(8,128)(2,1)S(1)}, u32[]{:S(2)}, u32[]{:S(2)}) collective-permute-start(bf16[192,528]{1,0:T(8,128)(2,1)S(1)} %slice.206), channel_id=1, source_target_pairs={{8,0},{16,8},{24,16},{28,24},{20,28},{12,20},{4,12},{0,4},{9,1},{1... | collective-permute-start | bytes 608264 | tf_op jit(solution)/shard_map/ppermute | solution.py:707
  45.3 5.7 %collective-permute-start.9 = (bf16[192,512]{1,0:T(8,128)(2,1)S(1)}, bf16[192,512]{1,0:T(8,128)(2,1)S(1)}, u32[]{:S(2)}, u32[]{:S(2)}) collective-permute-start(bf16[192,512]{1,0:T(8,128)(2,1)S(1)} %slice.205), channel_id=1, source_target_pairs={{0,8},{8,16},{16,24},{24,28},{28,20},{20,12},{12,4},{4,0},{1,9},{9... | collective-permute-start | bytes 589832 | tf_op jit(solution)/shard_map/ppermute | solution.py:707
  46.8 18.7 %collective-permute-start.13 = (bf16[256,1536]{1,0:T(8,128)(2,1)S(1)}, bf16[256,1536]{1,0:T(8,128)(2,1)S(1)}, u32[]{:S(2)}, u32[]{:S(2)}) collective-permute-start(bf16[256,1536]{1,0:T(8,128)(2,1)S(1)} %multiply_convert_fusion.1.refs_9_.refs_0_), channel_id=1, source_target_pairs={{0,2},{1,3},{2,0},{3,1},{4,6},{5,7},{6,4},{7,5},{8,10},{9,11},{10,... | collective-permute-start | bytes 2359304 | tf_op jit(solution)/shard_map/ppermute | solution.py:758
  51.6 13.9 %collective-permute-start.11 = (bf16[192,1536]{1,0:T(8,128)(2,1)S(1)}, bf16[192,1536]{1,0:T(8,128)(2,1)S(1)}, u32[]{:S(2)}, u32[]{:S(2)}) collective-permute-start(bf16[192,1536]{1,0:T(8,128)(2,1)S(1)} %pad_maximum_fusion.1.refs_0_), channel_id=1, source_target_pairs={{0,8},{8,16},{16,24},{24,28},{28,20},{20,12},{12,4},{4,0},{1,9},{9... | collective-permute-start | bytes 1769480 | tf_op jit(solution)/shard_map/ppermute | solution.py:707
  53.2 13.0 %collective-permute-start.12 = (bf16[192,1536]{1,0:T(8,128)(2,1)S(1)}, bf16[192,1536]{1,0:T(8,128)(2,1)S(1)}, u32[]{:S(2)}, u32[]{:S(2)}) collective-permute-start(bf16[192,1536]{1,0:T(8,128)(2,1)S(1)} %pad_maximum_fusion.1.refs_0_), channel_id=1, source_target_pairs={{8,0},{16,8},{24,16},{28,24},{20,28},{12,20},{4,12},{0,4},{9,1},{1... | collective-permute-start | bytes 1769480 | tf_op jit(solution)/shard_map/ppermute | solution.py:707
  66.2 12.1 %collective-permute-start.14 = (bf16[192,1536]{1,0:T(8,128)(2,1)S(1)}, bf16[192,1536]{1,0:T(8,128)(2,1)S(1)}, u32[]{:S(2)}, u32[]{:S(2)}) collective-permute-start(bf16[192,1536]{1,0:T(8,128)(2,1)S(1)} %collective-permute-done.11.refs_1_), channel_id=1, source_target_pairs={{0,8},{8,16},{16,24},{24,28},{28,20},{20,12},{12,4},{4,0},{1,9},{9... | collective-permute-start | bytes 1769480 | tf_op jit(solution)/shard_map/ppermute | solution.py:707
  67.7 11.9 %collective-permute-start.15 = (bf16[192,1536]{1,0:T(8,128)(2,1)S(1)}, bf16[192,1536]{1,0:T(8,128)(2,1)S(1)}, u32[]{:S(2)}, u32[]{:S(2)}) collective-permute-start(bf16[192,1536]{1,0:T(8,128)(2,1)S(1)} %collective-permute-done.12.refs_2_), channel_id=1, source_target_pairs={{8,0},{16,8},{24,16},{28,24},{20,28},{12,20},{4,12},{0,4},{9,1},{1... | collective-permute-start | bytes 1769480 | tf_op jit(solution)/shard_map/ppermute | solution.py:707
  68.2 25.6 %collective-permute-start.18 = (bf16[256,1536]{1,0:T(8,128)(2,1)S(1)}, bf16[256,1536]{1,0:T(8,128)(2,1)S(1)}, u32[]{:S(2)}, u32[]{:S(2)}) collective-permute-start(bf16[256,1536]{1,0:T(8,128)(2,1)S(1)} %multiply_convert_fusion.1.refs_9_.refs_0_), channel_id=1, source_target_pairs={{0,1},{1,0},{2,3},{3,2},{4,5},{5,4},{6,7},{7,6},{8,9},{9,8},{10,11... | collective-permute-start | bytes 2359304 | tf_op jit(solution)/shard_map/ppermute | solution.py:758
  68.2 25.6 %collective-permute-start.19 = (bf16[256,1536]{1,0:T(8,128)(2,1)S(1)}, bf16[256,1536]{1,0:T(8,128)(2,1)S(1)}, u32[]{:S(2)}, u32[]{:S(2)}) collective-permute-start(bf16[256,1536]{1,0:T(8,128)(2,1)S(1)} %collective-permute-done.13.refs_10_.refs_1_), channel_id=1, source_target_pairs={{0,1},{1,0},{2,3},{3,2},{4,5},{5,4},{6,7},{7,6},{8,9},{9,8},{10,11... | collective-permute-start | bytes 2359304 | tf_op jit(solution)/shard_map/ppermute | solution.py:758
  79.6 13.0 %collective-permute-start.16 = (bf16[192,1536]{1,0:T(8,128)(2,1)S(1)}, bf16[192,1536]{1,0:T(8,128)(2,1)S(1)}, u32[]{:S(2)}, u32[]{:S(2)}) collective-permute-start(bf16[192,1536]{1,0:T(8,128)(2,1)S(1)} %collective-permute-done.14.refs_3_), channel_id=1, source_target_pairs={{0,8},{8,16},{16,24},{24,28},{28,20},{20,12},{12,4},{4,0},{1,9},{9... | collective-permute-start | bytes 1769480 | tf_op jit(solution)/shard_map/ppermute | solution.py:707
  81.1 12.7 %collective-permute-start.17 = (bf16[192,1536]{1,0:T(8,128)(2,1)S(1)}, bf16[192,1536]{1,0:T(8,128)(2,1)S(1)}, u32[]{:S(2)}, u32[]{:S(2)}) collective-permute-start(bf16[192,1536]{1,0:T(8,128)(2,1)S(1)} %collective-permute-done.15.refs_4_), channel_id=1, source_target_pairs={{8,0},{16,8},{24,16},{28,24},{20,28},{12,20},{4,12},{0,4},{9,1},{1... | collective-permute-start | bytes 1769480 | tf_op jit(solution)/shard_map/ppermute | solution.py:707
  93.8 6.8 %collective-permute-start.20 = (bf16[192,768]{1,0:T(8,128)(2,1)S(1)}, bf16[192,768]{1,0:T(8,128)(2,1)S(1)}, u32[]{:S(2)}, u32[]{:S(2)}) collective-permute-start(bf16[192,768]{1,0:T(8,128)(2,1)S(1)} %slice.207), channel_id=1, source_target_pairs={{0,8},{8,16},{16,24},{24,28},{28,20},{20,12},{12,4},{4,0},{1,9},{9... | collective-permute-start | bytes 884744 | tf_op jit(solution)/shard_map/ppermute | solution.py:707
  94.8 6.7 %collective-permute-start.21 = (bf16[192,768]{1,0:T(8,128)(2,1)S(1)}, bf16[192,768]{1,0:T(8,128)(2,1)S(1)}, u32[]{:S(2)}, u32[]{:S(2)}) collective-permute-start(bf16[192,768]{1,0:T(8,128)(2,1)S(1)} %slice.208), channel_id=1, source_target_pairs={{8,0},{16,8},{24,16},{28,24},{20,28},{12,20},{4,12},{0,4},{9,1},{1... | collective-permute-start | bytes 884744 | tf_op jit(solution)/shard_map/ppermute | solution.py:707
  111.7 6.2 %collective-permute-start.22 = (f32[4,8,256]{2,1,0:T(8,128)S(1)}, f32[4,8,256]{2,1,0:T(8,128)S(1)}, u32[]{:S(2)}, u32[]{:S(2)}) collective-permute-start(f32[4,8,256]{2,1,0:T(8,128)S(1)} %get-tuple-element.266), channel_id=1, source_target_pairs={{0,1},{1,0},{2,3},{3,2},{4,5},{5,4},{6,7},{7,6},{8,9},{9,8},{10,11... | collective-permute-start | bytes 98312 | tf_op jit(solution)/shard_map/ppermute | solution.py:758
  111.7 6.2 %collective-permute-start.23 = (f32[4,8,256]{2,1,0:T(8,128)S(1)}, f32[4,8,256]{2,1,0:T(8,128)S(1)}, u32[]{:S(2)}, u32[]{:S(2)}) collective-permute-start(f32[4,8,256]{2,1,0:T(8,128)S(1)} %get-tuple-element.266), channel_id=1, source_target_pairs={{0,2},{1,3},{2,0},{3,1},{4,6},{5,7},{6,4},{7,5},{8,10},{9,11},{10,... | collective-permute-start | bytes 98312 | tf_op jit(solution)/shard_map/ppermute | solution.py:758
  113.3 4.6 %collective-permute-start.24 = (f32[4,8,256]{2,1,0:T(8,128)S(1)}, f32[4,8,256]{2,1,0:T(8,128)S(1)}, u32[]{:S(2)}, u32[]{:S(2)}) collective-permute-start(f32[4,8,256]{2,1,0:T(8,128)S(1)} %get-tuple-element.266), channel_id=1, source_target_pairs={{0,3},{1,2},{2,1},{3,0},{4,7},{5,6},{6,5},{7,4},{8,11},{9,10},{10,... | collective-permute-start | bytes 98312 | tf_op jit(solution)/shard_map/ppermute | solution.py:758
  122.6 10.4 %collective-permute-start.27 = (bf16[2,256,1536]{2,1,0:T(8,128)(2,1)S(1)}, bf16[2,256,1536]{2,1,0:T(8,128)(2,1)S(1)}, u32[]{:S(2)}, u32[]{:S(2)}) collective-permute-start(bf16[2,256,1536]{2,1,0:T(8,128)(2,1)S(1)} %get-tuple-element.286), channel_id=1, source_target_pairs={{0,1},{1,0},{2,3},{3,2},{4,5},{5,4},{6,7},{7,6},{8,9},{9,8},{10,11... | collective-permute-start | bytes 4718600 | tf_op jit(solution)/shard_map/ppermute | solution.py:758
  123.0 9.1 %collective-permute-start.25 = (bf16[192,768]{1,0:T(8,128)(2,1)S(1)}, bf16[192,768]{1,0:T(8,128)(2,1)S(1)}, u32[]{:S(2)}, u32[]{:S(2)}) collective-permute-start(bf16[192,768]{1,0:T(8,128)(2,1)S(1)} %get-tuple-element.281), channel_id=1, source_target_pairs={{0,8},{8,16},{16,24},{24,28},{28,20},{20,12},{12,4},{4,0},{1,9},{9... | collective-permute-start | bytes 884744 | tf_op jit(solution)/shard_map/ppermute | solution.py:707
  124.2 8.8 %collective-permute-start.26 = (bf16[192,768]{1,0:T(8,128)(2,1)S(1)}, bf16[192,768]{1,0:T(8,128)(2,1)S(1)}, u32[]{:S(2)}, u32[]{:S(2)}) collective-permute-start(bf16[192,768]{1,0:T(8,128)(2,1)S(1)} %get-tuple-element.282), channel_id=1, source_target_pairs={{8,0},{16,8},{24,16},{28,24},{20,28},{12,20},{4,12},{0,4},{9,1},{1... | collective-permute-start | bytes 884744 | tf_op jit(solution)/shard_map/ppermute | solution.py:707
  131.3 33.9 %copy-start.3 = (bf16[8,192,1536]{2,1,0:T(8,128)(2,1)}, bf16[8,192,1536]{2,1,0:T(8,128)(2,1)S(1)}, u32[]{:S(2)}) copy-start(bf16[8,192,1536]{2,1,0:T(8,128)(2,1)S(1)} %pair_grad.1) | copy-start | bytes 14155780
  133.4 15.8 %collective-permute-start.28 = (bf16[192,1536]{1,0:T(8,128)(2,1)S(1)}, bf16[192,1536]{1,0:T(8,128)(2,1)S(1)}, u32[]{:S(2)}, u32[]{:S(2)}) collective-permute-start(bf16[192,1536]{1,0:T(8,128)(2,1)S(1)} %get-tuple-element.297), channel_id=1, source_target_pairs={{0,8},{8,16},{16,24},{24,28},{28,20},{20,12},{12,4},{4,0},{1,9},{9... | collective-permute-start | bytes 1769480 | tf_op jit(solution)/shard_map/ppermute | solution.py:707
  134.6 14.6 %collective-permute-start.29 = (bf16[192,1536]{1,0:T(8,128)(2,1)S(1)}, bf16[192,1536]{1,0:T(8,128)(2,1)S(1)}, u32[]{:S(2)}, u32[]{:S(2)}) collective-permute-start(bf16[192,1536]{1,0:T(8,128)(2,1)S(1)} %get-tuple-element.298), channel_id=1, source_target_pairs={{8,0},{16,8},{24,16},{28,24},{20,28},{12,20},{4,12},{0,4},{9,1},{1... | collective-permute-start | bytes 1769480 | tf_op jit(solution)/shard_map/ppermute | solution.py:707
  135.4 13.7 %collective-permute-start.30 = (bf16[128,1536]{1,0:T(8,128)(2,1)S(1)}, bf16[128,1536]{1,0:T(8,128)(2,1)S(1)}, u32[]{:S(2)}, u32[]{:S(2)}) collective-permute-start(bf16[128,1536]{1,0:T(8,128)(2,1)S(1)} %get-tuple-element.299), channel_id=1, source_target_pairs={{0,2},{1,3},{2,0},{3,1},{4,6},{5,7},{6,4},{7,5},{8,10},{9,11},{10,... | collective-permute-start | bytes 1179656 | tf_op jit(solution)/shard_map/ppermute | solution.py:758
  149.5 15.7 %collective-permute-start.31 = (bf16[192,1536]{1,0:T(8,128)(2,1)S(1)}, bf16[192,1536]{1,0:T(8,128)(2,1)S(1)}, u32[]{:S(2)}, u32[]{:S(2)}) collective-permute-start(bf16[192,1536]{1,0:T(8,128)(2,1)S(1)} %get-tuple-element.310), channel_id=1, source_target_pairs={{0,8},{8,16},{16,24},{24,28},{28,20},{20,12},{12,4},{4,0},{1,9},{9... | collective-permute-start | bytes 1769480 | tf_op jit(solution)/shard_map/ppermute | solution.py:707
  150.8 14.4 %collective-permute-start.32 = (bf16[192,1536]{1,0:T(8,128)(2,1)S(1)}, bf16[192,1536]{1,0:T(8,128)(2,1)S(1)}, u32[]{:S(2)}, u32[]{:S(2)}) collective-permute-start(bf16[192,1536]{1,0:T(8,128)(2,1)S(1)} %get-tuple-element.311), channel_id=1, source_target_pairs={{8,0},{16,8},{24,16},{28,24},{20,28},{12,20},{4,12},{0,4},{9,1},{1... | collective-permute-start | bytes 1769480 | tf_op jit(solution)/shard_map/ppermute | solution.py:707
  151.6 13.6 %collective-permute-start.33 = (bf16[128,1536]{1,0:T(8,128)(2,1)S(1)}, bf16[128,1536]{1,0:T(8,128)(2,1)S(1)}, u32[]{:S(2)}, u32[]{:S(2)}) collective-permute-start(bf16[128,1536]{1,0:T(8,128)(2,1)S(1)} %get-tuple-element.312), channel_id=1, source_target_pairs={{0,2},{1,3},{2,0},{3,1},{4,6},{5,7},{6,4},{7,5},{8,10},{9,11},{10,... | collective-permute-start | bytes 1179656 | tf_op jit(solution)/shard_map/ppermute | solution.py:758
  165.5 12.3 %collective-permute-start.34 = (bf16[192,1536]{1,0:T(8,128)(2,1)S(1)}, bf16[192,1536]{1,0:T(8,128)(2,1)S(1)}, u32[]{:S(2)}, u32[]{:S(2)}) collective-permute-start(bf16[192,1536]{1,0:T(8,128)(2,1)S(1)} %get-tuple-element.323), channel_id=1, source_target_pairs={{0,8},{8,16},{16,24},{24,28},{28,20},{20,12},{12,4},{4,0},{1,9},{9... | collective-permute-start | bytes 1769480 | tf_op jit(solution)/shard_map/ppermute | solution.py:707
  166.4 12.3 %collective-permute-start.35 = (bf16[192,1536]{1,0:T(8,128)(2,1)S(1)}, bf16[192,1536]{1,0:T(8,128)(2,1)S(1)}, u32[]{:S(2)}, u32[]{:S(2)}) collective-permute-start(bf16[192,1536]{1,0:T(8,128)(2,1)S(1)} %get-tuple-element.324), channel_id=1, source_target_pairs={{8,0},{16,8},{24,16},{28,24},{20,28},{12,20},{4,12},{0,4},{9,1},{1... | collective-permute-start | bytes 1769480 | tf_op jit(solution)/shard_map/ppermute | solution.py:707
  180.0 7.7 %collective-permute-start.37 = (bf16[192,640]{1,0:T(8,128)(2,1)S(1)}, bf16[192,640]{1,0:T(8,128)(2,1)S(1)}, u32[]{:S(2)}, u32[]{:S(2)}) collective-permute-start(bf16[192,640]{1,0:T(8,128)(2,1)S(1)} %get-tuple-element.329), channel_id=1, source_target_pairs={{8,0},{16,8},{24,16},{28,24},{20,28},{12,20},{4,12},{0,4},{9,1},{1... | collective-permute-start | bytes 737288 | tf_op jit(solution)/shard_map/ppermute | solution.py:707
  180.9 6.8 %collective-permute-start.36 = (bf16[192,512]{1,0:T(8,128)(2,1)S(1)}, bf16[192,512]{1,0:T(8,128)(2,1)S(1)}, u32[]{:S(2)}, u32[]{:S(2)}) collective-permute-start(bf16[192,512]{1,0:T(8,128)(2,1)S(1)} %get-tuple-element.328), channel_id=1, source_target_pairs={{0,8},{8,16},{16,24},{24,28},{28,20},{20,12},{12,4},{4,0},{1,9},{9... | collective-permute-start | bytes 589832 | tf_op jit(solution)/shard_map/ppermute | solution.py:707
  187.8 12.2 %collective-permute-start.38 = (bf16[192,1152]{1,0:T(8,128)(2,1)S(1)}, bf16[192,1152]{1,0:T(8,128)(2,1)S(1)}, u32[]{:S(2)}, u32[]{:S(2)}) collective-permute-start(bf16[192,1152]{1,0:T(8,128)(2,1)S(1)} %get-tuple-element.340), channel_id=1, source_target_pairs={{0,8},{8,16},{16,24},{24,28},{28,20},{20,12},{12,4},{4,0},{1,9},{9... | collective-permute-start | bytes 1327112 | tf_op jit(solution)/shard_map/ppermute | solution.py:707
  188.8 11.2 %collective-permute-start.39 = (bf16[192,1152]{1,0:T(8,128)(2,1)S(1)}, bf16[192,1152]{1,0:T(8,128)(2,1)S(1)}, u32[]{:S(2)}, u32[]{:S(2)}) collective-permute-start(bf16[192,1152]{1,0:T(8,128)(2,1)S(1)} %get-tuple-element.341), channel_id=1, source_target_pairs={{8,0},{16,8},{24,16},{28,24},{20,28},{12,20},{4,12},{0,4},{9,1},{1... | collective-permute-start | bytes 1327112 | tf_op jit(solution)/shard_map/ppermute | solution.py:707
  203.5 3.8 %collective-permute-start.42 = (bf16[2,256,1536]{2,1,0:T(8,128)(2,1)}, bf16[2,256,1536]{2,1,0:T(8,128)(2,1)}, u32[]{:S(2)}, u32[]{:S(2)}) collective-permute-start(bf16[2,256,1536]{2,1,0:T(8,128)(2,1)} %get-tuple-element.353), channel_id=1, source_target_pairs={{0,1},{1,0},{2,3},{3,2},{4,5},{5,4},{6,7},{7,6},{8,9},{9,8},{10,11... | collective-permute-start | bytes 4718600 | tf_op jit(solution)/shard_map/ppermute | solution.py:758
  203.7 6.0 %collective-permute-start.44 = (f32[16,256]{1,0:T(8,128)S(1)}, f32[16,256]{1,0:T(8,128)S(1)}, u32[]{:S(2)}, u32[]{:S(2)}) collective-permute-start(f32[16,256]{1,0:T(8,128)S(1)} %maximum_maximum_fusion), channel_id=1, source_target_pairs={{0,1},{1,0},{2,3},{3,2},{4,5},{5,4},{6,7},{7,6},{8,9},{9,8},{10,11... | collective-permute-start | bytes 49160 | tf_op jit(solution)/shard_map/ppermute | solution.py:758
  204.3 9.9 %collective-permute-start.45 = (f32[16,256]{1,0:T(8,128)S(1)}, f32[16,256]{1,0:T(8,128)S(1)}, u32[]{:S(2)}, u32[]{:S(2)}) collective-permute-start(f32[16,256]{1,0:T(8,128)S(1)} %maximum_maximum_fusion), channel_id=1, source_target_pairs={{0,2},{1,3},{2,0},{3,1},{4,6},{5,7},{6,4},{7,5},{8,10},{9,11},{10,... | collective-permute-start | bytes 49160 | tf_op jit(solution)/shard_map/ppermute | solution.py:758
  205.5 8.7 %collective-permute-start.46 = (f32[16,256]{1,0:T(8,128)S(1)}, f32[16,256]{1,0:T(8,128)S(1)}, u32[]{:S(2)}, u32[]{:S(2)}) collective-permute-start(f32[16,256]{1,0:T(8,128)S(1)} %maximum_maximum_fusion), channel_id=1, source_target_pairs={{0,3},{1,2},{2,1},{3,0},{4,7},{5,6},{6,5},{7,4},{8,11},{9,10},{10,... | collective-permute-start | bytes 49160 | tf_op jit(solution)/shard_map/ppermute | solution.py:758
  205.7 13.1 %collective-permute-start.40 = (bf16[192,1152]{1,0:T(8,128)(2,1)}, bf16[192,1152]{1,0:T(8,128)(2,1)}, u32[]{:S(2)}, u32[]{:S(2)}) collective-permute-start(bf16[192,1152]{1,0:T(8,128)(2,1)} %get-tuple-element.351), channel_id=1, source_target_pairs={{0,8},{8,16},{16,24},{24,28},{28,20},{20,12},{12,4},{4,0},{1,9},{9... | collective-permute-start | bytes 1327112 | tf_op jit(solution)/shard_map/ppermute | solution.py:707
  207.3 12.5 %collective-permute-start.41 = (bf16[192,1152]{1,0:T(8,128)(2,1)}, bf16[192,1152]{1,0:T(8,128)(2,1)}, u32[]{:S(2)}, u32[]{:S(2)}) collective-permute-start(bf16[192,1152]{1,0:T(8,128)(2,1)} %get-tuple-element.352), channel_id=1, source_target_pairs={{8,0},{16,8},{24,16},{28,24},{20,28},{12,20},{4,12},{0,4},{9,1},{1... | collective-permute-start | bytes 1327112 | tf_op jit(solution)/shard_map/ppermute | solution.py:707
  209.7 11.0 %collective-permute-start.43 = (bf16[128,1536]{1,0:T(8,128)(2,1)S(1)}, bf16[128,1536]{1,0:T(8,128)(2,1)}, u32[]{:S(2)}, u32[]{:S(2)}) collective-permute-start(bf16[128,1536]{1,0:T(8,128)(2,1)S(1)} %slice_bitcast_fusion.1), channel_id=1, source_target_pairs={{0,2},{1,3},{2,0},{3,1},{4,6},{5,7},{6,4},{7,5},{8,10},{9,11},{10,... | collective-permute-start | bytes 1179656 | tf_op jit(solution)/shard_map/ppermute | solution.py:758
  223.5 6.0 %collective-permute-start.49 = (f32[12,1024]{1,0:T(8,128)S(1)}, f32[12,1024]{1,0:T(8,128)S(1)}, u32[]{:S(2)}, u32[]{:S(2)}) collective-permute-start(f32[12,1024]{1,0:T(8,128)S(1)} %pad_maximum_fusion.2), channel_id=1, source_target_pairs={{0,4},{4,0},{8,12},{12,8},{16,20},{20,16},{24,28},{28,24},{1,5},{5... | collective-permute-start | bytes 147464 | tf_op jit(solution)/shard_map/ppermute | solution.py:758
  224.3 11.7 %collective-permute-start.47 = (bf16[192,1152]{1,0:T(8,128)(2,1)S(1)}, bf16[192,1152]{1,0:T(8,128)(2,1)S(1)}, u32[]{:S(2)}, u32[]{:S(2)}) collective-permute-start(bf16[192,1152]{1,0:T(8,128)(2,1)S(1)} %get-tuple-element.362), channel_id=1, source_target_pairs={{0,8},{8,16},{16,24},{24,28},{28,20},{20,12},{12,4},{4,0},{1,9},{9... | collective-permute-start | bytes 1327112 | tf_op jit(solution)/shard_map/ppermute | solution.py:707
  225.6 10.5 %collective-permute-start.48 = (bf16[192,1152]{1,0:T(8,128)(2,1)S(1)}, bf16[192,1152]{1,0:T(8,128)(2,1)S(1)}, u32[]{:S(2)}, u32[]{:S(2)}) collective-permute-start(bf16[192,1152]{1,0:T(8,128)(2,1)S(1)} %get-tuple-element.363), channel_id=1, source_target_pairs={{8,0},{16,8},{24,16},{28,24},{20,28},{12,20},{4,12},{0,4},{9,1},{1... | collective-permute-start | bytes 1327112 | tf_op jit(solution)/shard_map/ppermute | solution.py:707
  226.3 9.2 %collective-permute-start.50 = (bf16[128,1536]{1,0:T(8,128)(2,1)S(1)}, bf16[128,1536]{1,0:T(8,128)(2,1)S(1)}, u32[]{:S(2)}, u32[]{:S(2)}) collective-permute-start(bf16[128,1536]{1,0:T(8,128)(2,1)S(1)} %slice.189), channel_id=1, source_target_pairs={{0,2},{1,3},{2,0},{3,1},{4,6},{5,7},{6,4},{7,5},{8,10},{9,11},{10,... | collective-permute-start | bytes 1179656 | tf_op jit(solution)/shard_map/ppermute | solution.py:758
  237.2 10.5 %collective-permute-start.51 = (f32[12,1024]{1,0:T(8,128)S(1)}, f32[12,1024]{1,0:T(8,128)S(1)}, u32[]{:S(2)}, u32[]{:S(2)}) collective-permute-start(f32[12,1024]{1,0:T(8,128)S(1)} %add.243), channel_id=1, source_target_pairs={{0,8},{4,12},{8,0},{12,4},{16,24},{20,28},{24,16},{28,20},{1,9},{5... | collective-permute-start | bytes 147464 | tf_op jit(solution)/shard_map/ppermute | solution.py:758
  238.0 10.3 %collective-permute-start.52 = (f32[12,1024]{1,0:T(8,128)S(1)}, f32[12,1024]{1,0:T(8,128)S(1)}, u32[]{:S(2)}, u32[]{:S(2)}) collective-permute-start(f32[12,1024]{1,0:T(8,128)S(1)} %add.243), channel_id=1, source_target_pairs={{0,16},{4,20},{8,24},{12,28},{16,0},{20,4},{24,8},{28,12},{1,17},{... | collective-permute-start | bytes 147464 | tf_op jit(solution)/shard_map/ppermute | solution.py:758
  240.9 7.5 %collective-permute-start.53 = (f32[12,1024]{1,0:T(8,128)S(1)}, f32[12,1024]{1,0:T(8,128)S(1)}, u32[]{:S(2)}, u32[]{:S(2)}) collective-permute-start(f32[12,1024]{1,0:T(8,128)S(1)} %add.243), channel_id=1, source_target_pairs={{0,24},{4,28},{8,16},{12,20},{16,8},{20,12},{24,0},{28,4},{1,25},{... | collective-permute-start | bytes 147464 | tf_op jit(solution)/shard_map/ppermute | solution.py:758
  241.7 11.8 %collective-permute-start.54 = (f32[48,256]{1,0:T(8,128)S(1)}, f32[48,256]{1,0:T(8,128)S(1)}, u32[]{:S(2)}, u32[]{:S(2)}) collective-permute-start(f32[48,256]{1,0:T(8,128)S(1)} %get-tuple-element.377), channel_id=1, source_target_pairs={{0,1},{1,0},{2,3},{3,2},{4,5},{5,4},{6,7},{7,6},{8,9},{9,8},{10,11... | collective-permute-start | bytes 147464 | tf_op jit(solution)/shard_map/ppermute | solution.py:758
  241.7 11.8 %collective-permute-start.55 = (f32[48,256]{1,0:T(8,128)S(1)}, f32[48,256]{1,0:T(8,128)S(1)}, u32[]{:S(2)}, u32[]{:S(2)}) collective-permute-start(f32[48,256]{1,0:T(8,128)S(1)} %get-tuple-element.378), channel_id=1, source_target_pairs={{0,2},{1,3},{2,0},{3,1},{4,6},{5,7},{6,4},{7,5},{8,10},{9,11},{10,... | collective-permute-start | bytes 147464 | tf_op jit(solution)/shard_map/ppermute | solution.py:758
  247.6 5.9 %collective-permute-start.56 = (f32[48,256]{1,0:T(8,128)S(1)}, f32[48,256]{1,0:T(8,128)S(1)}, u32[]{:S(2)}, u32[]{:S(2)}) collective-permute-start(f32[48,256]{1,0:T(8,128)S(1)} %get-tuple-element.379), channel_id=1, source_target_pairs={{0,3},{1,2},{2,1},{3,0},{4,7},{5,6},{6,5},{7,4},{8,11},{9,10},{10,... | collective-permute-start | bytes 147464 | tf_op jit(solution)/shard_map/ppermute | solution.py:758
  (30 other events, 136.2 us)
